TPU v7x, 32 devices: a whole 2x2x4 slice. The times are simulated.
32 devices in a mesh: dp: 8 (over y, x, core), ctx: 4 (over z).
Axes of the slice: x: 2, y: 2, z: 4, core: 2. Of those that a mesh axis runs over, the one named last changes fastest.
Arguments:
- tokens: bfloat16 [4096, 1536], P(('dp', 'ctx')), may hold values from -6 to 6
- cotangent: float32 [4096, 1536], P(('dp', 'ctx')), may hold values from -6 to 6
- w_qkv: bfloat16 [2, 1536, 3072], P(None, ('dp', 'ctx')), may hold values from -0.15625 to 0.15625
- w_out: bfloat16 [2, 1536, 1536], P(None, None, ('dp', 'ctx')), may hold values from -1.25 to 1.25
- w_gate_up: bfloat16 [2, 1536, 2, 4096], P(None, ('dp', 'ctx')), may hold values from -0.15625 to 0.15625
- w_down: bfloat16 [2, 4096, 1536], P(None, ('dp', 'ctx')), may hold values from -0.09375 to 0.09375
- gains: bfloat16 [2, 2, 1536], P(None, None, ('dp', 'ctx')), may hold values from 0.25 to 1.75
Outputs:
- out_act: float32 [4096, 1536], P(('dp', 'ctx'))
- grad_tokens: float32 [4096, 1536], P(('dp', 'ctx'))
- grad_qkv: float32 [2, 1536, 3072], P(None, ('dp', 'ctx'))
- grad_out: float32 [2, 1536, 1536], P(None, None, ('dp', 'ctx'))
- grad_gate_up: float32 [2, 1536, 2, 4096], P(None, ('dp', 'ctx'))
- grad_down: float32 [2, 4096, 1536], P(None, ('dp', 'ctx'))
- grad_gains: float32 [2, 2, 1536], P(None, None, ('dp', 'ctx'))
All inputs are finite; a program needn't handle non-finite values.
Results may differ from a plain program's by a relative error of at most 0.025.
Values may be sent and summed in bfloat16 or wider, within the bound.
A program may use at most 640 MiB of HBM per device.

v0:
```python
import jax
import jax.numpy as jnp
from jax import lax
from jax.sharding import PartitionSpec as P

HEADS = 16
KV_HEADS = 8
HEAD_DIM = 96
LAYERS = 2


NORM_EPS = 1e-05
ROPE_BASE = 100000.0
MASKED = -1e30


def rotary_tables(positions, head_size):
    half_size = head_size // 2
    freq_index = jnp.arange(half_size).astype(jnp.float32)
    inverse = jnp.exp(freq_index * (-2.0 * jnp.log(ROPE_BASE) / head_size))
    angles = positions.astype(jnp.float32)[:, None] * inverse[None, :]
    return (jnp.cos(angles), jnp.sin(angles))


def rotate(values, cosine, sine_tab):
    half_size = values.shape[-1] // 2
    first_half = values[..., :half_size]
    second_half = values[..., half_size:]
    cos_wide = cosine[:, None, :]
    sin_wide = sine_tab[:, None, :]
    return jnp.concatenate(
        [
            first_half * cos_wide - second_half * sin_wide,
            second_half * cos_wide + first_half * sin_wide,
        ],
        axis=-1,
    )


def unrotate(grads, cosine, sine_tab):
    half_size = grads.shape[-1] // 2
    first_half = grads[..., :half_size]
    second_half = grads[..., half_size:]
    cos_wide = cosine[:, None, :]
    sin_wide = sine_tab[:, None, :]
    return jnp.concatenate(
        [
            first_half * cos_wide + second_half * sin_wide,
            second_half * cos_wide - first_half * sin_wide,
        ],
        axis=-1,
    )


def norm_forward(state, gain_row):
    factor = lax.rsqrt(jnp.mean(state * state, axis=-1, keepdims=True) + NORM_EPS)
    return (state * factor * gain_row.astype(jnp.float32), factor)


def norm_backward(state, factor, gain_row, grad_normed):
    weighted = grad_normed * gain_row.astype(jnp.float32)
    features = state.shape[-1]
    inner = jnp.sum(weighted * state, axis=-1, keepdims=True)
    grad_state = factor * weighted - state * factor * factor * factor * inner / features
    grad_gain = jnp.sum(grad_normed * state * factor, axis=0)
    return (grad_state, grad_gain)


def split_pair(pair_all):
    kv_cols = KV_HEADS * HEAD_DIM
    seq_length = pair_all.shape[0]
    keys_all = pair_all[:, :kv_cols].reshape(seq_length, KV_HEADS, HEAD_DIM)
    values_all = pair_all[:, kv_cols:].reshape(seq_length, KV_HEADS, HEAD_DIM)
    return (keys_all, values_all)


def fetch_layer(w_qkv, w_out, w_gate_up, w_down, gains, layer_index):
    return (
        lax.all_gather(w_qkv[layer_index], ("dp", "ctx"), axis=0, tiled=True),
        lax.all_gather(w_out[layer_index], ("dp", "ctx"), axis=1, tiled=True),
        lax.all_gather(w_gate_up[layer_index], ("dp", "ctx"), axis=0, tiled=True),
        lax.all_gather(w_down[layer_index], ("dp", "ctx"), axis=0, tiled=True),
        lax.all_gather(gains[layer_index], ("dp", "ctx"), axis=1, tiled=True),
    )


def fetch_again(w_qkv, w_out, w_gate_up, w_down, gains, layer_index):
    return (
        lax.all_gather(w_qkv[layer_index], ("dp", "ctx"), axis=0, tiled=True),
        lax.all_gather(w_out[layer_index], ("dp", "ctx"), axis=1, tiled=True),
        lax.all_gather(w_gate_up[layer_index], ("dp", "ctx"), axis=0, tiled=True),
        lax.all_gather(w_down[layer_index], ("dp", "ctx"), axis=0, tiled=True),
        lax.all_gather(gains[layer_index], ("dp", "ctx"), axis=1, tiled=True),
    )


def fetch_pairs(local_pair):
    return lax.all_gather(local_pair, "ctx", axis=0, tiled=True)


def reduce_grads(grad_tuple):
    blocks = (
        lax.psum_scatter(
            grad_tuple[0].astype(jnp.bfloat16), "dp", scatter_dimension=0, tiled=True
        ).astype(jnp.float32),
        lax.psum_scatter(
            grad_tuple[1].astype(jnp.bfloat16), "dp", scatter_dimension=1, tiled=True
        ).astype(jnp.float32),
        lax.psum_scatter(
            grad_tuple[2].astype(jnp.bfloat16), "dp", scatter_dimension=0, tiled=True
        ).astype(jnp.float32),
        lax.psum_scatter(
            grad_tuple[3].astype(jnp.bfloat16), "dp", scatter_dimension=0, tiled=True
        ).astype(jnp.float32),
        lax.psum_scatter(
            grad_tuple[4].astype(jnp.bfloat16), "dp", scatter_dimension=1, tiled=True
        ).astype(jnp.float32),
    )
    return (
        lax.psum_scatter(
            blocks[0].astype(jnp.bfloat16), "ctx", scatter_dimension=0, tiled=True
        ).astype(jnp.float32),
        lax.psum_scatter(
            blocks[1].astype(jnp.bfloat16), "ctx", scatter_dimension=1, tiled=True
        ).astype(jnp.float32),
        lax.psum_scatter(
            blocks[2].astype(jnp.bfloat16), "ctx", scatter_dimension=0, tiled=True
        ).astype(jnp.float32),
        lax.psum_scatter(
            blocks[3].astype(jnp.bfloat16), "ctx", scatter_dimension=0, tiled=True
        ).astype(jnp.float32),
        lax.psum_scatter(
            blocks[4].astype(jnp.bfloat16), "ctx", scatter_dimension=1, tiled=True
        ).astype(jnp.float32),
    )


def shards(tokens, cotangent, w_qkv, w_out, w_gate_up, w_down, gains):
    row_count = tokens.shape[0]
    seq_length = row_count * lax.axis_size("ctx")
    offset = lax.axis_index("ctx") * row_count
    query_pos = offset + jnp.arange(row_count, dtype=jnp.int32)
    key_pos = jnp.arange(seq_length, dtype=jnp.int32)
    cosine, sine_tab = rotary_tables(query_pos, HEAD_DIM)
    causal = key_pos[None, :] <= query_pos[:, None]
    attn_cols = HEADS * HEAD_DIM
    kv_cols = KV_HEADS * HEAD_DIM
    groups = HEADS // KV_HEADS
    scale = HEAD_DIM ** (-0.5)
    state = tokens.astype(jnp.float32)
    records = []
    for layer_index in range(LAYERS):
        gathered = fetch_layer(w_qkv, w_out, w_gate_up, w_down, gains, layer_index)
        qkv_w, out_w, gu_w, down_w, gain_pair = gathered
        normed, factor_one = norm_forward(state, gain_pair[0])
        normed_b = normed.astype(jnp.bfloat16)
        project = jnp.dot(normed_b, qkv_w, preferred_element_type=jnp.float32)
        query = rotate(project[:, :attn_cols].reshape(row_count, HEADS, HEAD_DIM), cosine, sine_tab)
        query_b = query.astype(jnp.bfloat16).reshape(row_count, KV_HEADS, groups, HEAD_DIM)
        key_part = project[:, attn_cols : attn_cols + kv_cols].reshape(
            row_count, KV_HEADS, HEAD_DIM
        )
        key_b = rotate(key_part, cosine, sine_tab).astype(jnp.bfloat16).reshape(row_count, kv_cols)
        value_b = project[:, attn_cols + kv_cols :].astype(jnp.bfloat16)
        local_pair = jnp.concatenate([key_b, value_b], axis=1)
        pair_all = fetch_pairs(local_pair)
        keys_all, values_all = split_pair(pair_all)
        scores = (
            jnp.einsum("qkgd,skd->kgqs", query_b, keys_all, preferred_element_type=jnp.float32)
            * scale
        )
        scores = jnp.where(causal[None, None], scores, MASKED)
        highest = jnp.max(scores, axis=-1, keepdims=True)
        log_total = highest + jnp.log(jnp.sum(jnp.exp(scores - highest), axis=-1, keepdims=True))
        attend_b = jnp.exp(scores - log_total).astype(jnp.bfloat16)
        mixed = jnp.einsum(
            "kgqs,skd->qkgd", attend_b, values_all, preferred_element_type=jnp.float32
        ).astype(jnp.bfloat16)
        middle = state + jnp.dot(
            mixed.reshape(row_count, attn_cols), out_w, preferred_element_type=jnp.float32
        )
        normed_two, factor_two = norm_forward(middle, gain_pair[1])
        normed_two_b = normed_two.astype(jnp.bfloat16)
        ff_width = down_w.shape[0]
        gate_up = jnp.dot(
            normed_two_b,
            gu_w.reshape(gu_w.shape[0], 2 * ff_width),
            preferred_element_type=jnp.float32,
        )
        gate = gate_up[:, :ff_width]
        up_part = gate_up[:, ff_width:]
        inner_b = (jax.nn.silu(gate) * up_part).astype(jnp.bfloat16)
        records.append(
            (
                state,
                normed_b,
                factor_one,
                query_b,
                local_pair,
                pair_all,
                mixed,
                log_total,
                middle,
                normed_two_b,
                factor_two,
                gate,
                up_part,
                inner_b,
            )
        )
        state = middle + jnp.dot(inner_b, down_w, preferred_element_type=jnp.float32)
    grad_state = cotangent
    shares_list = [None] * LAYERS
    for layer_index in reversed(range(LAYERS)):
        (
            layer_in,
            normed_b,
            factor_one,
            query_b,
            local_pair,
            pair_all,
            mixed,
            log_total,
            middle,
            normed_two_b,
            factor_two,
            gate,
            up_part,
            inner_b,
        ) = records[layer_index]
        gathered = fetch_again(w_qkv, w_out, w_gate_up, w_down, gains, layer_index)
        qkv_w, out_w, gu_w, down_w, gain_pair = gathered
        keys_all, values_all = split_pair(pair_all)
        ff_width = down_w.shape[0]
        grad_b = grad_state.astype(jnp.bfloat16)
        grad_down = jnp.dot(inner_b.T, grad_b, preferred_element_type=jnp.float32)
        grad_inner = jnp.dot(grad_b, down_w.T, preferred_element_type=jnp.float32)
        sigmoid_gate = jax.nn.sigmoid(gate)
        grad_gate = grad_inner * up_part * sigmoid_gate * (1.0 + gate * (1.0 - sigmoid_gate))
        grad_up = grad_inner * gate * sigmoid_gate
        grad_gu_b = jnp.concatenate([grad_gate, grad_up], axis=1).astype(jnp.bfloat16)
        gu_flat = gu_w.reshape(gu_w.shape[0], 2 * ff_width)
        grad_gu = jnp.dot(normed_two_b.T, grad_gu_b, preferred_element_type=jnp.float32).reshape(
            gu_w.shape
        )
        grad_normed_two = jnp.dot(grad_gu_b, gu_flat.T, preferred_element_type=jnp.float32)
        grad_middle_part, grad_gain_two = norm_backward(
            middle, factor_two, gain_pair[1], grad_normed_two
        )
        grad_middle = grad_state + grad_middle_part
        grad_middle_b = grad_middle.astype(jnp.bfloat16)
        grad_out = jnp.dot(
            mixed.reshape(row_count, attn_cols).T, grad_middle_b, preferred_element_type=jnp.float32
        )
        grad_mixed = (
            jnp.dot(grad_middle_b, out_w.T, preferred_element_type=jnp.float32)
            .astype(jnp.bfloat16)
            .reshape(mixed.shape)
        )
        scores = (
            jnp.einsum("qkgd,skd->kgqs", query_b, keys_all, preferred_element_type=jnp.float32)
            * scale
        )
        scores = jnp.where(causal[None, None], scores, MASKED)
        attend_f = jnp.exp(scores - log_total)
        attend_b = attend_f.astype(jnp.bfloat16)
        grad_attend = jnp.einsum(
            "qkgd,skd->kgqs", grad_mixed, values_all, preferred_element_type=jnp.float32
        )
        delta = jnp.sum(grad_mixed.astype(jnp.float32) * mixed.astype(jnp.float32), axis=-1)
        delta = jnp.transpose(delta, (1, 2, 0))[..., None]
        grad_scores_b = (attend_f * (grad_attend - delta) * scale).astype(jnp.bfloat16)
        grad_query = jnp.einsum(
            "kgqs,skd->qkgd", grad_scores_b, keys_all, preferred_element_type=jnp.float32
        )
        grad_key_all = jnp.einsum(
            "kgqs,qkgd->skd", grad_scores_b, query_b, preferred_element_type=jnp.float32
        )
        grad_value_all = jnp.einsum(
            "kgqs,qkgd->skd", attend_b, grad_mixed, preferred_element_type=jnp.float32
        )
        pair_grads = jnp.concatenate(
            [
                grad_key_all.reshape(seq_length, kv_cols),
                grad_value_all.reshape(seq_length, kv_cols),
            ],
            axis=1,
        )
        own_grads = lax.psum_scatter(
            pair_grads.astype(jnp.bfloat16), "ctx", scatter_dimension=0, tiled=True
        ).astype(jnp.float32)
        grad_key = unrotate(
            own_grads[:, :kv_cols].reshape(row_count, KV_HEADS, HEAD_DIM), cosine, sine_tab
        ).reshape(row_count, kv_cols)
        grad_value = own_grads[:, kv_cols:]
        grad_query = unrotate(
            grad_query.reshape(row_count, HEADS, HEAD_DIM), cosine, sine_tab
        ).reshape(row_count, attn_cols)
        grad_qkv_b = jnp.concatenate([grad_query, grad_key, grad_value], axis=1).astype(
            jnp.bfloat16
        )
        grad_qkv = jnp.dot(normed_b.T, grad_qkv_b, preferred_element_type=jnp.float32)
        grad_normed = jnp.dot(grad_qkv_b, qkv_w.T, preferred_element_type=jnp.float32)
        grad_state_part, grad_gain_one = norm_backward(
            layer_in, factor_one, gain_pair[0], grad_normed
        )
        grad_state = grad_middle + grad_state_part
        shares_list[layer_index] = reduce_grads(
            (grad_qkv, grad_out, grad_gu, grad_down, jnp.stack([grad_gain_one, grad_gain_two]))
        )
    stacked = [
        jnp.stack([shares_list[layer_index][which] for layer_index in range(LAYERS)])
        for which in range(5)
    ]
    return (state, grad_state, stacked[0], stacked[1], stacked[2], stacked[3], stacked[4])


def solution(mesh):
    return jax.shard_map(
        shards,
        mesh=mesh,
        in_specs=(
            P(("dp", "ctx"), None),
            P(("dp", "ctx"), None),
            P(None, ("dp", "ctx"), None),
            P(None, None, ("dp", "ctx")),
            P(None, ("dp", "ctx"), None, None),
            P(None, ("dp", "ctx"), None),
            P(None, None, ("dp", "ctx")),
        ),
        out_specs=(
            P(("dp", "ctx"), None),
            P(("dp", "ctx"), None),
            P(None, ("dp", "ctx"), None),
            P(None, None, ("dp", "ctx")),
            P(None, ("dp", "ctx"), None, None),
            P(None, ("dp", "ctx"), None),
            P(None, None, ("dp", "ctx")),
        ),
        check_vma=False,
    )
```

profile of v0, /device:TPU:0, one launch (start us, length us, event | category | flops | bytes accessed | tf_op | source)
XLA Modules:
  0.0 2717.9 jit_solution(81654333496502707)
XLA Ops:
  10.0 83.4 %all-gather = bf16[1,2,1536]{1,0,2:T(2,128)(2,1)S(1)} all-gather(bf16[1,2,48]{1,0,2:T(2,128)(2,1)S(1)} %copy.140), channel_id=2, replica_groups=mesh['dp'=8,'ctx'=4] {'dp','ctx'}, dimensions={2}, use_global_device_ids=true | all-gather | bytes 6336 | tf_op jit(solution)/shard_map/all_gather | solution.py:83
  94.8 25.1 fusion.68
  137.0 77.0 %all-gather.5 = bf16[1,2,1536]{1,0,2:T(2,128)(2,1)S(1)} all-gather(bf16[1,2,48]{1,0,2:T(2,128)(2,1)S(1)} %copy.142), channel_id=7, replica_groups=mesh['dp'=8,'ctx'=4] {'dp','ctx'}, dimensions={2}, use_global_device_ids=true | all-gather | bytes 6336 | tf_op jit(solution)/shard_map/all_gather | solution.py:83
  214.0 25.3 fusion.66
  250.2 139.6 %all-gather.29.cloned.1.call-done = bf16[1,1536,2,4096]{3,2,0,1:T(2,128)(2,1)} async-done(((bf16[1,48,2,4096]{3,2,0,1:T(2,128)(2,1)}), bf16[1,1536,2,4096]{3,2,0,1:T(2,128)(2,1)}) %all-gather.29.cloned.1.call-update) | async-done | bytes 25165840 | tf_op jit(solution)/shard_map/all_gather | solution.py:81
  389.8 26.9 copy.148
  416.7 10.4 fusion.107
  429.8 57.6 %all-gather.31.cloned.1.call-done = bf16[1,4096,1536]{2,1,0:T(8,128)(2,1)} async-done(((bf16[1,128,1536]{2,1,0:T(8,128)(2,1)}), bf16[1,4096,1536]{2,1,0:T(8,128)(2,1)}) %all-gather.31.cloned.1.call-update) | async-done | bytes 12582928 | tf_op jit(solution)/shard_map/all_gather | solution.py:82
  493.8 77.0 %all-gather.33.cloned.1.call-done = bf16[1,1536,3072]{2,1,0:T(8,128)(2,1)} async-done(((bf16[1,48,3072]{2,1,0:T(8,128)(2,1)}), bf16[1,1536,3072]{2,1,0:T(8,128)(2,1)}) %all-gather.33.cloned.1.call-update) | async-done | bytes 9437200 | tf_op jit(solution)/shard_map/all_gather | solution.py:79
  579.8 147.9 %all-gather.37.cloned.1.call-done = bf16[1,1536,2,4096]{3,2,0,1:T(2,128)(2,1)} async-done(((bf16[1,48,2,4096]{3,2,0,1:T(2,128)(2,1)}), bf16[1,1536,2,4096]{3,2,0,1:T(2,128)(2,1)}) %all-gather.37.cloned.1.call-update) | async-done | bytes 25165840 | tf_op jit(solution)/shard_map/all_gather | solution.py:81
  727.6 27.3 %copy.149 = bf16[192,8,2,4096]{3,1,2,0:T(8,128)(2,1)} copy(bf16[192,8,2,4096]{3,2,1,0:T(2,128)(2,1)} %bitcast.252) | data formatting | bytes 50331648
  758.0 7.1 all-gather.23.cloned.1.call-done
  777.5 52.9 %all-gather.35.cloned.1.call-done = bf16[1,1536,1536]{1,2,0:T(8,128)(2,1)} async-done(((bf16[1,1536,48]{1,2,0:T(8,128)(2,1)}), bf16[1,1536,1536]{1,2,0:T(8,128)(2,1)}) %all-gather.35.cloned.1.call-update) | async-done | bytes 4718608 | tf_op jit(solution)/shard_map/all_gather | solution.py:80
  834.5 14.1 fusion.108
  848.6 79.9 %all-gather.39.cloned.1.call-done = bf16[1,4096,1536]{2,1,0:T(8,128)(2,1)} async-done(((bf16[1,128,1536]{2,1,0:T(8,128)(2,1)}), bf16[1,4096,1536]{2,1,0:T(8,128)(2,1)}) %all-gather.39.cloned.1.call-update) | async-done | bytes 12582928 | tf_op jit(solution)/shard_map/all_gather | solution.py:82
  928.5 11.9 multiply_convert_fusion.3
  940.4 14.7 multiply_reduce_fusion
  979.7 30.4 %reduce-scatter.55.cloned.1.call-done = bf16[128,1536]{1,0:T(8,128)(2,1)} async-done(((bf16[512,1536]{1,0:T(8,128)(2,1)}), bf16[128,1536]{1,0:T(8,128)(2,1)}) %reduce-scatter.55.cloned.1.call-update) | async-done | bytes 393232
  1014.9 7.3 multiply_reduce_fusion.1
  1022.6 10.7 multiply_convert_fusion.1
  1033.3 14.8 multiply_reduce_fusion.2
  1075.3 28.4 %reduce-scatter.57.cloned.1.call-done = bf16[128,1536]{1,0:T(8,128)(2,1)} async-done(((bf16[512,1536]{1,0:T(8,128)(2,1)}), bf16[128,1536]{1,0:T(8,128)(2,1)}) %reduce-scatter.57.cloned.1.call-update) | async-done | bytes 393232
  1109.1 8.2 fusion.65
  1128.5 13.4 convolution_convert_fusion
  1141.9 41.2 %convert_element_type.225 = bf16[1536,2,4096]{2,1,0:T(2,128)(2,1)} reshape(bf16[1536,8192]{1,0:T(8,128)(2,1)} %convolution_convert_fusion) | data formatting | bytes 50331648 | tf_op jit(solution)/shard_map/convert_element_type | solution.py:110
  1183.2 14.4 convolution_convert_fusion.1
  1197.6 41.3 %convert_element_type.223 = bf16[1536,2,4096]{2,1,0:T(2,128)(2,1)} reshape(bf16[1536,8192]{1,0:T(8,128)(2,1)} %convolution_convert_fusion.1) | data formatting | bytes 50331648 | tf_op jit(solution)/shard_map/convert_element_type | solution.py:110
  1240.0 7.0 convolution_convert_fusion.4
  1248.3 7.1 convolution_convert_fusion.5
  1256.6 7.5 convolution_convert_fusion.2
  1265.3 7.4 convolution_convert_fusion.3
  1274.8 16.3 reduce-scatter.39.cloned.1.call-done
  1292.7 309.2 %all-reduce.11.cloned.1.call-done = bf16[1536,2,4096]{2,1,0:T(2,128)(2,1)} async-done(((bf16[1536,2,4096]{2,1,0:T(2,128)(2,1)}), bf16[1536,2,4096]{2,1,0:T(2,128)(2,1)}) %all-reduce.11.cloned.1.call-update) | async-done | bytes 25165840
  1608.5 304.6 %all-reduce.9.cloned.1.call-done = bf16[1536,2,4096]{2,1,0:T(2,128)(2,1)} async-done(((bf16[1536,2,4096]{2,1,0:T(2,128)(2,1)}), bf16[1536,2,4096]{2,1,0:T(2,128)(2,1)}) %all-reduce.9.cloned.1.call-update) | async-done | bytes 25165840
  1919.9 73.4 %reduce-scatter.35.cloned.1.call-done = bf16[192,3072]{1,0:T(8,128)(2,1)} async-done(((bf16[1536,3072]{1,0:T(8,128)(2,1)}), bf16[192,3072]{1,0:T(8,128)(2,1)}) %reduce-scatter.35.cloned.1.call-update) | async-done | bytes 1179664 | tf_op jit(solution)/shard_map/reduce_scatter | solution.py:103
  1993.3 79.8 %reduce-scatter.31.cloned.1.call-done = bf16[192,3072]{1,0:T(8,128)(2,1)} async-done(((bf16[1536,3072]{1,0:T(8,128)(2,1)}), bf16[192,3072]{1,0:T(8,128)(2,1)}) %reduce-scatter.31.cloned.1.call-update) | async-done | bytes 1179664 | tf_op jit(solution)/shard_map/reduce_scatter | solution.py:103
  2073.2 95.9 %reduce-scatter.51.cloned.1.call-done = bf16[512,1536]{1,0:T(8,128)(2,1)} async-done(((bf16[4096,1536]{1,0:T(8,128)(2,1)}), bf16[512,1536]{1,0:T(8,128)(2,1)}) %reduce-scatter.51.cloned.1.call-update) | async-done | bytes 1572880 | tf_op jit(solution)/shard_map/reduce_scatter | solution.py:112
  2169.4 95.6 %reduce-scatter.47.cloned.1.call-done = bf16[512,1536]{1,0:T(8,128)(2,1)} async-done(((bf16[4096,1536]{1,0:T(8,128)(2,1)}), bf16[512,1536]{1,0:T(8,128)(2,1)}) %reduce-scatter.47.cloned.1.call-update) | async-done | bytes 1572880 | tf_op jit(solution)/shard_map/reduce_scatter | solution.py:112
  2266.3 7.7 fusion.43
  2274.0 12.2 reduce-scatter.65.cloned.1.call-done
  2288.2 17.5 reduce-scatter.61.cloned.1.call-done
  2307.1 21.1 reduce-scatter.45.cloned.1.call-done
  2328.1 22.5 reduce-scatter.41.cloned.1.call-done
  2352.5 222.5 %all-reduce.13.cloned.1.call-done = (bf16[192,2,4096]{2,1,0:T(2,128)(2,1)}, bf16[192,2,4096]{2,1,0:T(2,128)(2,1)}) async-done(((bf16[192,2,4096]{2,1,0:T(2,128)(2,1)}, bf16[192,2,4096]{2,1,0:T(2,128)(2,1)}), (bf16[192,2,4096]{2,1,0:T(2,128)(2,1)}, bf16[192,2,4096]{2,1,0:T(2,128)(2,1)})) %all-reduce.13.cloned.1.call-update) | async-done | bytes 6291472
  2581.5 24.0 reduce-scatter.37.cloned.1.call-done
  2605.4 30.2 %reduce-scatter.33.cloned.1.call-done = bf16[48,3072]{1,0:T(8,128)(2,1)} async-done(((bf16[192,3072]{1,0:T(8,128)(2,1)}), bf16[48,3072]{1,0:T(8,128)(2,1)}) %reduce-scatter.33.cloned.1.call-update) | async-done | bytes 294928 | tf_op jit(solution)/shard_map/reduce_scatter | solution.py:120
  2637.8 34.0 %reduce-scatter.53.cloned.1.call-done = bf16[128,1536]{1,0:T(8,128)(2,1)} async-done(((bf16[512,1536]{1,0:T(8,128)(2,1)}), bf16[128,1536]{1,0:T(8,128)(2,1)}) %reduce-scatter.53.cloned.1.call-update) | async-done | bytes 393232 | tf_op jit(solution)/shard_map/reduce_scatter | solution.py:129
  2671.9 36.6 %reduce-scatter.49.cloned.1.call-done = bf16[128,1536]{1,0:T(8,128)(2,1)} async-done(((bf16[512,1536]{1,0:T(8,128)(2,1)}), bf16[128,1536]{1,0:T(8,128)(2,1)}) %reduce-scatter.49.cloned.1.call-update) | async-done | bytes 393232 | tf_op jit(solution)/shard_map/reduce_scatter | solution.py:129
  (286 shorter events, 180.7 us)
Async XLA Ops:
  7.2 112.8 %copy-start.8 = (bf16[128,1536]{1,0:T(8,128)(2,1)S(1)}, bf16[128,1536]{1,0:T(8,128)(2,1)}, u32[]{:S(2)}) copy-start(bf16[128,1536]{1,0:T(8,128)(2,1)} %param.7) | copy-start | bytes 1179652
  7.2 112.8 %all-gather.25.cloned.1.call-start = ((), (), s32[]{:S(2)}) async-start(), calls=%async_computation.32 | async-start | bytes 9732096 | tf_op jit(solution)/shard_map/all_gather | solution.py:79
  9.2 230.7 %all-gather.21.cloned.1.call-start = ((), (), s32[]{:S(2)}) async-start(), calls=%async_computation.18 | async-start | bytes 1966080 | tf_op jit(solution)/shard_map/all_gather | solution.py:98
  94.6 30.5 %copy-start.44 = (f32[128]{0:T(128)}, f32[128]{0:T(128)S(1)}, u32[]{:S(2)}) copy-start(f32[128]{0:T(128)S(1)} %add_rsqrt_fusion.3) | copy-start | bytes 1540
  126.0 8.5 copy-start.33
  128.0 118.1 %all-gather.27.cloned.1.call-start = ((), (), s32[]{:S(2)}) async-start(), calls=%async_computation.33 | async-start | bytes 4866048 | tf_op jit(solution)/shard_map/all_gather | solution.py:80
  129.8 260.0 %all-gather.29.cloned.1.call-start = ((), (), s32[]{:S(2)}) async-start(), calls=%async_computation.34 | async-start | bytes 25952256 | tf_op jit(solution)/shard_map/all_gather | solution.py:81
  134.5 352.8 %all-gather.31.cloned.1.call-start = ((), (), s32[]{:S(2)}) async-start(), calls=%async_computation.35 | async-start | bytes 12976128 | tf_op jit(solution)/shard_map/all_gather | solution.py:82
  135.5 435.4 %all-gather.33.cloned.1.call-start = ((), (), s32[]{:S(2)}) async-start(), calls=%async_computation.36 | async-start | bytes 9732096 | tf_op jit(solution)/shard_map/all_gather | solution.py:79
  136.1 591.5 %all-gather.37.cloned.1.call-start = ((), (), s32[]{:S(2)}) async-start(), calls=%async_computation.38 | async-start | bytes 25952256 | tf_op jit(solution)/shard_map/all_gather | solution.py:81
  136.8 628.2 %all-gather.23.cloned.1.call-start = ((), (), s32[]{:S(2)}) async-start(), calls=%async_computation.19 | async-start | bytes 1966080 | tf_op jit(solution)/shard_map/all_gather | solution.py:98
  429.7 64.1 %copy-start.6 = (bf16[128,4096]{1,0:T(8,128)(2,1)}, bf16[128,4096]{1,0:T(8,128)(2,1)S(1)}, u32[]{:S(2)}) copy-start(bf16[128,4096]{1,0:T(8,128)(2,1)S(1)} %multiply_convert_fusion.5) | copy-start | bytes 3145732
  578.4 251.9 %all-gather.35.cloned.1.call-start = ((), (), s32[]{:S(2)}) async-start(), calls=%async_computation.37 | async-start | bytes 4866048 | tf_op jit(solution)/shard_map/all_gather | solution.py:80
  579.1 349.4 %all-gather.39.cloned.1.call-start = ((), (), s32[]{:S(2)}) async-start(), calls=%async_computation.39 | async-start | bytes 12976128 | tf_op jit(solution)/shard_map/all_gather | solution.py:82
  579.7 430.4 %reduce-scatter.55.cloned.1.call-start = ((), (), s32[]{:S(2)}) async-start(), calls=%async_computation.40 | async-start | bytes 1966080
  727.6 27.3 %slice-start = ((f32[128,3072]{1,0:T(8,128)}), f32[128,1536]{1,0:T(8,128)S(1)}, s32[]{:S(2)}) async-start(f32[128,3072]{1,0:T(8,128)} %copy-done.19), calls=%async_computation.49 | async-start | bytes 1572864 | tf_op jit(solution)/shard_map/slice | solution.py:158
  976.4 127.3 %reduce-scatter.57.cloned.1.call-start = ((), (), s32[]{:S(2)}) async-start(), calls=%async_computation.41 | async-start | bytes 1966080
  1013.7 8.5 copy-start.29
  1014.8 7.4 copy-start.31
  1014.9 7.4 copy-start.12
  1014.9 7.7 copy-start.5
  1022.6 10.7 copy-start.16
  1069.3 203.5 %reduce-scatter.63.cloned.1.call-start = ((), (), s32[]{:S(2)}) async-start(), calls=%async_computation.44 | async-start | bytes 442368
  1070.4 38.7 %copy-start.43 = (f32[1536]{0:T(1024)S(1)}, f32[1536]{0:T(1024)}, u32[]{:S(2)}) copy-start(f32[1536]{0:T(1024)} %copy-done.42) | copy-start | bytes 18436
  1070.4 38.7 %copy-start.45 = (f32[128]{0:T(128)S(1)}, f32[128]{0:T(128)}, u32[]{:S(2)}) copy-start(f32[128]{0:T(128)} %copy-done.44) | copy-start | bytes 1540
  1073.5 200.0 %reduce-scatter.59.cloned.1.call-start = ((), (), s32[]{:S(2)}) async-start(), calls=%async_computation.42 | async-start | bytes 442368
  1109.0 8.2 copy-start.40
  1118.3 155.8 %reduce-scatter.43.cloned.1.call-start = ((), (), s32[]{:S(2)}) async-start(), calls=%async_computation.26 | async-start | bytes 5308416 | tf_op jit(solution)/shard_map/reduce_scatter | solution.py:106
  1123.7 167.5 %reduce-scatter.39.cloned.1.call-start = ((), (), s32[]{:S(2)}) async-start(), calls=%async_computation.24 | async-start | bytes 5308416 | tf_op jit(solution)/shard_map/reduce_scatter | solution.py:106
  1128.4 473.4 %all-reduce.11.cloned.1.call-start = ((), (), s32[]{:S(2)}) async-start(), calls=%async_computation.47 | async-start | bytes 50331648
  1183.1 730.1 %all-reduce.9.cloned.1.call-start = ((), (), s32[]{:S(2)}) async-start(), calls=%async_computation.46 | async-start | bytes 50331648
  1238.9 754.4 %reduce-scatter.35.cloned.1.call-start = ((), (), s32[]{:S(2)}) async-start(), calls=%async_computation.22 | async-start | bytes 10616832 | tf_op jit(solution)/shard_map/reduce_scatter | solution.py:103
  1247.0 826.1 %reduce-scatter.31.cloned.1.call-start = ((), (), s32[]{:S(2)}) async-start(), calls=%async_computation.20 | async-start | bytes 10616832 | tf_op jit(solution)/shard_map/reduce_scatter | solution.py:103
  1255.4 913.7 %reduce-scatter.51.cloned.1.call-start = ((), (), s32[]{:S(2)}) async-start(), calls=%async_computation.30 | async-start | bytes 14155776 | tf_op jit(solution)/shard_map/reduce_scatter | solution.py:112
  1264.1 1000.9 %reduce-scatter.47.cloned.1.call-start = ((), (), s32[]{:S(2)}) async-start(), calls=%async_computation.28 | async-start | bytes 14155776 | tf_op jit(solution)/shard_map/reduce_scatter | solution.py:112
  1272.7 18.7 copy-start.49
  1272.7 1013.5 %reduce-scatter.65.cloned.1.call-start = ((), (), s32[]{:S(2)}) async-start(), calls=%async_computation.45 | async-start | bytes 61440
  1273.5 1032.2 %reduce-scatter.61.cloned.1.call-start = ((), (), s32[]{:S(2)}) async-start(), calls=%async_computation.43 | async-start | bytes 61440
  1274.0 1054.1 %reduce-scatter.45.cloned.1.call-start = ((), (), s32[]{:S(2)}) async-start(), calls=%async_computation.27 | async-start | bytes 737280 | tf_op jit(solution)/shard_map/reduce_scatter | solution.py:123
  1274.8 1075.8 %reduce-scatter.41.cloned.1.call-start = ((), (), s32[]{:S(2)}) async-start(), calls=%async_computation.25 | async-start | bytes 737280 | tf_op jit(solution)/shard_map/reduce_scatter | solution.py:123
  1291.2 1283.8 %all-reduce.13.cloned.1.call-start = ((), (), s32[]{:S(2)}) async-start(), calls=%async_computation.48 | async-start | bytes 12582912
  1919.8 345.2 %copy-start.48 = (u32[32]{0:T(128)S(1)}, u32[32]{0:T(128)}, u32[]{:S(2)}) copy-start(u32[32]{0:T(128)} %constant.44) | copy-start | bytes 388
  1919.8 685.6 %reduce-scatter.37.cloned.1.call-start = ((), (), s32[]{:S(2)}) async-start(), calls=%async_computation.23 | async-start | bytes 1474560 | tf_op jit(solution)/shard_map/reduce_scatter | solution.py:120
  1993.3 642.4 %reduce-scatter.33.cloned.1.call-start = ((), (), s32[]{:S(2)}) async-start(), calls=%async_computation.21 | async-start | bytes 1474560 | tf_op jit(solution)/shard_map/reduce_scatter | solution.py:120
  2073.2 598.7 %reduce-scatter.53.cloned.1.call-start = ((), (), s32[]{:S(2)}) async-start(), calls=%async_computation.31 | async-start | bytes 1966080 | tf_op jit(solution)/shard_map/reduce_scatter | solution.py:129
  2169.1 539.4 %reduce-scatter.49.cloned.1.call-start = ((), (), s32[]{:S(2)}) async-start(), calls=%async_computation.29 | async-start | bytes 1966080 | tf_op jit(solution)/shard_map/reduce_scatter | solution.py:129
  2266.3 20.8 copy-start.10
  2266.3 20.7 copy-start.38
  (34 other events, 99.0 us)
Sparse Core Ops, SparseCore 0:
  11.4 88.8 all-gather.24
  128.1 39.2 all-gather.20
  170.2 62.6 all-gather.26
  236.3 153.4 all-gather.28
  393.1 94.2 all-gather.30
  490.6 80.2 all-gather.32
  574.3 153.2 all-gather.36
  729.8 35.2 all-gather.22
  767.9 62.3 all-gather.34
  833.6 94.8 all-gather.38
  976.5 33.5 reduce-scatter.54
  1069.4 34.2 reduce-scatter.56
  1106.8 32.7 reduce-scatter.62
  1142.5 33.7 reduce-scatter.58
  1179.6 53.8 reduce-scatter.42
  1237.2 53.8 reduce-scatter.38
  1294.7 307.1 all-reduce.10
  1605.9 307.2 all-reduce.8
  1916.7 76.5 reduce-scatter.34
  1996.6 76.4 reduce-scatter.30
  2076.6 92.3 reduce-scatter.50
  2172.6 92.3 reduce-scatter.46
  2267.2 18.9 reduce-scatter.64
  2288.4 17.2 reduce-scatter.60
  2308.0 20.1 reduce-scatter.44
  2330.3 20.2 reduce-scatter.40
  2353.4 221.4 all-reduce.12
  2577.3 28.1 reduce-scatter.36
  2607.8 27.8 reduce-scatter.32
  2637.8 33.9 reduce-scatter.52
  2674.2 34.2 reduce-scatter.48
where the time goes:
time: 2730 us; the launch traced here: 2720 us
  waiting for transfers between devices  2020 us (74%)
  matrix products  222 us (8%)
  local copies, waits for them, and re-layouts  210 us (8%)
  blocking collectives  160 us (6%)
  other arithmetic  85.1 us (3%)
    unnamed x40, waiting for transfers between devices  930 us
    all_gather x2, waiting for transfers between devices, fetch_layer(): lax.all_gather(w_gate_up[layer_index], ('dp', 'ctx'), axis=0, tiled=True)  287 us
    reduce_scatter x2, waiting for transfers between devices, reduce_grads(): lax.psum_scatter(grad_tuple[3].astype(jnp.bfloat16), 'dp', scatter_dimens...  191 us
    all_gather x2, blocking collectives, fetch_layer(): lax.all_gather(gains[layer_index], ('dp', 'ctx'), axis=1, tiled=True)  160 us
    reduce_scatter x2, waiting for transfers between devices, reduce_grads(): lax.psum_scatter(grad_tuple[0].astype(jnp.bfloat16), 'dp', scatter_dimens...  153 us
    all_gather x2, waiting for transfers between devices, fetch_layer(): lax.all_gather(w_down[layer_index], ('dp', 'ctx'), axis=0, tiled=True)  137 us
    unnamed x119, local copies, waits for them, and re-layouts  100 us
    convert_element_type x2, local copies, waits for them, and re-layouts, reduce_grads(): grad_tuple[2].astype(jnp.bfloat16)  82.5 us
  transfers between devices with their start and end apart: 31, of which 25 were waited for; matrix products, arithmetic and copies ran while one was open for 14% of the time, Pallas kernels for 0%

commit v1 on v0

v1 whole, which is shorter than its diff:
```python
import functools

import jax
import jax.numpy as jnp
from jax import lax
from jax.experimental import pallas as pl
from jax.experimental.pallas import tpu as pltpu
from jax.sharding import PartitionSpec as P

HEADS = 16
KV_HEADS = 8
HEAD_DIM = 96
LAYERS = 2
RANKS = 4
GAIN_COLS = 128

NORM_EPS = 1e-05
ROPE_BASE = 100000.0
MASKED = -1e30
MESH = pl.DeviceIdType.MESH
BF16 = jnp.bfloat16
F32 = jnp.float32
VMEM_BYTES = 60 * 1024 * 1024


class Place:
    def __init__(self):
        self.dp = lax.axis_index("dp")
        self.ctx = lax.axis_index("ctx")
        self.core = lax.rem(self.dp, 2)
        self.x = lax.rem(lax.div(self.dp, 2), 2)
        self.a = lax.div(self.dp, 4)
        self.zh = lax.div(self.ctx, 2)
        self.zl = lax.rem(self.ctx, 2)
        self.rank = self.x * 2 + self.zl

    def rank_peers(self):
        dpx = self.dp + 2 - 4 * self.x
        ctz = self.ctx + 1 - 2 * self.zl
        x2, z2 = 1 - self.x, 1 - self.zl
        return (
            ((dpx, self.ctx), x2 * 2 + self.zl),
            ((self.dp, ctz), self.x * 2 + z2),
            ((dpx, ctz), x2 * 2 + z2),
        )

    def core_peer(self):
        return (self.dp + 1 - 2 * self.core, self.ctx)

    def zh_peer(self):
        return (self.dp, self.ctx + 2 - 4 * self.zh)

    def a_peer(self, k, count):
        ahead = lax.rem(self.a + k, count)
        behind = lax.rem(self.a + count - k, count)
        return (self.dp + (ahead - self.a) * 4, self.ctx), ahead, behind


def greet(devices):
    barrier = pltpu.get_barrier_semaphore()
    for device in devices:
        pl.semaphore_signal(barrier, inc=1, device_id=device, device_id_type=MESH)
    pl.semaphore_wait(barrier, len(devices))


def remote(src, dst, send, recv, device):
    return pltpu.make_async_remote_copy(
        src_ref=src, dst_ref=dst, send_sem=send, recv_sem=recv, device_id=device, device_id_type=MESH
    )


def products(x, w_ref, count, tile, transposed, use):
    @pl.loop(0, count // tile)
    def _(j):
        cols = pl.ds(pl.multiple_of(j * tile, tile), tile)
        if transposed:
            w, dims = w_ref[cols, :], (((1,), (1,)), ((), ()))
        else:
            w, dims = w_ref[:, cols], (((1,), (0,)), ((), ()))
        use(cols, lax.dot_general(x(), w, dims, preferred_element_type=F32))


def norm_rows(h, gain):
    factor = lax.rsqrt(jnp.mean(h * h, axis=-1, keepdims=True) + NORM_EPS)
    return (h * factor * gain).astype(BF16)


def norm_rows_back(h, gain, grad):
    factor = lax.rsqrt(jnp.mean(h * h, axis=-1, keepdims=True) + NORM_EPS)
    z = grad * gain
    inner = jnp.sum(z * h, axis=-1, keepdims=True)
    back = factor * z - h * (factor * factor * factor * inner / h.shape[-1])
    return back, jnp.sum(grad * h * factor, axis=0, keepdims=True)


class Exchange:
    def __init__(self, place, land, send, recv, base):
        self.place, self.land, self.send, self.recv, self.base = place, land, send, recv, base
        self.started = []

    def spread(self):
        me = self.place.rank
        for i, (device, _) in enumerate(self.place.rank_peers()):
            copy = remote(
                self.land.at[me], self.land.at[me],
                self.send.at[self.base + i], self.recv.at[self.base + i], device,
            )
            copy.start()
            self.started.append(copy)

    def push(self, i, out):
        copy = remote(
            out.at[i], self.land.at[i],
            self.send.at[self.base + i], self.recv.at[self.base + i],
            self.place.rank_peers()[i][0],
        )
        copy.start()
        self.started.append(copy)


def head_kernel(rows, h_ref, gain_ref, wq_hbm, proj_ref, ng_hbm, wq, land, send, recv, local):
    load = pltpu.make_async_copy(wq_hbm.at[:, pl.ds(0, wq.shape[1])], wq, local.at[0])
    load.start()
    place = Place()
    greet([d for d, _ in place.rank_peers()])
    land[place.rank] = norm_rows(h_ref[...], gain_ref[...])
    gather = Exchange(place, land, send, recv, 0)
    gather.spread()
    load.wait()
    project_blocks(place, rows, gather, wq, proj_ref)
    keep = pltpu.make_async_copy(land, ng_hbm, local.at[0])
    keep.start()
    for copy in gather.started:
        copy.wait_send()
    keep.wait()


def project_blocks(place, rows, gather, wq, proj_ref):
    land = gather.land
    count = wq.shape[1]

    def block(rank):
        span = pl.ds(pl.multiple_of(rank * rows, rows), rows)

        def use(cols, y):
            proj_ref[span, cols] = y

        products(lambda: land[rank], wq, count, 256, False, use)

    block(place.rank)
    for i, (_, rank) in enumerate(place.rank_peers()):
        gather.started[i].wait_recv()
        block(rank)


def body_kernel(rows, more, *refs):
    refs = list(refs)
    take = lambda n: [refs.pop(0) for _ in range(n)]
    o_ref, h_ref, gain_ref, wo_hbm, wgu_hbm, wd_hbm = take(6)
    if more:
        gain_next, wq_hbm = take(2)
    h1_ref, hn_ref, gate_ref, up_ref, u_ref, ng_hbm = take(6)
    if more:
        proj_ref, nn_hbm = take(2)
    wo, wgu, wd = take(3)
    if more:
        (wq,) = take(1)
    out_a, land_a, land_n, out_b, land_b = take(5)
    if more:
        (land_q,) = take(1)
    send, recv, local = take(3)

    loads = [
        pltpu.make_async_copy(wo_hbm, wo, local.at[0]),
        pltpu.make_async_copy(wgu_hbm, wgu, local.at[1]),
        pltpu.make_async_copy(wd_hbm, wd, local.at[2]),
    ]
    if more:
        loads.append(pltpu.make_async_copy(wq_hbm.at[:, pl.ds(0, wq.shape[1])], wq, local.at[3]))
    for load in loads:
        load.start()
    place = Place()
    peers = place.rank_peers()
    greet([d for d, _ in peers])
    width = h_ref.shape[1]
    hidden = wd.shape[0]
    loads[0].wait()

    total = Exchange(place, land_a, send, recv, 0)
    for i in (2, 0, 1):
        span = pl.ds(pl.multiple_of(peers[i][1] * rows, rows), rows)

        def use(cols, y, i=i):
            out_a[i, :, cols] = y.astype(BF16)

        products(lambda: o_ref[span, :], wo, width, 512, True, use)
        total.push(i, out_a)
    span = pl.ds(pl.multiple_of(place.rank * rows, rows), rows)

    def use_own(cols, y):
        h1_ref[:, cols] = h_ref[:, cols] + y

    products(lambda: o_ref[span, :], wo, width, 512, True, use_own)
    for copy in total.started:
        copy.wait_recv()
    h1 = h1_ref[...] + land_a[0].astype(F32) + land_a[1].astype(F32) + land_a[2].astype(F32)
    h1_ref[...] = h1
    land_n[place.rank] = norm_rows(h1, gain_ref[...])
    gather = Exchange(place, land_n, send, recv, 3)
    gather.spread()
    loads[1].wait()
    loads[2].wait()

    def inner_block(rank):
        span = pl.ds(pl.multiple_of(rank * rows, rows), rows)

        @pl.loop(0, hidden // 256)
        def _(j):
            cols = pl.ds(pl.multiple_of(j * 256, 256), 256)
            ups = pl.ds(pl.multiple_of(j * 256 + hidden, 256), 256)
            gate = jnp.dot(land_n[rank], wgu[:, cols], preferred_element_type=F32)
            up = jnp.dot(land_n[rank], wgu[:, ups], preferred_element_type=F32)
            gate_ref[span, cols] = gate
            up_ref[span, cols] = up
            u_ref[span, cols] = (gate / (1.0 + jnp.exp(-gate)) * up).astype(BF16)

        return span

    span = inner_block(place.rank)

    def use_down(cols, y):
        hn_ref[:, cols] = h1_ref[:, cols] + y

    products(lambda: u_ref[span, :], wd, width, 512, False, use_down)
    second = Exchange(place, land_b, send, recv, 6)
    for i, (_, rank) in enumerate(peers):
        gather.started[i].wait_recv()
        span = inner_block(rank)

        def use(cols, y, i=i):
            out_b[i, :, cols] = y.astype(BF16)

        products(lambda: u_ref[span, :], wd, width, 512, False, use)
        second.push(i, out_b)
    keep = pltpu.make_async_copy(land_n, ng_hbm, local.at[0])
    keep.start()
    for copy in second.started:
        copy.wait_recv()
    hn = hn_ref[...] + land_b[0].astype(F32) + land_b[1].astype(F32) + land_b[2].astype(F32)
    hn_ref[...] = hn
    every = [total, gather, second]
    if more:
        land_q[place.rank] = norm_rows(hn, gain_next[...])
        third = Exchange(place, land_q, send, recv, 9)
        third.spread()
        loads[3].wait()
        project_blocks(place, rows, third, wq, proj_ref)
        keep_next = pltpu.make_async_copy(land_q, nn_hbm, local.at[1])
        keep_next.start()
        keep_next.wait()
        every.append(third)
    keep.wait()
    for exchange in every:
        for copy in exchange.started:
            copy.wait_send()


def back_kernel(rows, first, last, *refs):
    refs = list(refs)
    take = lambda n: [refs.pop(0) for _ in range(n)]
    if first:
        (g_ref,) = take(1)
    else:
        dqkv_ref, wq_hbm, ghin_ref, hin_ref, gainin_ref = take(5)
    if not last:
        wd_hbm, wgu_hbm, wo_hbm, gate_ref, up_ref, h1_ref, gain_ref = take(7)
    if not first:
        gnew_ref, ggin_ref = take(2)
    if not last:
        gbg_hbm, dgu_ref, gh_ref, gg_ref, ghg_hbm, do_ref = take(6)
    if not first:
        wq, out_a, land_a = take(3)
    if not last:
        wd, wgu, wo, land_g, out_b, land_b, land_h = take(7)
    send, recv, local = take(3)

    loads = []
    if not first:
        loads.append(pltpu.make_async_copy(wq_hbm.at[:, pl.ds(0, wq.shape[1])], wq, local.at[0]))
    if not last:
        loads.append(pltpu.make_async_copy(wd_hbm, wd, local.at[1]))
        loads.append(pltpu.make_async_copy(wgu_hbm, wgu, local.at[2]))
        loads.append(pltpu.make_async_copy(wo_hbm, wo, local.at[3]))
    for load in loads:
        load.start()
    place = Place()
    peers = place.rank_peers()
    greet([d for d, _ in peers])
    own = pl.ds(pl.multiple_of(place.rank * rows, rows), rows)
    every = []
    if not first:
        loads.pop(0).wait()
        width = ghin_ref.shape[1]
        total = Exchange(place, land_a, send, recv, 0)
        every.append(total)
        for i in (2, 0, 1):
            span = pl.ds(pl.multiple_of(peers[i][1] * rows, rows), rows)

            def use(cols, y, i=i):
                out_a[i, :, cols] = y.astype(BF16)

            products(lambda: dqkv_ref[span, :], wq, width, 512, True, use)
            total.push(i, out_a)

        def use_own(cols, y):
            gnew_ref[:, cols] = y

        products(lambda: dqkv_ref[own, :], wq, width, 512, True, use_own)
        for copy in total.started:
            copy.wait_recv()
        dn = gnew_ref[...] + land_a[0].astype(F32) + land_a[1].astype(F32) + land_a[2].astype(F32)
        back, ggain = norm_rows_back(hin_ref[...], gainin_ref[...], dn)
        gnew_ref[...] = ghin_ref[...] + back
        ggin_ref[...] = ggain
        g_ref = gnew_ref
    if not last:
        width = g_ref.shape[1]
        hidden = wd.shape[0]
        land_g[place.rank] = g_ref[...].astype(BF16)
        gather = Exchange(place, land_g, send, recv, 3)
        gather.spread()
        every.append(gather)
        loads[0].wait()
        loads[1].wait()

        def inner_block(rank):
            span = pl.ds(pl.multiple_of(rank * rows, rows), rows)

            @pl.loop(0, hidden // 256)
            def _(j):
                cols = pl.ds(pl.multiple_of(j * 256, 256), 256)
                ups = pl.ds(pl.multiple_of(j * 256 + hidden, 256), 256)
                du = lax.dot_general(
                    land_g[rank], wd[cols, :], (((1,), (1,)), ((), ())), preferred_element_type=F32
                )
                gate, up = gate_ref[span, cols], up_ref[span, cols]
                sg = 1.0 / (1.0 + jnp.exp(-gate))
                dgu_ref[span, cols] = (du * up * sg * (1.0 + gate * (1.0 - sg))).astype(BF16)
                dgu_ref[span, ups] = (du * gate * sg).astype(BF16)

            return span

        span = inner_block(place.rank)

        def use_mid(cols, y):
            gh_ref[:, cols] = y

        products(lambda: dgu_ref[span, :], wgu, width, 512, True, use_mid)
        second = Exchange(place, land_b, send, recv, 6)
        every.append(second)
        for i, (_, rank) in enumerate(peers):
            gather.started[i].wait_recv()
            span = inner_block(rank)

            def use(cols, y, i=i):
                out_b[i, :, cols] = y.astype(BF16)

            products(lambda: dgu_ref[span, :], wgu, width, 512, True, use)
            second.push(i, out_b)
        keep = pltpu.make_async_copy(land_g, gbg_hbm, local.at[0])
        keep.start()
        for copy in second.started:
            copy.wait_recv()
        dn = gh_ref[...] + land_b[0].astype(F32) + land_b[1].astype(F32) + land_b[2].astype(F32)
        back, ggain = norm_rows_back(h1_ref[...], gain_ref[...], dn)
        gh = g_ref[...] + back
        gh_ref[...] = gh
        gg_ref[...] = ggain
        land_h[place.rank] = gh.astype(BF16)
        third = Exchange(place, land_h, send, recv, 9)
        third.spread()
        every.append(third)
        loads[2].wait()

        def out_block(rank):
            span = pl.ds(pl.multiple_of(rank * rows, rows), rows)

            def use(cols, y):
                do_ref[span, cols] = y.astype(BF16)

            products(lambda: land_h[rank], wo, wo.shape[1], wo.shape[1], False, use)

        out_block(place.rank)
        for i, (_, rank) in enumerate(peers):
            third.started[i].wait_recv()
            out_block(rank)
        keep_h = pltpu.make_async_copy(land_h, ghg_hbm, local.at[1])
        keep_h.start()
        keep_h.wait()
        keep.wait()
    for exchange in every:
        for copy in exchange.started:
            copy.wait_send()


def gather_kernel(count, n_cols, *refs):
    pieces, down = refs[:n_cols], refs[n_cols]
    outs, down_out = refs[n_cols + 1 : 2 * n_cols + 1], refs[2 * n_cols + 1]
    send, recv, local = refs[2 * n_cols + 2 :]
    place = Place()
    peers = place.rank_peers()
    others = [place.a_peer(k, count) for k in range(1, count)]
    a, x, core, zh, zl = place.a, place.x, place.core, place.zh, place.zl
    greet([d for d, _ in peers] + [place.zh_peer(), place.core_peer()] + [o[0] for o in others])
    sends = []

    def go(src, dst, i, slot, device):
        copy = remote(src, dst, send.at[i, slot], recv.at[i, slot], device)
        copy.start()
        sends.append(copy)
        return copy

    first, locals_ = [], []
    down_local = pltpu.make_async_copy(down, down_out.at[a, core, zh], local.at[n_cols])
    down_local.start()
    for i in range(n_cols):
        mine = outs[i].at[a, x, core, zh, zl]
        first.append([go(pieces[i].at[rank], mine, i, j, device) for j, (device, rank) in enumerate(peers)])
        own = pltpu.make_async_copy(pieces[i].at[place.rank], mine, local.at[i])
        own.start()
        locals_.append(own)
    down_local.wait()

    def block(i, aa, zz):
        if i == n_cols:
            return down_out.at[aa, core, zz]
        return outs[i].at[aa, :, core, zz, :]

    def column(i, aa):
        if i == n_cols:
            return down_out.at[aa, core]
        return outs[i].at[aa, :, core, :, :]

    base_y = 8
    base_c = base_y + 2 * (count - 1)
    across, near, far, cores = {}, {}, {}, {}
    order = [n_cols] + list(range(n_cols))
    for i in order:
        if i < n_cols:
            for copy in first[i]:
                copy.wait_recv()
            locals_[i].wait()
        across[i] = go(block(i, a, zh), block(i, a, zh), i, 3, place.zh_peer())
        near[i] = [
            go(block(i, a, zh), block(i, a, zh), i, base_y + k, others[k][0]) for k in range(count - 1)
        ]
    for i in order:
        across[i].wait_recv()
        far[i] = [
            go(block(i, a, 1 - zh), block(i, a, 1 - zh), i, base_y + count - 1 + k, others[k][0])
            for k in range(count - 1)
        ]
        cores[i] = [go(column(i, a), column(i, a), i, base_c, place.core_peer())]
    for i in order:
        for k in range(count - 1):
            near[i][k].wait_recv()
            far[i][k].wait_recv()
            behind = others[k][2]
            cores[i].append(
                go(column(i, behind), column(i, behind), i, base_c + 1 + k, place.core_peer())
            )
    for i in order:
        for copy in cores[i]:
            copy.wait_recv()
    for copy in sends:
        copy.wait_send()


def gather_layer(pieces, down, count):
    n = len(pieces)
    slots = 8 + 2 * (count - 1) + count
    outs = [
        jax.ShapeDtypeStruct((count, 2, 2, 2, 2) + p.shape[1:], BF16) for p in pieces
    ] + [jax.ShapeDtypeStruct((count, 2, 2) + down.shape, BF16)]
    any_space = pl.BlockSpec(memory_space=pl.ANY)
    full = pl.pallas_call(
        functools.partial(gather_kernel, count, n),
        out_shape=outs,
        in_specs=[any_space] * (n + 1),
        out_specs=[any_space] * (n + 1),
        scratch_shapes=[
            pltpu.SemaphoreType.DMA((n + 1, slots)),
            pltpu.SemaphoreType.DMA((n + 1, slots)),
            pltpu.SemaphoreType.DMA((n + 1,)),
        ],
        compiler_params=pltpu.CompilerParams(
            collective_id=1, has_side_effects=True, vmem_limit_bytes=VMEM_BYTES
        ),
        name="gather_layer",
    )(*pieces, down)
    return [f.reshape(-1, f.shape[-1]) for f in full]


def reduce_kernel(count, n_cols, *refs):
    n = n_cols + 1
    parts, outs = refs[:n], refs[n : 2 * n]
    rest = list(refs[2 * n :])
    held = [rest.pop(0) for _ in range(n)]
    from_core = [rest.pop(0) for _ in range(n)]
    from_a = [rest.pop(0) for _ in range(n)]
    from_zh = [rest.pop(0) for _ in range(n)]
    from_rank = [rest.pop(0) for _ in range(n_cols)]
    send, recv, local = rest
    place = Place()
    peers = place.rank_peers()
    others = [place.a_peer(k, count) for k in range(1, count)]
    a, core, zh = place.a, place.core, place.zh
    sends = []

    def go(src, dst, i, slot, device):
        copy = remote(src, dst, send.at[i, slot], recv.at[i, slot], device)
        copy.start()
        sends.append(copy)
        return copy

    def half(i, c):
        if i == n_cols:
            return parts[i].at[:, c]
        return parts[i].at[:, :, c]

    order = [n_cols] + list(range(n_cols))
    loads = {}
    for i in order:
        loads[i] = pltpu.make_async_copy(half(i, core), held[i], local.at[i])
        loads[i].start()
    greet([d for d, _ in peers] + [place.zh_peer(), place.core_peer()] + [o[0] for o in others])
    by_core, by_a, by_zh, by_rank = {}, {}, {}, {}
    for i in order:
        by_core[i] = go(half(i, 1 - core), from_core[i], i, 0, place.core_peer())

    for i in order:
        loads[i].wait()
        by_core[i].wait_recv()
        h, s = held[i], from_core[i]
        for aa in range(count):
            add_into(h.at[aa], s.at[aa])
        by_a[i] = []
        for k in range(count - 1):
            device, ahead, _ = others[k]
            by_a[i].append(go(h.at[ahead], from_a[i].at[k], i, 1 + k, device))
    for i in order:
        h = held[i].at[a]
        for k in range(count - 1):
            by_a[i][k].wait_recv()
            add_into(h, from_a[i].at[k])
        if i == n_cols:
            by_zh[i] = go(h.at[1 - zh], from_zh[i], i, count, place.zh_peer())
        else:
            by_zh[i] = go(h.at[:, 1 - zh], from_zh[i], i, count, place.zh_peer())
    stores = []
    for i in order:
        by_zh[i].wait_recv()
        if i == n_cols:
            outs[i][...] = held[i][a, zh].astype(F32) + from_zh[i][...].astype(F32)
            continue
        for xx in range(2):
            for ll in range(2):
                h = held[i]
                h[a, xx, zh, ll] = (
                    h[a, xx, zh, ll].astype(F32) + from_zh[i][xx, ll].astype(F32)
                ).astype(BF16)
        by_rank[i] = []
        for j, (device, rank) in enumerate(peers):
            xx, ll = lax.div(rank, 2), lax.rem(rank, 2)
            by_rank[i].append(
                go(held[i].at[a, xx, zh, ll], from_rank[i].at[j], i, count + 1 + j, device)
            )
    for i in range(n_cols):
        outs[i][place.rank] = held[i][a, place.x, zh, place.zl].astype(F32)
        for j, (_, rank) in enumerate(peers):
            by_rank[i][j].wait_recv()
            outs[i][rank] = from_rank[i][j].astype(F32)
    for copy in sends:
        copy.wait_send()


def add_into(target, source):
    lead = target.shape[:-2]
    total = 1
    for size in lead:
        total *= size

    @pl.loop(0, total)
    def _(j):
        index, left = [], j
        for size in reversed(lead):
            index.append(lax.rem(left, size))
            left = lax.div(left, size)
        index = tuple(reversed(index))
        target[index] = (target[index].astype(F32) + source[index].astype(F32)).astype(BF16)


def reduce_layer(parts, down, count):
    n_cols = len(parts)
    shaped = [p.reshape(count, 2, 2, 2, 2, -1, p.shape[-1]) for p in parts]
    shaped.append(down.reshape(count, 2, 2, -1, down.shape[-1]))
    n = n_cols + 1
    tails = [s.shape[-2:] for s in shaped]
    held = [(count, 2, 2, 2) + t for t in tails[:-1]] + [(count, 2) + tails[-1]]
    from_a = [(max(count - 1, 1), 2, 2, 2) + t for t in tails[:-1]] + [(max(count - 1, 1), 2) + tails[-1]]
    from_zh = [(2, 2) + t for t in tails[:-1]] + [tails[-1]]
    from_rank = [(3,) + t for t in tails[:-1]]
    vmem = pl.BlockSpec(memory_space=pltpu.VMEM)
    scratch = [pltpu.VMEM(s, BF16) for s in held + held + from_a + from_zh + from_rank]
    slots = count + 4
    return pl.pallas_call(
        functools.partial(reduce_kernel, count, n_cols),
        out_shape=[jax.ShapeDtypeStruct((RANKS,) + t, F32) for t in tails[:-1]]
        + [jax.ShapeDtypeStruct(tails[-1], F32)],
        in_specs=[pl.BlockSpec(memory_space=pl.ANY)] * n,
        out_specs=[vmem] * n,
        scratch_shapes=scratch
        + [
            pltpu.SemaphoreType.DMA((n, slots)),
            pltpu.SemaphoreType.DMA((n, slots)),
            pltpu.SemaphoreType.DMA((n,)),
        ],
        compiler_params=pltpu.CompilerParams(
            collective_id=2, has_side_effects=True, vmem_limit_bytes=VMEM_BYTES
        ),
        name="reduce_layer",
    )(*shaped)


def pack_weights(w_qkv, w_out, w_gate_up, gains, count, layer):
    rows = w_qkv.shape[1]
    attn_cols = HEADS * HEAD_DIM
    kv_cols = KV_HEADS * HEAD_DIM
    qkv = w_qkv[layer]
    q = qkv[:, :attn_cols].reshape(rows, RANKS, -1)
    k = qkv[:, attn_cols : attn_cols + kv_cols].reshape(rows, RANKS, -1)
    v = qkv[:, attn_cols + kv_cols :].reshape(rows, RANKS, -1)
    scales = jnp.pad(gains[layer].T, ((0, 0), (0, GAIN_COLS - 2)))
    scales = jnp.broadcast_to(scales[:, None], (rows, RANKS, GAIN_COLS))
    head = jnp.concatenate([q, k, v, scales], axis=2).transpose(1, 0, 2)
    out = w_out[layer].T.reshape(rows, RANKS, -1).transpose(1, 0, 2)
    gu = w_gate_up[layer].reshape(rows, 2, count, 2, 2, 2, 2, -1)
    gu = gu.transpose(3, 6, 0, 1, 2, 4, 5, 7).reshape(RANKS, rows, -1)
    return head, out, gu


def unpack_grads(head, out, gu, count):
    rows = head.shape[1]
    q_cols = HEADS * HEAD_DIM // RANKS
    kv_cols = KV_HEADS * HEAD_DIM // RANKS
    wide = lambda part: part.transpose(1, 0, 2).reshape(rows, -1)
    qkv = jnp.concatenate(
        [
            wide(head[:, :, :q_cols]),
            wide(head[:, :, q_cols : q_cols + kv_cols]),
            wide(head[:, :, q_cols + kv_cols : q_cols + 2 * kv_cols]),
        ],
        axis=1,
    )
    gains = jnp.sum(head[:, :, q_cols + 2 * kv_cols :][:, :, :2], axis=0).T
    w_out = wide(out).T
    w_gu = gu.reshape(2, 2, rows, 2, count, 2, 2, -1).transpose(2, 3, 4, 0, 5, 6, 1, 7)
    return qkv, w_out, w_gu.reshape(rows, 2, -1), gains


def rotary_tables(positions, head_size):
    half_size = head_size // 2
    freq_index = jnp.arange(half_size).astype(F32)
    inverse = jnp.exp(freq_index * (-2.0 * jnp.log(ROPE_BASE) / head_size))
    angles = positions.astype(F32)[:, None] * inverse[None, :]
    return (jnp.cos(angles), jnp.sin(angles))


def rotate(values, cosine, sine_tab):
    half_size = values.shape[-1] // 2
    first, second = values[..., :half_size], values[..., half_size:]
    c, s = cosine[:, None, :], sine_tab[:, None, :]
    return jnp.concatenate([first * c - second * s, second * c + first * s], axis=-1)


def unrotate(grads, cosine, sine_tab):
    return rotate(grads, cosine, -sine_tab)


def attend(proj, cosine, sine_tab, causal):
    length = proj.shape[0]
    kv = KV_HEADS // RANKS
    groups = HEADS // KV_HEADS
    q_cols = kv * groups * HEAD_DIM
    kv_cols = kv * HEAD_DIM
    query = rotate(proj[:, :q_cols].reshape(length, kv * groups, HEAD_DIM), cosine, sine_tab)
    query = query.astype(BF16).reshape(length, kv, groups, HEAD_DIM)
    key = rotate(proj[:, q_cols : q_cols + kv_cols].reshape(length, kv, HEAD_DIM), cosine, sine_tab)
    key = key.astype(BF16)
    value = proj[:, q_cols + kv_cols :].astype(BF16).reshape(length, kv, HEAD_DIM)
    scale = HEAD_DIM ** (-0.5)
    scores = jnp.einsum("qkgd,skd->kgqs", query, key, preferred_element_type=F32) * scale
    scores = jnp.where(causal[None, None], scores, MASKED)
    highest = jnp.max(scores, axis=-1, keepdims=True)
    lse = highest + jnp.log(jnp.sum(jnp.exp(scores - highest), axis=-1, keepdims=True))
    weights = jnp.exp(scores - lse).astype(BF16)
    mixed = jnp.einsum("kgqs,skd->qkgd", weights, value, preferred_element_type=F32).astype(BF16)
    return mixed.reshape(length, q_cols), (query, key, value, lse)


def attend_back(saved, mixed, grad_mixed, cosine, sine_tab, causal):
    query, key, value, lse = saved
    length = query.shape[0]
    grad_mixed = grad_mixed.reshape(query.shape)
    mixed = mixed.reshape(query.shape)
    scale = HEAD_DIM ** (-0.5)
    scores = jnp.einsum("qkgd,skd->kgqs", query, key, preferred_element_type=F32) * scale
    scores = jnp.where(causal[None, None], scores, MASKED)
    weights = jnp.exp(scores - lse)
    grad_weights = jnp.einsum("qkgd,skd->kgqs", grad_mixed, value, preferred_element_type=F32)
    delta = jnp.sum(grad_mixed.astype(F32) * mixed.astype(F32), axis=-1)
    delta = jnp.transpose(delta, (1, 2, 0))[..., None]
    grad_scores = (weights * (grad_weights - delta) * scale).astype(BF16)
    grad_query = jnp.einsum("kgqs,skd->qkgd", grad_scores, key, preferred_element_type=F32)
    grad_key = jnp.einsum("kgqs,qkgd->skd", grad_scores, query, preferred_element_type=F32)
    grad_value = jnp.einsum(
        "kgqs,qkgd->skd", weights.astype(BF16), grad_mixed, preferred_element_type=F32
    )
    grad_query = unrotate(grad_query.reshape(length, -1, HEAD_DIM), cosine, sine_tab)
    grad_key = unrotate(grad_key, cosine, sine_tab)
    return jnp.concatenate(
        [g.reshape(length, -1) for g in (grad_query, grad_key, grad_value)], axis=1
    ).astype(BF16)


VM = pl.BlockSpec(memory_space=pltpu.VMEM)
AN = pl.BlockSpec(memory_space=pl.ANY)


def params(collective_id):
    return pltpu.CompilerParams(
        collective_id=collective_id, has_side_effects=True, vmem_limit_bytes=VMEM_BYTES
    )


def sems(n):
    return [
        pltpu.SemaphoreType.DMA((n,)),
        pltpu.SemaphoreType.DMA((n,)),
        pltpu.SemaphoreType.DMA((4,)),
    ]


def call_head(h, gain, wq):
    rows, width = h.shape
    cols = wq.shape[1] - GAIN_COLS
    return pl.pallas_call(
        functools.partial(head_kernel, rows),
        out_shape=[
            jax.ShapeDtypeStruct((RANKS * rows, cols), F32),
            jax.ShapeDtypeStruct((RANKS, rows, width), BF16),
        ],
        in_specs=[VM, VM, AN],
        out_specs=[VM, AN],
        scratch_shapes=[pltpu.VMEM((width, cols), BF16), pltpu.VMEM((RANKS, rows, width), BF16)] + sems(3),
        compiler_params=params(3),
        name="head",
    )(h, gain, wq)


def call_body(o, h, gain, wo, wgu, wd, gain_next=None, wq=None):
    rows, width = h.shape
    tall = RANKS * rows
    hidden = wd.shape[0]
    more = wq is not None
    cols = wq.shape[1] - GAIN_COLS if more else 0
    three = pltpu.VMEM((3, rows, width), BF16)
    four = pltpu.VMEM((RANKS, rows, width), BF16)
    return pl.pallas_call(
        functools.partial(body_kernel, rows, more),
        out_shape=[
            jax.ShapeDtypeStruct((rows, width), F32),
            jax.ShapeDtypeStruct((rows, width), F32),
            jax.ShapeDtypeStruct((tall, hidden), F32),
            jax.ShapeDtypeStruct((tall, hidden), F32),
            jax.ShapeDtypeStruct((tall, hidden), BF16),
            jax.ShapeDtypeStruct((RANKS, rows, width), BF16),
        ]
        + (
            [
                jax.ShapeDtypeStruct((tall, cols), F32),
                jax.ShapeDtypeStruct((RANKS, rows, width), BF16),
            ]
            if more
            else []
        ),
        in_specs=[VM, VM, VM, AN, AN, AN] + ([VM, AN] if more else []),
        out_specs=[VM] * 5 + [AN] + ([VM, AN] if more else []),
        scratch_shapes=[
            pltpu.VMEM(wo.shape, BF16),
            pltpu.VMEM(wgu.shape, BF16),
            pltpu.VMEM(wd.shape, BF16),
        ]
        + ([pltpu.VMEM((width, cols), BF16)] if more else [])
        + [three, three, four, three, three]
        + ([four] if more else [])
        + sems(12),
        compiler_params=params(4 if more else 5),
        name="body_more" if more else "body",
    )(o, h, gain, wo, wgu, wd, *((gain_next, wq) if more else ()))


def call_back(start, rest):
    first, last = len(start) == 1, rest is None
    rows, width = start[0].shape if first else start[2].shape
    tall = RANKS * rows
    outs, out_specs, scratch = [], [], []
    three = pltpu.VMEM((3, rows, width), BF16)
    four = pltpu.VMEM((RANKS, rows, width), BF16)
    in_specs = [VM] if first else [VM, AN, VM, VM, VM]
    if not first:
        outs += [jax.ShapeDtypeStruct((rows, width), F32), jax.ShapeDtypeStruct((1, width), F32)]
        out_specs += [VM, VM]
        scratch += [pltpu.VMEM((width, start[0].shape[1]), BF16), three, three]
    if not last:
        wd, wgu, wo = rest[:3]
        in_specs += [AN, AN, AN, VM, VM, VM, VM]
        outs += [
            jax.ShapeDtypeStruct((RANKS, rows, width), BF16),
            jax.ShapeDtypeStruct((tall, wgu.shape[1]), BF16),
            jax.ShapeDtypeStruct((rows, width), F32),
            jax.ShapeDtypeStruct((1, width), F32),
            jax.ShapeDtypeStruct((RANKS, rows, width), BF16),
            jax.ShapeDtypeStruct((tall, wo.shape[1]), BF16),
        ]
        out_specs += [AN, VM, VM, VM, AN, VM]
        scratch += [pltpu.VMEM(w.shape, BF16) for w in (wd, wgu, wo)] + [four, three, three, four]
    return pl.pallas_call(
        functools.partial(back_kernel, rows, first, last),
        out_shape=outs,
        in_specs=in_specs,
        out_specs=out_specs,
        scratch_shapes=scratch + sems(12),
        compiler_params=params(6 if first else (7 if not last else 8)),
        name="back_first" if first else ("back_last" if last else "back_mid"),
    )(*start, *(rest or ()))


def dot_t(a, b):
    return lax.dot_general(a, b, (((0,), (0,)), ((), ())), preferred_element_type=F32).astype(BF16)


def swap_pairs(dp_size, ctx_size):
    pairs = []
    for dp in range(dp_size):
        for ctx in range(ctx_size):
            a, x, core = dp // 4, dp // 2 % 2, dp % 2
            zh, zl = ctx // 2, ctx % 2
            pairs.append((dp * ctx_size + ctx, (a * 4 + zh * 2 + core) * ctx_size + x * 2 + zl))
    return pairs


def shards(dp_size, ctx_size, tokens, cotangent, w_qkv, w_out, w_gate_up, w_down, gains):
    count = dp_size // 4
    pairs = swap_pairs(dp_size, ctx_size)
    swap = lambda value: lax.ppermute(value, ("dp", "ctx"), pairs)
    rows, width = tokens.shape
    length = RANKS * rows
    positions = jnp.arange(length, dtype=jnp.int32)
    cosine, sine_tab = rotary_tables(positions, HEAD_DIM)
    causal = positions[None, :] <= positions[:, None]

    full, gain_rows = [], []
    for layer in range(LAYERS):
        head, out, gu = pack_weights(w_qkv, w_out, w_gate_up, gains, count, layer)
        wq, wo, wgu, wd = gather_layer([head, out, gu], w_down[layer], count)
        full.append((wq, wo, wgu, wd))
        gain_rows.append(wq[:, -GAIN_COLS:][:, :2].astype(F32).T)
    h = swap(tokens).astype(F32)
    g = swap(cotangent.astype(BF16)).astype(F32)

    gain = lambda layer, which: gain_rows[layer][which : which + 1]
    records = []
    proj, n1 = call_head(h, gain(0, 0), full[0][0])
    for layer in range(LAYERS):
        mixed, saved = attend(proj, cosine, sine_tab, causal)
        wq, wo, wgu, wd = full[layer]
        more = (gain(layer + 1, 0), full[layer + 1][0]) if layer + 1 < LAYERS else ()
        h1, h_next, gate, up, u, n2, *ahead = call_body(mixed, h, gain(layer, 1), wo, wgu, wd, *more)
        records.append((h, n1, saved, mixed, h1, n2, gate, up, u))
        h = h_next
        if more:
            proj, n1 = ahead

    start = (g,)
    grads = [None] * LAYERS
    late = None
    tall = lambda value: value.reshape(length, width)
    for layer in reversed(range(LAYERS)):
        h_in, n1, saved, mixed, h1, n2, gate, up, u = records[layer]
        wq, wo, wgu, wd = full[layer]
        got = call_back(start, (wd, wgu, wo, gate, up, h1, gain(layer, 1)))
        if layer + 1 < LAYERS:
            _, gg_in, *got = got
            late(gg_in)
        gbg, dgu, gh, gg2, ghg, do = got
        g_down = dot_t(u, tall(gbg))
        g_gu = dot_t(tall(n2), dgu)
        g_out = dot_t(tall(ghg), mixed)
        dqkv = attend_back(saved, mixed, do, cosine, sine_tab, causal)
        g_qkv = dot_t(tall(n1), dqkv)

        def late(gg1, layer=layer, g_qkv=g_qkv, g_out=g_out, g_gu=g_gu, g_down=g_down, gg2=gg2):
            scales = jnp.concatenate([gg1, gg2], axis=0).astype(BF16).T
            scales = jnp.pad(scales, ((0, 0), (0, GAIN_COLS - 2)))
            head = jnp.concatenate([g_qkv, scales], axis=1)
            r_head, r_out, r_gu, r_down = reduce_layer([head, g_out, g_gu], g_down, count)
            grads[layer] = unpack_grads(r_head, r_out, r_gu, count) + (r_down,)

        start = (dqkv, wq, gh, h_in, gain(layer, 0))
    g, gg_in = call_back(start, None)
    late(gg_in)
    stacked = [jnp.stack([grads[layer][which] for layer in range(LAYERS)]) for which in range(5)]
    s_qkv, s_out, s_gu, s_gains, s_down = stacked
    return (swap(h), swap(g), s_qkv, s_out, s_gu, s_down, s_gains)


def solution(mesh):
    both = ("dp", "ctx")
    return jax.shard_map(
        functools.partial(shards, mesh.shape["dp"], mesh.shape["ctx"]),
        mesh=mesh,
        in_specs=(
            P(both, None),
            P(both, None),
            P(None, both, None),
            P(None, None, both),
            P(None, both, None, None),
            P(None, both, None),
            P(None, None, both),
        ),
        out_specs=(
            P(both, None),
            P(both, None),
            P(None, both, None),
            P(None, None, both),
            P(None, both, None, None),
            P(None, both, None),
            P(None, None, both),
        ),
        check_vma=False,
    )
```

time: 2730 us -> 1030 us (0.38)
  the two profiles are of different devices: /device:TPU:0 before, /device:TPU:2 now
where the time goes in v1:
time: 1030 us
  Pallas kernels  823 us (80%)
  local copies, waits for them, and re-layouts  67.1 us (7%)
  matrix products  50 us (5%)
  waiting for transfers between devices  38.7 us (4%)
  other arithmetic  30.9 us (3%)
  starting transfers between devices  15.3 us (1%)
    pallas_call x2, Pallas kernels, reduce_layer(): pl.pallas_call(functools.partial(reduce_kernel, count, n_cols), out_shape...  256 us
    pallas_call x2, Pallas kernels, gather_layer(): pl.pallas_call(functools.partial(gather_kernel, count, n), out_shape=outs...  225 us
    pallas_call x3, Pallas kernels, call_back(): pl.pallas_call(functools.partial(back_kernel, rows, first, last), out_sha...  172 us
    pallas_call x2, Pallas kernels, call_body(): pl.pallas_call(functools.partial(body_kernel, rows, more), out_shape=[jax...  144 us
    ppermute x4, waiting for transfers between devices, shards(): swap = lambda value: lax.ppermute(value, ('dp', 'ctx'), pairs)  38.7 us
    dot_general x8, matrix products, dot_t(): lax.dot_general(a, b, (((0,), (0,)), ((), ())), preferred_element_type=F32)  29.7 us
    pallas_call x1, Pallas kernels, call_head(): pl.pallas_call(functools.partial(head_kernel, rows), out_shape=[jax.Shape...  25.2 us
  transfers between devices with their start and end apart: 4, of which 2 were waited for; matrix products, arithmetic and copies ran while one was open for 7% of the time, Pallas kernels for 38%

profile of v1, /device:TPU:2, one launch (start us, length us, event | category | flops | bytes accessed | tf_op | source)
XLA Modules:
  0.0 1027.1 jit_solution(4782292790468585079)
XLA Ops:
  0.6 1.9 convert_element_type.238
  2.6 4.5 collective-permute-start.2
  7.0 3.2 collective-permute-start
  23.7 1.5 fusion.31
  26.2 1.5 reshape.347.refs_2_
  28.7 1.5 reshape.334.refs_2_
  31.1 113.9 %gather_layer.2 = (bf16[2,2,2,2,2,48,896]{6,5,4,3,2,1,0:T(8,128)(2,1)}, bf16[2,2,2,2,2,48,384]{6,5,4,3,2,1,0:T(8,128)(2,1)}, bf16[2,2,2,2,2,48,2048]{6,5,4,3,2,1,0:T(8,128)(2,1)}, bf16[2,2,2,128,1536]{4,3,2,1,0:T(8,128)(2,1)}) custom-call(bf16[4,48,896]{2,1,0:T(8,128)(2,1)} %maximum_bitcast_fusion.2.refs_0_, bf16[4,48,384]{2,1,0:T(8,128)(2,1)} %bitcast.341, ...), custom_call_target="tpu_custom_call" | custom-call | tf_op jit(solution)/shard_map/gather_layer/pallas_call | solution.py:486
  147.9 111.5 %gather_layer.3 = (bf16[2,2,2,2,2,48,896]{6,5,4,3,2,1,0:T(8,128)(2,1)}, bf16[2,2,2,2,2,48,384]{6,5,4,3,2,1,0:T(8,128)(2,1)}, bf16[2,2,2,2,2,48,2048]{6,5,4,3,2,1,0:T(8,128)(2,1)}, bf16[2,2,2,128,1536]{4,3,2,1,0:T(8,128)(2,1)}) custom-call(bf16[4,48,896]{2,1,0:T(8,128)(2,1)} %maximum_bitcast_fusion.3.refs_0_, bf16[4,48,384]{2,1,0:T(8,128)(2,1)} %bitcast.340, ...), custom_call_target="tpu_custom_call" | custom-call | tf_op jit(solution)/shard_map/gather_layer/pallas_call | solution.py:486
  261.8 2.0 convert_element_type.229.h_ref.refs_1_.refs_3_
  263.8 25.2 %head.1 = (f32[512,768]{1,0:T(8,128)}, bf16[4,128,1536]{2,1,0:T(8,128)(2,1)}) custom-call(f32[128,1536]{1,0:T(8,128)} %convert_element_type.229.h_ref.refs_1_.refs_3_, f32[1,1536]{1,0:T(1,128)} %get-tuple-element.136.gain_ref.refs_4_, bf16[1536,896]{1,0:T(8,128)(2,1)} %bitcast.281), custom_call_target="tpu_custom_call" | custom-call | tf_op jit(solution)/shard_map/head/pallas_call | solution.py:757
  297.4 82.7 %body_more.1 = (f32[128,1536]{1,0:T(8,128)}, f32[128,1536]{1,0:T(8,128)}, f32[512,1024]{1,0:T(8,128)}, f32[512,1024]{1,0:T(8,128)}, bf16[512,1024]{1,0:T(8,128)(...) custom-call(bf16[512,384]{1,0:T(8,128)(2,1)} %copy.135.refs_0_, ...), custom_call_target="tpu_custom_call" | custom-call | tf_op jit(solution)/shard_map/body_more/pallas_call | solution.py:779
  384.1 1.8 fusion.13
  386.0 2.0 copy-done.3
  390.2 3.4 convolution_convert_fusion.8
  394.6 60.9 %body.1 = (f32[128,1536]{1,0:T(8,128)}, f32[128,1536]{1,0:T(8,128)}, f32[512,1024]{1,0:T(8,128)}, f32[512,1024]{1,0:T(8,128)}, bf16[512,1024]{1,0:T(8,128)(2,1)}, /*index=5*/bf16[4,128,1536]{2,1,0:T(8,128)(2,1)}) custom-call(bf16[512,384]{1,0:T(8,128)(2,1)} %copy.140.refs_0_, f32[128,1536]{1,0:T(8,128)} %get-tuple-element.61.refs_1_.refs_3_, ...), custom_call_target="tpu_custom_call" | custom-call | tf_op jit(solution)/shard_map/body/pallas_call | solution.py:779
  455.5 2.0 convert_element_type.239.refs_0_
  457.5 59.8 %back_first.1 = (bf16[4,128,1536]{2,1,0:T(8,128)(2,1)}, bf16[512,2048]{1,0:T(8,128)(2,1)}, f32[128,1536]{1,0:T(8,128)}, f32[1,1536]{1,0:T(1,128)}, bf16[4,128,15...) custom-call(f32[128,1536]{1,0:T(8,128)} %convert_element_type.239.refs_0_, bf16[1024,1536]{1,0:T(8,128)(2,1)} %bitcast.287, ...), custom_call_target="tpu_custom_call" | custom-call | tf_op jit(solution)/shard_map/back_first/pallas_call | solution.py:838
  518.6 3.6 fusion.14
  522.2 1.6 fusion.7
  527.0 88.2 %back_mid.1 = (f32[128,1536]{1,0:T(8,128)}, f32[1,1536]{1,0:T(1,128)}, bf16[4,128,1536]{2,1,0:T(8,128)(2,1)}, bf16[512,2048]{1,0:T(8,128)(2,1)}, f32[128,1536]{1...) custom-call(bf16[512,768]{1,0:T(8,128)(2,1)} %pad_maximum_fusion.3.refs_0_, ...), custom_call_target="tpu_custom_call" | custom-call | tf_op jit(solution)/shard_map/back_mid/pallas_call | solution.py:838
  616.6 3.6 fusion.15
  620.2 1.6 fusion.4
  624.9 24.4 %back_last.1 = (f32[128,1536]{1,0:T(8,128)}, f32[1,1536]{1,0:T(1,128)}) custom-call(bf16[512,768]{1,0:T(8,128)(2,1)} %pad_maximum_fusion.4.refs_0_, bf16[1536,896]{1,0:T(8,128)(2,1)} %bitcast.282, f32[128,1536]{1,0:T(8,128)} %get-tuple-element.75.refs_2_, f32[128,1536]{1,0:T(8,128)} %convert_element_type.229.h_ref.refs_1_.refs_3_, ...), custom_call_target="tpu_custom_call" | custom-call | tf_op jit(solution)/shard_map/back_last/pallas_call | solution.py:838
  649.3 2.8 convolution_convert_fusion.5
  652.4 3.0 copy.155
  655.4 3.6 convolution_convert_fusion.7
  659.1 3.5 convolution_convert_fusion.3
  662.6 5.4 convolution_convert_fusion.1
  668.0 129.0 %reduce_layer.2 = (f32[4,48,896]{2,1,0:T(8,128)}, f32[4,48,384]{2,1,0:T(8,128)}, f32[4,48,2048]{2,1,0:T(8,128)}, f32[128,1536]{1,0:T(8,128)}) custom-call(bf16[2,2,2,2,2,48,896]{6,5,4,3,2,1,0:T(8,128)(2,1)} %bitcast.291, bf16[2,2,2,2,2,48,384]{6,5,4,3,2,1,0:T(8,128)(2,1)} %bitcast.323, bf16[2,2,2,2,2,48,2048]{6,5,4,3,2,1,0:T(8,128)(2,1)} %bitcast.292, ...), custom_call_target="tpu_custom_call" | custom-call | tf_op jit(solution)/shard_map/reduce_layer/pallas_call | solution.py:616
  797.9 1.7 slice_bitcast_fusion.3
  799.6 1.8 slice_bitcast_fusion.9
  803.1 2.8 copy.159
  806.0 3.6 convolution_convert_fusion.6
  809.6 3.5 convolution_convert_fusion.2
  813.1 5.8 convolution_convert_fusion
  818.9 127.4 %reduce_layer.3 = (f32[4,48,896]{2,1,0:T(8,128)}, f32[4,48,384]{2,1,0:T(8,128)}, f32[4,48,2048]{2,1,0:T(8,128)}, f32[128,1536]{1,0:T(8,128)}) custom-call(bf16[2,2,2,2,2,48,896]{6,5,4,3,2,1,0:T(8,128)(2,1)} %bitcast.290, bf16[2,2,2,2,2,48,384]{6,5,4,3,2,1,0:T(8,128)(2,1)} %bitcast.322, bf16[2,2,2,2,2,48,2048]{6,5,4,3,2,1,0:T(8,128)(2,1)} %bitcast.293, ...), custom_call_target="tpu_custom_call" | custom-call | tf_op jit(solution)/shard_map/reduce_layer/pallas_call | solution.py:616
  949.4 4.2 collective-permute-start.3
  953.6 3.5 collective-permute-start.1
  959.6 2.6 pad_maximum_fusion.1
  966.2 2.9 stack_reshape.6
  969.8 2.8 reshape.391
  973.9 3.0 stack_reshape.7
  976.8 1.9 pad_maximum_fusion.5
  978.7 5.4 pad_maximum_fusion
  984.1 22.8 %collective-permute-done.3 = f32[128,1536]{1,0:T(8,128)} collective-permute-done((f32[128,1536]{1,0:T(8,128)}, f32[128,1536]{1,0:T(8,128)}, u32[]{:S(2)}, u32[]{:S(2)}) %collective-permute-start.3) | collective-permute-done | bytes 786464 | tf_op jit(solution)/shard_map/ppermute | solution.py:866
  1007.0 15.8 %collective-permute-done.1 = f32[128,1536]{1,0:T(8,128)} collective-permute-done((f32[128,1536]{1,0:T(8,128)}, f32[128,1536]{1,0:T(8,128)}, u32[]{:S(2)}, u32[]{:S(2)}) %collective-permute-start.1) | collective-permute-done | bytes 786464 | tf_op jit(solution)/shard_map/ppermute | solution.py:866
  1022.8 2.1 copy.213
  1024.9 2.1 copy.214
  (214 shorter events, 59.9 us)
Async XLA Ops:
  0.6 12.7 %copy-start.34 = (bf16[2,2,48]{2,1,0:T(2,128)(2,1)S(1)}, bf16[2,2,48]{2,1,0:T(2,128)(2,1)}, u32[]{:S(2)}) copy-start(bf16[2,2,48]{2,1,0:T(2,128)(2,1)} %param.13) | copy-start | bytes 1156
  2.6 452.9 %collective-permute-start.2 = (bf16[128,1536]{1,0:T(8,128)(2,1)}, bf16[128,1536]{1,0:T(8,128)(2,1)}, u32[]{:S(2)}, u32[]{:S(2)}) collective-permute-start(bf16[128,1536]{1,0:T(8,128)(2,1)} %convert_element_type.238), channel_id=1, source_target_pairs={{0,0},{1,1},{2,8},{3,9},{4,4},{5,5},{6,12},{7,13},{8,2},{9,3},{10,... | collective-permute-start | bytes 1179656 | tf_op jit(solution)/shard_map/ppermute | solution.py:866
  7.0 254.8 %collective-permute-start = (bf16[128,1536]{1,0:T(8,128)(2,1)}, bf16[128,1536]{1,0:T(8,128)(2,1)}, u32[]{:S(2)}, u32[]{:S(2)}) collective-permute-start(bf16[128,1536]{1,0:T(8,128)(2,1)} %param.7), channel_id=1, source_target_pairs={{0,0},{1,1},{2,8},{3,9},{4,4},{5,5},{6,12},{7,13},{8,2},{9,3},{10,... | collective-permute-start | bytes 1179656 | tf_op jit(solution)/shard_map/ppermute | solution.py:866
  11.5 11.3 %copy-start.12 = (bf16[2,128,1536]{2,1,0:T(8,128)(2,1)S(1)}, bf16[2,128,1536]{2,1,0:T(8,128)(2,1)}, u32[]{:S(2)}) copy-start(bf16[2,128,1536]{2,1,0:T(8,128)(2,1)} %param.12) | copy-start | bytes 2359300
  13.3 10.4 %copy-start.7 = (bf16[2,48,2,4096]{3,2,1,0:T(2,128)(2,1)S(1)}, bf16[2,48,2,4096]{3,2,1,0:T(2,128)(2,1)}, u32[]{:S(2)}) copy-start(bf16[2,48,2,4096]{3,2,1,0:T(2,128)(2,1)} %param.11) | copy-start | bytes 4718596
  27.7 2.5 copy-start.28
  27.7 2.5 copy-start.16
  27.7 2.5 copy-start.21
  27.7 2.6 copy-start.22
  28.7 118.3 %copy-start.27 = (bf16[48,128]{1,0:T(8,128)(2,1)S(1)}, bf16[48,128]{1,0:T(8,128)(2,1)}, u32[]{:S(2)}) copy-start(bf16[48,128]{1,0:T(8,128)(2,1)} %pad.15.clone) | copy-start | bytes 36868
  28.7 118.3 %copy-start.19 = (bf16[48,4,192]{2,0,1:T(8,128)(2,1)S(1)}, bf16[48,4,192]{2,0,1:T(8,128)(2,1)}, u32[]{:S(2)}) copy-start(bf16[48,4,192]{2,0,1:T(8,128)(2,1)} %copy.130) | copy-start | bytes 221188
  28.7 118.3 %copy-start.20 = (bf16[48,4,192]{2,0,1:T(8,128)(2,1)S(1)}, bf16[48,4,192]{2,0,1:T(8,128)(2,1)}, u32[]{:S(2)}) copy-start(bf16[48,4,192]{2,0,1:T(8,128)(2,1)} %copy.131) | copy-start | bytes 221188
  146.1 114.6 %copy-start.29 = (f32[512]{0:T(512)S(1)}, f32[512]{0:T(512)}, u32[]{:S(2)}) copy-start(f32[512]{0:T(512)} %iota_convert_fusion) | copy-start | bytes 6148
  146.1 114.6 %copy-start.35 = (f32[48]{0:T(128)S(1)}, f32[48]{0:T(128)}, u32[]{:S(2)}) copy-start(f32[48]{0:T(128)} %multiply_exponential_fusion) | copy-start | bytes 580
  292.5 2.6 copy-start.25
  294.2 2.3 copy-start.1
  383.6 2.3 copy-start.14
  386.0 2.0 copy-start.3
  393.6 124.8 %copy-start.9 = (bf16[2,96,2,512]{3,1,2,0:T(8,128)(2,1)}, bf16[2,96,2,512]{3,1,2,0:T(8,128)(2,1)S(1)}, u32[]{:S(2)}) copy-start(bf16[2,96,2,512]{3,1,2,0:T(8,128)(2,1)S(1)} %convolution_convert_fusion.8) | copy-start | bytes 1179652
  518.6 3.6 copy-start.4
  522.2 1.7 copy-start.15
  523.9 0.9 copy-start.18
  616.6 3.6 copy-start.2
  616.6 3.6 copy-start.26
  621.8 1.3 copy-start.32
  624.9 24.4 %copy-start.5 = (bf16[512,768]{1,0:T(8,128)(2,1)S(1)}, bf16[512,768]{1,0:T(8,128)(2,1)}, u32[]{:S(2)}) copy-start(bf16[512,768]{1,0:T(8,128)(2,1)} %pad_maximum_fusion.4.refs_0_) | copy-start | bytes 2359300
  649.3 2.9 copy-start.33
  655.4 3.6 copy-start.42
  655.4 3.6 copy-start.43
  659.0 3.5 copy-start.37
  659.0 3.5 copy-start.40
  668.0 133.4 %copy-start.30 = (f32[1,1536]{1,0:T(1,128)S(1)}, f32[1,1536]{1,0:T(1,128)}, u32[]{:S(2)}) copy-start(f32[1,1536]{1,0:T(1,128)} %get-tuple-element.88) | copy-start | bytes 18436
  668.0 133.4 %copy-start.6 = (bf16[512,768]{1,0:T(8,128)(2,1)S(1)}, bf16[512,768]{1,0:T(8,128)(2,1)}, u32[]{:S(2)}) copy-start(bf16[512,768]{1,0:T(8,128)(2,1)} %pad_maximum_fusion.3.refs_0_) | copy-start | bytes 2359300
  668.0 133.4 %copy-start.38 = (bf16[4,128,1536]{2,1,0:T(8,128)(2,1)S(1)}, bf16[4,128,1536]{2,1,0:T(8,128)(2,1)}, u32[]{:S(2)}) copy-start(bf16[4,128,1536]{2,1,0:T(8,128)(2,1)} %get-tuple-element.86) | copy-start | bytes 4718596
  801.4 1.5 copy-start.31
  803.1 2.8 copy-start.10
  805.9 3.6 copy-start.41
  805.9 3.6 copy-start.44
  809.6 3.5 copy-start.36
  809.6 3.5 copy-start.39
  818.9 138.3 %copy-start.13 = (f32[48,4,192]{2,0,1:T(8,128)S(1)}, f32[48,4,192]{2,0,1:T(8,128)}, u32[]{:S(2)}) copy-start(f32[48,4,192]{2,0,1:T(8,128)} %get-tuple-element.113) | copy-start | bytes 442372
  818.9 138.6 %copy-start.11 = (f32[4,6,8,384]{3,2,1,0:T(8,128)S(1)}, f32[4,6,8,384]{3,2,1,0:T(8,128)}, u32[]{:S(2)}) copy-start(f32[4,6,8,384]{3,2,1,0:T(8,128)} %slice_bitcast_fusion.3) | copy-start | bytes 884740
  949.4 57.5 %collective-permute-start.3 = (f32[128,1536]{1,0:T(8,128)}, f32[128,1536]{1,0:T(8,128)}, u32[]{:S(2)}, u32[]{:S(2)}) collective-permute-start(f32[128,1536]{1,0:T(8,128)} %get-tuple-element.76), channel_id=1, source_target_pairs={{0,0},{1,1},{2,8},{3,9},{4,4},{5,5},{6,12},{7,13},{8,2},{9,3},{10,... | collective-permute-start | bytes 2359304 | tf_op jit(solution)/shard_map/ppermute | solution.py:866
  953.6 69.2 %collective-permute-start.1 = (f32[128,1536]{1,0:T(8,128)}, f32[128,1536]{1,0:T(8,128)}, u32[]{:S(2)}, u32[]{:S(2)}) collective-permute-start(f32[128,1536]{1,0:T(8,128)} %get-tuple-element.65), channel_id=1, source_target_pairs={{0,0},{1,1},{2,8},{3,9},{4,4},{5,5},{6,12},{7,13},{8,2},{9,3},{10,... | collective-permute-start | bytes 2359304 | tf_op jit(solution)/shard_map/ppermute | solution.py:866
  958.5 4.3 copy-start.23
  958.5 5.0 copy-start.8
  966.1 3.0 copy-start.24
  973.8 4.9 copy-start
  (1 other events, 0.9 us)

commit v2 on v0

v2 whole, which is shorter than its diff:
```python
import functools

import jax
import jax.numpy as jnp
from jax import lax
from jax.experimental import pallas as pl
from jax.experimental.pallas import tpu as pltpu
from jax.sharding import PartitionSpec as P

HEADS = 16
KV_HEADS = 8
HEAD_DIM = 96
LAYERS = 2
RANKS = 4
GAIN_COLS = 128

NORM_EPS = 1e-05
ROPE_BASE = 100000.0
MASKED = -1e30
MESH = pl.DeviceIdType.MESH
BF16 = jnp.bfloat16
F32 = jnp.float32
VMEM_BYTES = 62 * 1024 * 1024


class Place:
    def __init__(self, count):
        self.count = count
        self.dp = lax.axis_index("dp")
        self.ctx = lax.axis_index("ctx")
        self.core = lax.rem(self.dp, 2)
        self.x = lax.rem(lax.div(self.dp, 2), 2)
        self.a = lax.div(self.dp, 4)
        self.zh = lax.div(self.ctx, 2)
        self.zl = lax.rem(self.ctx, 2)
        self.rank = self.x * 2 + self.zl
        dpx = self.dp + 2 - 4 * self.x
        ctz = self.ctx + 1 - 2 * self.zl
        x2, z2 = 1 - self.x, 1 - self.zl
        self.peers = (
            ((dpx, self.ctx), x2 * 2 + self.zl),
            ((self.dp, ctz), self.x * 2 + z2),
            ((dpx, ctz), x2 * 2 + z2),
        )
        self.core_peer = (self.dp + 1 - 2 * self.core, self.ctx)
        self.zh_peer = (self.dp, self.ctx + 2 - 4 * self.zh)
        self.others = []
        for k in range(1, count):
            ahead = lax.rem(self.a + k, count)
            behind = lax.rem(self.a + count - k, count)
            self.others.append(((self.dp + (ahead - self.a) * 4, self.ctx), ahead, behind))
        self.moves = self.x != self.zh
        self.swap_peer = (self.dp + (self.zh - self.x) * 2, self.ctx + (self.x - self.zh) * 2)

    def greet(self, weights, swap):
        devices = [d for d, _ in self.peers]
        if weights:
            devices += [self.core_peer, self.zh_peer] + [o[0] for o in self.others]
        barrier = pltpu.get_barrier_semaphore()
        for device in devices:
            pl.semaphore_signal(barrier, inc=1, device_id=device, device_id_type=MESH)
        if swap:

            @pl.when(self.moves)
            def _():
                pl.semaphore_signal(barrier, inc=1, device_id=self.swap_peer, device_id_type=MESH)

        expected = len(devices)
        if swap:
            expected = expected + self.x + self.zh - 2 * self.x * self.zh
        pl.semaphore_wait(barrier, expected)


class Net:
    def __init__(self, place, send, recv, local):
        self.place, self.send, self.recv, self.local = place, send, recv, local
        self.n, self.m = 0, 0
        self.sends = []

    def remote(self, src, dst, device):
        copy = self.prepare(src, dst, device)
        copy.start()
        self.sends.append(copy)
        return copy

    def prepare(self, src, dst, device):
        i = self.n
        self.n += 1
        return pltpu.make_async_remote_copy(
            src_ref=src, dst_ref=dst, send_sem=self.send.at[i], recv_sem=self.recv.at[i],
            device_id=device, device_id_type=MESH,
        )

    def here(self, src, dst):
        i = self.m
        self.m += 1
        copy = pltpu.make_async_copy(src, dst, self.local.at[i])
        copy.start()
        return copy

    def finish(self):
        for copy in self.sends:
            copy.wait_send()


REMOTE_SEMS, LOCAL_SEMS = 128, 32


def sems(count=2):
    n = REMOTE_SEMS * max(1, count // 2)
    return [
        pltpu.SemaphoreType.DMA((n,)),
        pltpu.SemaphoreType.DMA((n,)),
        pltpu.SemaphoreType.DMA((LOCAL_SEMS,)),
    ]


class Swap:
    def __init__(self, net, src, dst):
        self.net, self.src, self.dst = net, src, dst

    def start(self):
        net, place = self.net, self.net.place
        self.copy = net.prepare(self.src, self.dst, place.swap_peer)
        self.stay = pltpu.make_async_copy(self.src, self.dst, net.local.at[net.m])
        net.m += 1

        @pl.when(place.moves)
        def _():
            self.copy.start()

        @pl.when(jnp.logical_not(place.moves))
        def _():
            self.stay.start()

    def wait(self):
        @pl.when(self.net.place.moves)
        def _():
            self.copy.wait_recv()
            self.copy.wait_send()

        @pl.when(jnp.logical_not(self.net.place.moves))
        def _():
            self.stay.wait()


class Share:
    def __init__(self, net, piece, block):
        self.net, self.piece, self.block = net, piece, block

    def start(self):
        net, place = self.net, self.net.place
        mine = self.block.at[place.x, place.zl]
        self.copies = [net.remote(self.piece.at[rank], mine, device) for device, rank in place.peers]
        self.own = net.here(self.piece.at[place.rank], mine)

    def wait(self):
        for copy in self.copies:
            copy.wait_recv()
        self.own.wait()


class Gather:
    def __init__(self, net, block, full, ranks=True):
        self.net, self.block, self.full, self.ranks = net, block, full, ranks

    def slot(self, a, core, zh):
        if self.ranks:
            return self.full.at[a, :, core, zh, :]
        return self.full.at[a, core, zh]

    def column(self, a, core):
        if self.ranks:
            return self.full.at[a, :, core, :, :]
        return self.full.at[a, core]

    def begin(self):
        net, p = self.net, self.net.place
        mine = self.slot(p.a, p.core, p.zh)
        self.across = net.remote(self.block, mine, p.zh_peer)
        self.near = [net.remote(self.block, mine, o[0]) for o in p.others]
        self.cores = [net.remote(self.block, mine, p.core_peer)]
        self.own = net.here(self.block, mine)

    def middle(self):
        net, p = self.net, self.net.place
        self.across.wait_recv()
        got = self.slot(p.a, p.core, 1 - p.zh)
        self.far = [net.remote(got, got, o[0]) for o in p.others]
        self.cores.append(net.remote(got, got, p.core_peer))

    def final(self):
        net, p = self.net, self.net.place
        for k, other in enumerate(p.others):
            self.near[k].wait_recv()
            self.far[k].wait_recv()
            got = self.column(other[2], p.core)
            self.cores.append(net.remote(got, got, p.core_peer))

    def done(self):
        self.own.wait()
        for copy in self.cores:
            copy.wait_recv()


class Reduce:
    def __init__(self, net, part, out, held, from_core, from_a, from_zh, from_rank, ranks=True, added=False):
        self.net, self.part, self.out = net, part, out
        self.held, self.from_core, self.from_a = held, from_core, from_a
        self.from_zh, self.from_rank = from_zh, from_rank
        self.ranks, self.added = ranks, added

    def half(self, core):
        return self.part.at[:, :, core] if self.ranks else self.part.at[:, core]

    def begin(self):
        net, p = self.net, self.net.place
        self.load = net.here(self.half(p.core), self.held)
        self.by_core = net.remote(self.half(1 - p.core), self.from_core, p.core_peer)

    def along_a(self):
        net, p = self.net, self.net.place
        self.load.wait()
        self.by_core.wait_recv()
        add_into(self.held, self.from_core)
        self.by_a = [
            net.remote(self.held.at[other[1]], self.from_a.at[k], other[0])
            for k, other in enumerate(p.others)
        ]

    def along_zh(self):
        net, p = self.net, self.net.place
        mine = self.held.at[p.a]
        for k, copy in enumerate(self.by_a):
            copy.wait_recv()
            add_into(mine, self.from_a.at[k])
        there = mine.at[:, 1 - p.zh] if self.ranks else mine.at[1 - p.zh]
        self.by_zh = net.remote(there, self.from_zh, p.zh_peer)

    def among_ranks(self):
        net, p = self.net, self.net.place
        self.by_zh.wait_recv()
        if not self.ranks:
            self.out[...] = self.held[p.a, p.zh].astype(F32) + self.from_zh[...].astype(F32)
            return
        for x in range(2):
            for zl in range(2):
                add_into(self.held.at[p.a, x, p.zh, zl], self.from_zh.at[x, zl])
        self.by_rank = []
        for device, rank in p.peers:
            rank_x, rank_zl = lax.div(rank, 2), lax.rem(rank, 2)
            self.by_rank.append(
                net.remote(
                    self.held.at[p.a, rank_x, p.zh, rank_zl], self.from_rank.at[len(self.by_rank)], device
                )
            )

    def done(self):
        if not self.ranks:
            return
        p = self.net.place
        own = self.held[p.a, p.x, p.zh, p.zl].astype(F32)
        for copy in self.by_rank:
            copy.wait_recv()
        if self.added:
            for j in range(3):
                own = own + self.from_rank[j].astype(F32)
            self.out[...] = own
            return
        self.out[p.rank] = own
        for j, (_, rank) in enumerate(p.peers):
            self.out[rank] = self.from_rank[j].astype(F32)

    @staticmethod
    def scratch(shape, ranks=True):
        tail = shape[-2:]
        count = shape[0]
        inner = ((2, 2, 2) if ranks else (2,)) + tail
        fewer = ((2, 2) if ranks else ()) + tail
        shapes = [(count,) + inner, (count,) + inner, (max(count - 1, 1),) + inner, fewer]
        if ranks:
            shapes.append((3,) + tail)
        return [pltpu.VMEM(s, BF16) for s in shapes]


def add_into(target, source):
    lead = target.shape[:-2]
    total = 1
    for size in lead:
        total *= size
    if total == 1 and not lead:
        target[...] = (target[...].astype(F32) + source[...].astype(F32)).astype(BF16)
        return

    @pl.loop(0, total)
    def _(j):
        index, left = [], j
        for size in reversed(lead):
            index.append(lax.rem(left, size))
            left = lax.div(left, size)
        index = tuple(reversed(index))
        target[index] = (target[index].astype(F32) + source[index].astype(F32)).astype(BF16)


def spread(net, land):
    mine = land.at[net.place.rank]
    return [net.remote(mine, mine, device) for device, _ in net.place.peers]


def push(net, out, land, i):
    return net.remote(out.at[i], land.at[i], net.place.peers[i][0])


def products(x, w_ref, count, tile, transposed, use):
    @pl.loop(0, count // tile)
    def _(j):
        cols = pl.ds(pl.multiple_of(j * tile, tile), tile)
        if transposed:
            w, dims = w_ref[cols, :], (((1,), (1,)), ((), ()))
        else:
            w, dims = w_ref[:, cols], (((1,), (0,)), ((), ()))
        use(cols, lax.dot_general(x(), w, dims, preferred_element_type=F32))


def norm_rows(h, gain):
    factor = lax.rsqrt(jnp.mean(h * h, axis=-1, keepdims=True) + NORM_EPS)
    return (h * factor * gain).astype(BF16)


def norm_rows_back(h, gain, grad):
    factor = lax.rsqrt(jnp.mean(h * h, axis=-1, keepdims=True) + NORM_EPS)
    z = grad * gain
    inner = jnp.sum(z * h, axis=-1, keepdims=True)
    back = factor * z - h * (factor * factor * factor * inner / h.shape[-1])
    return back, jnp.sum(grad * h * factor, axis=0, keepdims=True)


def landed_sum(first, land):
    return first + land[0].astype(F32) + land[1].astype(F32) + land[2].astype(F32)


def rows_of(rank, rows):
    return pl.ds(pl.multiple_of(rank * rows, rows), rows)


class Refs:
    def __init__(self, refs):
        self.refs = list(refs)

    def take(self, n):
        got, self.refs = self.refs[:n], self.refs[n:]
        return got


class Ticks:
    def __init__(self, plan):
        self.plan = list(plan)

    def __call__(self):
        if self.plan:
            for step in self.plan.pop(0):
                step()

    def rest(self):
        while self.plan:
            self()


def start_kernel(count, n, ahead, *refs):
    refs = Refs(refs)
    (tokens,) = refs.take(1)
    pieces, later = refs.take(n), refs.take(ahead)
    (all_tokens,) = refs.take(1)
    full, blocks_later = refs.take(n), refs.take(ahead)
    (land,) = refs.take(1)
    blocks = refs.take(n)
    send, recv, local = refs.take(3)
    place = Place(count)
    net = Net(place, send, recv, local)
    shares = [Share(net, pieces[i], blocks[i]) for i in range(n)]
    gathers = [Gather(net, blocks[i], full[i]) for i in range(n)]
    shares_later = [Share(net, later[i], blocks_later[i]) for i in range(ahead)]
    swap = Swap(net, tokens, land.at[place.zh * 2 + place.zl])
    place.greet(True, True)
    shares[0].start()
    swap.start()
    shares[1].start()
    shares[0].wait()
    gathers[0].begin()
    swap.wait()
    spreads = spread(net, land)
    shares[1].wait()
    gathers[1].begin()
    for share in shares[2:]:
        share.start()
    gathers[0].middle()
    for i in range(2, n):
        shares[i].wait()
        gathers[i].begin()
        gathers[i - 1].middle()
        gathers[i - 2].final()
        if i == 2:
            for copy in spreads:
                copy.wait_recv()
            keep = net.here(land, all_tokens)
            for share in shares_later:
                share.start()
    gathers[n - 1].middle()
    gathers[n - 2].final()
    gathers[n - 1].final()
    for gather in gathers:
        gather.done()
    for share in shares_later:
        share.wait()
    keep.wait()
    net.finish()


def body_kernel(count, rows, more, *refs):
    refs = Refs(refs)
    o_ref, h_ref, gain_ref, wo_hbm, wgate_hbm, wup_hbm, down_hbm = refs.take(7)
    if more:
        (gain_next,) = refs.take(1)
        blocks = refs.take(more)
    else:
        (swap_src,) = refs.take(1)
    h1_ref, hn_ref, gate_ref, up_ref, u_ref, ng_hbm, wd_out = refs.take(7)
    if more:
        (nn_hbm,) = refs.take(1)
        full = refs.take(more)
    else:
        (swap_dst,) = refs.take(1)
    wo, wgu, wd_blocks, out_a, land_a, land_n, out_b, land_b = refs.take(8)
    if more:
        (land_q,) = refs.take(1)
    send, recv, local = refs.take(3)

    place = Place(count)
    net = Net(place, send, recv, local)
    width = h_ref.shape[1]
    hidden = wgate_hbm.shape[1]
    load_out = net.here(wo_hbm, wo)
    load_gate = net.here(wgate_hbm, wgu.at[:, pl.ds(0, hidden)])
    load_up = net.here(wup_hbm, wgu.at[:, pl.ds(hidden, hidden)])
    peers = place.peers
    place.greet(True, not more)
    down = Gather(net, down_hbm, wd_blocks, ranks=False)
    wd = wd_blocks.reshape(hidden, width)
    jobs = [Gather(net, blocks[i], full[i]) for i in range(more)]
    if more:
        j = jobs
        tick = Ticks(
            [
                [down.begin],
                [j[0].begin],
                [down.middle],
                [j[1].begin, down.final],
                [j[0].middle, j[2].begin],
                [j[0].final, j[1].middle],
                [j[1].final],
                [j[2].middle, j[3].begin],
                [j[2].final],
                [j[3].middle],
                [j[3].final],
            ]
        )
    else:
        swap = Swap(net, swap_src, swap_dst)
        tick = Ticks([[down.begin], [], [down.middle], [swap.start, down.final]])
    tick()
    load_out.wait()

    sums = [None] * 3
    for i in (2, 0, 1):
        span = rows_of(peers[i][1], rows)

        def use(cols, y, i=i):
            out_a[i, :, cols] = y.astype(BF16)

        products(lambda: o_ref[span, :], wo, width, 512, True, use)
        sums[i] = push(net, out_a, land_a, i)
    span = rows_of(place.rank, rows)

    def use_own(cols, y):
        h1_ref[:, cols] = h_ref[:, cols].astype(F32) + y

    products(lambda: o_ref[span, :], wo, width, 512, True, use_own)
    tick()
    for copy in sums:
        copy.wait_recv()
    h1 = landed_sum(h1_ref[...], land_a)
    h1_ref[...] = h1
    land_n[place.rank] = norm_rows(h1, gain_ref[...])
    gather = spread(net, land_n)
    tick()
    load_gate.wait()
    load_up.wait()

    def inner_block(rank):
        span = rows_of(rank, rows)

        @pl.loop(0, hidden // 256)
        def _(j):
            cols = pl.ds(pl.multiple_of(j * 256, 256), 256)
            ups = pl.ds(pl.multiple_of(j * 256 + hidden, 256), 256)
            gate = jnp.dot(land_n[rank], wgu[:, cols], preferred_element_type=F32)
            up = jnp.dot(land_n[rank], wgu[:, ups], preferred_element_type=F32)
            gate_ref[span, cols] = gate
            up_ref[span, cols] = up
            u_ref[span, cols] = (gate / (1.0 + jnp.exp(-gate)) * up).astype(BF16)

        return span

    span = inner_block(place.rank)
    tick()
    second = []
    for i, (_, rank) in enumerate(peers):
        gather[i].wait_recv()
        span = inner_block(rank)
        if i == 0:
            down.done()
            keep_down = net.here(wd_blocks, wd_out)

        def use(cols, y, i=i):
            out_b[i, :, cols] = y.astype(BF16)

        products(lambda: u_ref[span, :], wd, width, 512, False, use)
        second.append(push(net, out_b, land_b, i))
        tick()
    keep = net.here(land_n, ng_hbm)
    span = rows_of(place.rank, rows)

    def use_down(cols, y):
        hn_ref[:, cols] = h1_ref[:, cols] + y

    products(lambda: u_ref[span, :], wd, width, 512, False, use_down)
    for copy in second:
        copy.wait_recv()
    hn = landed_sum(hn_ref[...], land_b)
    hn_ref[...] = hn
    if more:
        land_q[place.rank] = norm_rows(hn, gain_next[...])
        third = spread(net, land_q)
        tick()
        for copy in third:
            copy.wait_recv()
            tick()
        keep_next = net.here(land_q, nn_hbm)
        keep_next.wait()
    tick.rest()
    if more:
        for job in jobs:
            job.done()
    else:
        swap.wait()
    keep.wait()
    keep_down.wait()
    net.finish()


def back_kernel(count, rows, first, last, n_red, *refs):
    refs = Refs(refs)
    if first:
        g_ref, swap_src = refs.take(2)
    else:
        dqkv_ref, wq_hbm, ghin_ref, hin_ref, gainin_ref = refs.take(5)
    if not last:
        wd_hbm, wgate_hbm, wup_hbm, wo_hbm, gate_ref, up_ref, h1_ref, gain_ref = refs.take(8)
    else:
        (other_gains,) = refs.take(1)
    parts = refs.take(n_red)
    if first:
        (swap_dst,) = refs.take(1)
    elif not last:
        gnew_ref, ggin_ref = refs.take(2)
    else:
        swap_dst, gains_out = refs.take(2)
    if not last:
        gbg_hbm, dgu_ref, gh_ref, gg_ref, ghg_hbm, do_ref = refs.take(6)
    red_out = refs.take(n_red)
    if not first:
        wq, out_a, land_a = refs.take(3)
    if last:
        gnew_ref, gains_all, gains_part = refs.take(3)
        gains_scratch = refs.take(5)
    if not last:
        wd, wgu, wo, land_g, out_b, land_b, land_h = refs.take(7)
    red_scratch = [refs.take(4 if i == 0 else 5) for i in range(n_red)]
    send, recv, local = refs.take(3)

    place = Place(count)
    net = Net(place, send, recv, local)
    jobs = []
    for i in range(n_red):
        scratch = red_scratch[i] + ([None] if i == 0 else [])
        jobs.append(Reduce(net, parts[i], red_out[i], *scratch, ranks=i > 0))
    peers = place.peers
    if not first:
        load_q = net.here(wq_hbm.at[:, pl.ds(0, wq.shape[1])], wq)
    if not last:
        hidden = wd.shape[0]
        load_down = net.here(wd_hbm, wd)
        load_gate = net.here(wgate_hbm, wgu.at[:, pl.ds(0, hidden)])
        load_up = net.here(wup_hbm, wgu.at[:, pl.ds(hidden, hidden)])
        load_out = net.here(wo_hbm, wo)
    place.greet(n_red > 0, first or last)
    if first:
        swap = Swap(net, swap_src, swap_dst)
        tick = Ticks([[swap.start]])
    elif not last:
        j = jobs
        tick = Ticks(
            [
                [j[0].begin, j[1].begin],
                [j[0].along_a, j[2].begin],
                [j[1].along_a, j[3].begin],
                [j[0].along_zh, j[4].begin],
                [],
                [j[2].along_a],
                [j[1].along_zh],
                [j[0].among_ranks, j[3].along_a],
                [j[2].along_zh],
                [j[1].among_ranks, j[4].along_a],
                [j[3].along_zh],
                [j[2].among_ranks, j[4].along_zh],
                [j[1].done, j[2].done, j[3].among_ranks, j[4].among_ranks],
                [j[3].done, j[4].done],
            ]
        )
    else:
        j = jobs
        tick = Ticks(
            [
                [j[0].begin, j[1].begin, j[2].begin],
                [j[0].along_a, j[3].begin, j[4].begin],
            ]
        )
    tick()
    own = rows_of(place.rank, rows)
    if not first:
        load_q.wait()
        width = ghin_ref.shape[1]
        total = [None] * 3
        for i in (2, 0, 1):
            span = rows_of(peers[i][1], rows)

            def use(cols, y, i=i):
                out_a[i, :, cols] = y.astype(BF16)

            products(lambda: dqkv_ref[span, :], wq, width, 512, True, use)
            total[i] = push(net, out_a, land_a, i)

        def use_own(cols, y):
            gnew_ref[:, cols] = y

        products(lambda: dqkv_ref[own, :], wq, width, 512, True, use_own)
        tick()
        for copy in total:
            copy.wait_recv()
        dn = landed_sum(gnew_ref[...], land_a)
        back, ggain = norm_rows_back(hin_ref[...].astype(F32), gainin_ref[...], dn)
        gnew_ref[...] = ghin_ref[...] + back
        if last:
            finish_last(
                place, net, jobs, gnew_ref, ggain, other_gains, gains_all, gains_part, gains_scratch,
                gains_out, swap_dst,
            )
            return
        ggin_ref[...] = ggain
        g_ref = gnew_ref
    width = g_ref.shape[1]
    land_g[place.rank] = g_ref[...].astype(BF16)
    gather = spread(net, land_g)
    tick()
    load_down.wait()
    load_gate.wait()
    load_up.wait()

    def inner_block(rank):
        span = rows_of(rank, rows)

        @pl.loop(0, hidden // 256)
        def _(j):
            cols = pl.ds(pl.multiple_of(j * 256, 256), 256)
            ups = pl.ds(pl.multiple_of(j * 256 + hidden, 256), 256)
            du = lax.dot_general(
                land_g[rank], wd[cols, :], (((1,), (1,)), ((), ())), preferred_element_type=F32
            )
            gate, up = gate_ref[span, cols], up_ref[span, cols]
            sg = 1.0 / (1.0 + jnp.exp(-gate))
            dgu_ref[span, cols] = (du * up * sg * (1.0 + gate * (1.0 - sg))).astype(BF16)
            dgu_ref[span, ups] = (du * gate * sg).astype(BF16)

        return span

    span = inner_block(place.rank)

    def use_mid(cols, y):
        gh_ref[:, cols] = y

    products(lambda: dgu_ref[span, :], wgu, width, 512, True, use_mid)
    tick()
    second = []
    for i, (_, rank) in enumerate(peers):
        gather[i].wait_recv()
        span = inner_block(rank)

        def use(cols, y, i=i):
            out_b[i, :, cols] = y.astype(BF16)

        products(lambda: dgu_ref[span, :], wgu, width, 512, True, use)
        second.append(push(net, out_b, land_b, i))
        tick()
    keep = net.here(land_g, gbg_hbm)
    for copy in second:
        copy.wait_recv()
    dn = landed_sum(gh_ref[...], land_b)
    back, ggain = norm_rows_back(h1_ref[...], gain_ref[...], dn)
    gh = g_ref[...].astype(F32) + back
    gh_ref[...] = gh
    gg_ref[...] = ggain
    land_h[place.rank] = gh.astype(BF16)
    third = spread(net, land_h)
    tick()
    load_out.wait()

    def out_block(rank):
        span = rows_of(rank, rows)

        def use(cols, y):
            do_ref[span, cols] = y.astype(BF16)

        products(lambda: land_h[rank], wo, wo.shape[1], wo.shape[1], False, use)

    out_block(place.rank)
    for i, (_, rank) in enumerate(peers):
        tick()
        third[i].wait_recv()
        out_block(rank)
    keep_h = net.here(land_h, ghg_hbm)
    tick.rest()
    keep_h.wait()
    keep.wait()
    if first:
        swap.wait()
    net.finish()


def finish_last(place, net, jobs, gnew_ref, ggain, other_gains, gains_all, gains_part, scratch, gains_out, swap_dst):
    swap = Swap(net, gnew_ref, swap_dst)
    swap.start()
    gains_all[...] = other_gains[...]
    gains_all[0:1, :] = ggain
    gains_part[...] = jnp.zeros(gains_part.shape, BF16)
    count = gains_part.shape[0]
    piece = gains_all.shape[1] // (16 * count)
    for block in range(16 * count):
        index = (block // 16, block // 8 % 2, block // 4 % 2, block // 2 % 2, block % 2)
        gains_part[index + (slice(None), slice(0, piece))] = gains_all[
            :, block * piece : (block + 1) * piece
        ].astype(BF16)
    small = Reduce(net, gains_part, gains_out, *scratch, added=True)
    small.begin()
    j = jobs
    j[1].along_a()
    j[0].along_zh()
    small.along_a()
    j[2].along_a()
    j[1].along_zh()
    small.along_zh()
    j[0].among_ranks()
    j[3].along_a()
    j[2].along_zh()
    small.among_ranks()
    j[1].among_ranks()
    j[4].along_a()
    j[3].along_zh()
    j[2].among_ranks()
    j[1].done()
    j[4].along_zh()
    j[3].among_ranks()
    j[2].done()
    small.done()
    j[4].among_ranks()
    j[3].done()
    j[4].done()
    swap.wait()
    net.finish()


def pack_weights(w_qkv, w_out, w_gate_up, gains, count, layer):
    rows = w_qkv.shape[1]
    attn_cols = HEADS * HEAD_DIM
    kv_cols = KV_HEADS * HEAD_DIM
    qkv = w_qkv[layer]
    q = qkv[:, :attn_cols].reshape(rows, RANKS, -1)
    k = qkv[:, attn_cols : attn_cols + kv_cols].reshape(rows, RANKS, -1)
    v = qkv[:, attn_cols + kv_cols :].reshape(rows, RANKS, -1)
    columns = [q, k, v]
    if layer == 0:
        scales = jnp.pad(gains.reshape(2 * LAYERS, rows).T, ((0, 0), (0, GAIN_COLS - 2 * LAYERS)))
        columns.append(jnp.broadcast_to(scales[:, None], (rows, RANKS, GAIN_COLS)))
    head = jnp.concatenate(columns, axis=2).transpose(1, 0, 2)
    out = w_out[layer].T.reshape(rows, RANKS, -1).transpose(1, 0, 2)
    gu = w_gate_up[layer].reshape(rows, 2, count, 2, 2, 2, 2, -1)
    gu = gu.transpose(1, 3, 6, 0, 2, 4, 5, 7).reshape(2, RANKS, rows, -1)
    return head, out, gu[0], gu[1]


def unpack_grads(head, out, gate, up, count):
    rows = head.shape[1]
    q_cols = HEADS * HEAD_DIM // RANKS
    kv_cols = KV_HEADS * HEAD_DIM // RANKS
    wide = lambda part: part.transpose(1, 0, 2).reshape(rows, -1)
    qkv = jnp.concatenate(
        [
            wide(head[:, :, :q_cols]),
            wide(head[:, :, q_cols : q_cols + kv_cols]),
            wide(head[:, :, q_cols + kv_cols : q_cols + 2 * kv_cols]),
        ],
        axis=1,
    )
    order = lambda part: (
        part.reshape(2, 2, rows, count, 2, 2, -1).transpose(2, 3, 0, 4, 5, 1, 6).reshape(rows, -1)
    )
    return qkv, wide(out).T, jnp.stack([order(gate), order(up)], axis=1)


def rotary_tables(positions, head_size):
    half_size = head_size // 2
    freq_index = jnp.arange(half_size).astype(F32)
    inverse = jnp.exp(freq_index * (-2.0 * jnp.log(ROPE_BASE) / head_size))
    angles = positions.astype(F32)[:, None] * inverse[None, :]
    return (jnp.cos(angles), jnp.sin(angles))


def rotate(values, cosine, sine_tab):
    half_size = values.shape[-1] // 2
    first, second = values[..., :half_size], values[..., half_size:]
    c, s = cosine[:, None, :], sine_tab[:, None, :]
    return jnp.concatenate([first * c - second * s, second * c + first * s], axis=-1)


def unrotate(grads, cosine, sine_tab):
    return rotate(grads, cosine, -sine_tab)


def attend(proj, cosine, sine_tab, causal):
    length = proj.shape[0]
    kv = KV_HEADS // RANKS
    groups = HEADS // KV_HEADS
    q_cols = kv * groups * HEAD_DIM
    kv_cols = kv * HEAD_DIM
    query = rotate(proj[:, :q_cols].reshape(length, kv * groups, HEAD_DIM), cosine, sine_tab)
    query = query.astype(BF16).reshape(length, kv, groups, HEAD_DIM)
    key = rotate(proj[:, q_cols : q_cols + kv_cols].reshape(length, kv, HEAD_DIM), cosine, sine_tab)
    key = key.astype(BF16)
    value = proj[:, q_cols + kv_cols :].astype(BF16).reshape(length, kv, HEAD_DIM)
    scale = HEAD_DIM ** (-0.5)
    scores = jnp.einsum("qkgd,skd->kgqs", query, key, preferred_element_type=F32) * scale
    scores = jnp.where(causal[None, None], scores, MASKED)
    highest = jnp.max(scores, axis=-1, keepdims=True)
    lse = highest + jnp.log(jnp.sum(jnp.exp(scores - highest), axis=-1, keepdims=True))
    weights = jnp.exp(scores - lse).astype(BF16)
    mixed = jnp.einsum("kgqs,skd->qkgd", weights, value, preferred_element_type=F32).astype(BF16)
    return mixed.reshape(length, q_cols), (query, key, value, lse)


def attend_back(saved, mixed, grad_mixed, cosine, sine_tab, causal):
    query, key, value, lse = saved
    length = query.shape[0]
    grad_mixed = grad_mixed.reshape(query.shape)
    mixed = mixed.reshape(query.shape)
    scale = HEAD_DIM ** (-0.5)
    scores = jnp.einsum("qkgd,skd->kgqs", query, key, preferred_element_type=F32) * scale
    scores = jnp.where(causal[None, None], scores, MASKED)
    weights = jnp.exp(scores - lse)
    grad_weights = jnp.einsum("qkgd,skd->kgqs", grad_mixed, value, preferred_element_type=F32)
    delta = jnp.sum(grad_mixed.astype(F32) * mixed.astype(F32), axis=-1)
    delta = jnp.transpose(delta, (1, 2, 0))[..., None]
    grad_scores = (weights * (grad_weights - delta) * scale).astype(BF16)
    grad_query = jnp.einsum("kgqs,skd->qkgd", grad_scores, key, preferred_element_type=F32)
    grad_key = jnp.einsum("kgqs,qkgd->skd", grad_scores, query, preferred_element_type=F32)
    grad_value = jnp.einsum(
        "kgqs,qkgd->skd", weights.astype(BF16), grad_mixed, preferred_element_type=F32
    )
    grad_query = unrotate(grad_query.reshape(length, -1, HEAD_DIM), cosine, sine_tab)
    grad_key = unrotate(grad_key, cosine, sine_tab)
    return jnp.concatenate(
        [g.reshape(length, -1) for g in (grad_query, grad_key, grad_value)], axis=1
    ).astype(BF16)


VM = pl.BlockSpec(memory_space=pltpu.VMEM)
AN = pl.BlockSpec(memory_space=pl.ANY)


def params(collective_id):
    return pltpu.CompilerParams(
        collective_id=collective_id, has_side_effects=True, vmem_limit_bytes=VMEM_BYTES
    )


def like(shape, dtype=BF16):
    return jax.ShapeDtypeStruct(tuple(shape), dtype)


def full_shape(count, tail):
    return (count, 2, 2, 2, 2) + tuple(tail)


def call_start(count, tokens, pieces, later):
    rows, width = tokens.shape
    n, ahead = len(pieces), len(later)
    got = pl.pallas_call(
        functools.partial(start_kernel, count, n, ahead),
        out_shape=[like((RANKS, rows, width))]
        + [like(full_shape(count, p.shape[1:])) for p in pieces]
        + [like((2, 2) + p.shape[1:]) for p in later],
        in_specs=[AN] * (1 + n + ahead),
        out_specs=[AN] * (1 + n + ahead),
        scratch_shapes=[pltpu.VMEM((RANKS, rows, width), BF16)]
        + [pltpu.VMEM((2, 2) + p.shape[1:], BF16) for p in pieces]
        + sems(count),
        compiler_params=params(1),
        name="start",
    )(tokens, *pieces, *later)
    return got[0], [f.reshape(-1, f.shape[-1]) for f in got[1 : n + 1]], got[n + 1 :]


def call_body(count, o, h, gain, weights, down, extra):
    rows, width = h.shape
    tall = RANKS * rows
    wo, wgate, wup = weights
    hidden = wgate.shape[1]
    more = len(extra) - 1
    blocks = extra[1:]
    three = pltpu.VMEM((3, rows, width), BF16)
    four = pltpu.VMEM((RANKS, rows, width), BF16)
    wd_shape = (count, 2, 2) + down.shape
    got = pl.pallas_call(
        functools.partial(body_kernel, count, rows, more),
        out_shape=[
            like((rows, width), F32),
            like((rows, width), F32),
            like((tall, hidden), F32),
            like((tall, hidden), F32),
            like((tall, hidden)),
            like((RANKS, rows, width)),
            like(wd_shape),
        ]
        + (
            [like((RANKS, rows, width))] + [like(full_shape(count, b.shape[2:])) for b in blocks]
            if more
            else [like(extra[0].shape)]
        ),
        in_specs=[VM, VM, VM, AN, AN, AN, AN] + ([VM] + [AN] * more if more else [AN]),
        out_specs=[VM] * 5 + [AN] * 2 + [AN] * (1 + more),
        scratch_shapes=[
            pltpu.VMEM(wo.shape, BF16),
            pltpu.VMEM((width, 2 * hidden), BF16),
            pltpu.VMEM(wd_shape, BF16),
            three,
            three,
            four,
            three,
            three,
        ]
        + ([four] if more else [])
        + sems(count),
        compiler_params=params(2 if more else 3),
        name="body_more" if more else "body",
    )(o, h, gain, wo, wgate, wup, down, *extra)
    got = list(got)
    got[6] = got[6].reshape(-1, width)
    return got[:7], got[7], [f.reshape(-1, f.shape[-1]) for f in got[8:]]


def call_back(count, start, rest, parts):
    first, last = len(start) == 2, len(rest) == 1
    rows, width = start[0].shape if first else start[2].shape
    tall = RANKS * rows
    three = pltpu.VMEM((3, rows, width), BF16)
    four = pltpu.VMEM((RANKS, rows, width), BF16)
    in_specs = [VM, AN] if first else [VM, AN, VM, VM, VM]
    in_specs += [VM] if last else [AN, AN, AN, AN, VM, VM, VM, VM]
    n_red = len(parts)
    in_specs += [AN] * n_red
    outs, out_specs, scratch = [], [], []
    if first:
        outs, out_specs = [like(start[1].shape, start[1].dtype)], [AN]
    elif not last:
        outs, out_specs = [like((rows, width), F32), like((1, width), F32)], [VM, VM]
    else:
        outs, out_specs = [like((rows, width), F32), like((16, GAIN_COLS), F32)], [AN, VM]
    if not first:
        scratch += [pltpu.VMEM((width, start[0].shape[1]), BF16), three, three]
    if last:
        gains_shape = full_shape(count, (16, GAIN_COLS))
        scratch += [
            pltpu.VMEM((rows, width), F32),
            pltpu.VMEM((16, width), F32),
            pltpu.VMEM(gains_shape, BF16),
        ]
        scratch += Reduce.scratch(gains_shape)
    else:
        wd, wgate, wup, wo = rest[:4]
        hidden = wgate.shape[1]
        outs += [
            like((RANKS, rows, width)),
            like((tall, 2 * hidden)),
            like((rows, width), F32),
            like((1, width), F32),
            like((RANKS, rows, width)),
            like((tall, wo.shape[1])),
        ]
        out_specs += [AN, VM, VM, VM, AN, VM]
        scratch += [pltpu.VMEM(s, BF16) for s in (wd.shape, (width, 2 * hidden), wo.shape)]
        scratch += [four, three, three, four]
    for i, part in enumerate(parts):
        scratch += Reduce.scratch(part.shape, ranks=i > 0)
        tail = part.shape[-2:]
        outs.append(like(tail if i == 0 else (RANKS,) + tail, F32))
        out_specs.append(VM)
    return pl.pallas_call(
        functools.partial(back_kernel, count, rows, first, last, n_red),
        out_shape=outs,
        in_specs=in_specs,
        out_specs=out_specs,
        scratch_shapes=scratch + sems(count),
        compiler_params=params(4 if first else (6 if last else 5)),
        name="back_first" if first else ("back_last" if last else "back_mid"),
    )(*start, *rest, *parts)


def dot_t(a, b):
    return lax.dot_general(a, b, (((0,), (0,)), ((), ())), preferred_element_type=F32).astype(BF16)


def shards(dp_size, ctx_size, tokens, cotangent, w_qkv, w_out, w_gate_up, w_down, gains):
    count = dp_size // 4
    rows, width = tokens.shape
    length = RANKS * rows
    hidden = w_gate_up.shape[-1] // RANKS
    positions = jnp.arange(length, dtype=jnp.int32)
    cosine, sine_tab = rotary_tables(positions, HEAD_DIM)
    causal = positions[None, :] <= positions[:, None]
    tall = lambda value: value.reshape(length, width)
    rank = lax.rem(lax.div(lax.axis_index("dp"), 2), 2) * 2 + lax.rem(lax.axis_index("ctx"), 2)

    packed = [pack_weights(w_qkv, w_out, w_gate_up, gains, count, layer) for layer in range(LAYERS)]
    all_tokens, full, blocks = call_start(count, tokens, packed[0], packed[1])
    gain_rows = full[0][:, -GAIN_COLS:][:, : 2 * LAYERS].astype(F32).T
    gain = lambda layer, which: gain_rows[2 * layer + which][None]
    h = lax.dynamic_index_in_dim(all_tokens, rank, 0, keepdims=False)
    states = tall(all_tokens).astype(F32)
    n1 = norm_rows(states, gain(0, 0))

    records = []
    swapped = None
    for layer in range(LAYERS):
        wq, wo, wgate, wup = full
        wq_now = wq[:, : wq.shape[1] - GAIN_COLS] if layer == 0 else wq
        proj = jnp.dot(tall(n1), wq_now, preferred_element_type=F32)
        mixed, saved = attend(proj, cosine, sine_tab, causal)
        if layer + 1 < LAYERS:
            extra = (gain(layer + 1, 0), *blocks)
        else:
            extra = (cotangent.astype(BF16),)
        got, ahead, full = call_body(
            count, mixed, h, gain(layer, 1), (wo, wgate, wup), w_down[layer], extra
        )
        h1, h_next, gate, up, u, n2, wd = got
        records.append((h, n1, saved, mixed, h1, n2, gate, up, u, (wq, wo, wgate, wup, wd)))
        h = h_next
        if layer + 1 < LAYERS:
            n1 = ahead
        else:
            g = ahead

    shape7 = lambda value: value.reshape(count, 2, 2, 2, 2, -1, value.shape[-1])
    start, parts = (g, h), []
    grads = [None] * LAYERS
    gain_grads = [None] * (2 * LAYERS)
    for layer in reversed(range(LAYERS)):
        h_in, n1, saved, mixed, h1, n2, gate, up, u, (wq, wo, wgate, wup, wd) = records[layer]
        got = call_back(count, start, (wd, wgate, wup, wo, gate, up, h1, gain(layer, 1)), parts)
        if layer == LAYERS - 1:
            out_act, *got = got
        else:
            _, gain_grads[2 * layer + 2], *got = got
            grads[layer + 1] = got[6:]
        gbg, dgu, gh, gain_grads[2 * layer + 1], ghg, do = got[:6]
        dqkv = attend_back(saved, mixed, do, cosine, sine_tab, causal)
        parts = [
            dot_t(u, tall(gbg)).reshape(count, 2, 2, -1, width),
            shape7(dot_t(tall(n2), dgu[:, :hidden])),
            shape7(dot_t(tall(n2), dgu[:, hidden:])),
            shape7(dot_t(tall(ghg), mixed)),
            shape7(dot_t(tall(n1), dqkv)),
        ]
        start = (dqkv, wq, gh, h_in, gain(layer, 0))
    others = jnp.concatenate([jnp.zeros((1, width), F32)] + gain_grads[1:], axis=0)
    others = jnp.pad(others, ((0, 16 - 2 * LAYERS), (0, 0)))
    grad_tokens, gains_sum, *last = call_back(count, start, (others,), parts)
    grads[0] = last
    piece = gains.shape[-1]
    grad_gains = gains_sum[: 2 * LAYERS, :piece].reshape(LAYERS, 2, piece)
    stacked = [unpack_grads(q, o, gate, up, count) for _, gate, up, o, q in grads]
    s_qkv, s_out, s_gu = (jnp.stack([s[i] for s in stacked]) for i in range(3))
    s_down = jnp.stack([g[0] for g in grads])
    return (out_act, grad_tokens, s_qkv, s_out, s_gu, s_down, grad_gains)


def solution(mesh):
    both = ("dp", "ctx")
    return jax.shard_map(
        functools.partial(shards, mesh.shape["dp"], mesh.shape["ctx"]),
        mesh=mesh,
        in_specs=(
            P(both, None),
            P(both, None),
            P(None, both, None),
            P(None, None, both),
            P(None, both, None, None),
            P(None, both, None),
            P(None, None, both),
        ),
        out_specs=(
            P(both, None),
            P(both, None),
            P(None, both, None),
            P(None, None, both),
            P(None, both, None, None),
            P(None, both, None),
            P(None, None, both),
        ),
        check_vma=False,
    )
```

time: 2730 us -> 834 us (0.31)
  waiting for transfers between devices: 2020 us -> 0 us
  Pallas kernels: 0 us -> 682 us
  local copies, waits for them, and re-layouts: 210 us -> 41.5 us
  blocking collectives: 160 us -> 0 us
  matrix products: 222 us -> 71.5 us
  other arithmetic: 85.1 us -> 25.3 us
    unnamed x40 -> x0, waiting for transfers between devices: 930 us -> none
    pallas_call x0 -> x6, Pallas kernels: none -> 682 us  [the longest x3 371 us: call_back(): pl.pallas_call(functools.partial(back_kernel, count, rows, first, last, n...]
    all_gather x10 -> x0, waiting for transfers between devices: 562 us -> none  [the longest x2 287 us: fetch_layer(): lax.all_gather(w_gate_up[layer_index], ('dp', 'ctx'), axis=0, tiled=True)]
    reduce_scatter x12 -> x0, waiting for transfers between devices: 529 us -> none  [the longest x2 191 us: reduce_grads(): lax.psum_scatter(grad_tuple[3].astype(jnp.bfloat16), 'dp', scatter_dimens...]
    all_gather x2 -> x0, blocking collectives: 160 us -> none  [fetch_layer(): lax.all_gather(gains[layer_index], ('dp', 'ctx'), axis=1, tiled=True)]
    dot_general x36 -> x24, matrix products: 222 us -> 71.5 us  [the longest x10 34.5 us: dot_t(): lax.dot_general(a, b, (((0,), (0,)), ((), ())), preferred_element_type=F32)]
    unnamed x119 -> x117, local copies, waits for them, and re-layouts: 100 us -> 6.49 us
    convert_element_type x6 -> x0, local copies, waits for them, and re-layouts: 86.6 us -> none  [the longest x2 82.5 us: reduce_grads(): grad_tuple[2].astype(jnp.bfloat16)]
  transfers between devices with their start and end apart: 31 -> 0, of which waited for: 25 -> 0; matrix products, arithmetic and copies ran while one was open for 14% -> 0% of each run, Pallas kernels for 0% -> 0%
where the time goes in v2:
time: 834 us; the launch traced here: 823 us
  Pallas kernels  682 us (82%)
  matrix products  71.5 us (9%)
  local copies, waits for them, and re-layouts  41.5 us (5%)
  other arithmetic  25.3 us (3%)
    pallas_call x3, Pallas kernels, call_back(): pl.pallas_call(functools.partial(back_kernel, count, rows, first, last, n...  371 us
    pallas_call x2, Pallas kernels, call_body(): pl.pallas_call(functools.partial(body_kernel, count, rows, more), out_sha...  215 us
    pallas_call x1, Pallas kernels, call_start(): pl.pallas_call(functools.partial(start_kernel, count, n, ahead), out_shap...  96.5 us
    dot_general x10, matrix products, dot_t(): lax.dot_general(a, b, (((0,), (0,)), ((), ())), preferred_element_type=F32)  34.5 us

profile of v2, /device:TPU:0, one launch (start us, length us, event | category | flops | bytes accessed | tf_op | source)
XLA Modules:
  0.0 822.7 jit_solution(4889836014215712366)
XLA Ops:
  0.6 1.1 slice_bitcast_fusion.4
  5.1 2.9 fusion.35
  9.6 1.0 squeeze.36.refs_3_
  10.6 1.0 squeeze.37.refs_4_
  13.2 1.0 squeeze.40.refs_7_
  15.3 96.5 %start.1 = (bf16[4,128,1536]{2,1,0:T(8,128)(2,1)}, bf16[2,2,2,2,2,48,896]{6,5,4,3,2,1,0:T(8,128)(2,1)}, bf16[2,2,2,2,2,48,384]{6,5,4,3,2,1,0:T(8,128)(2,1)}, bf1...) custom-call(bf16[128,1536]{1,0:T(8,128)(2,1)} %refs_0_.1, ...), custom_call_target="tpu_custom_call" | custom-call | tf_op jit(solution)/shard_map/start/pallas_call | solution.py:915
  111.8 1.2 slice_convert_fusion.2
  115.7 1.4 fusion.12
  117.1 1.1 copy-done.4
  120.9 2.9 fusion.10
  123.8 3.2 exponential_reduce_fusion.1
  128.0 3.6 convolution_convert_fusion.11
  134.3 127.7 %body_more.1 = (f32[128,1536]{1,0:T(8,128)}, f32[128,1536]{1,0:T(8,128)}, f32[512,1024]{1,0:T(8,128)}, f32[512,1024]{1,0:T(8,128)}, bf16[512,1024]{1,0:T(8,128)(...) custom-call(bf16[512,384]{1,0:T(8,128)(2,1)} %copy.77.refs_0_, ...), custom_call_target="tpu_custom_call" | custom-call | tf_op jit(solution)/shard_map/body_more/pallas_call | solution.py:941
  262.0 3.5 fusion.42
  265.5 1.1 copy-done.6
  268.0 2.9 fusion.11
  271.0 3.2 exponential_reduce_fusion
  274.5 3.5 convolution_convert_fusion.10
  279.8 87.0 %body.1 = (f32[128,1536]{1,0:T(8,128)}, f32[128,1536]{1,0:T(8,128)}, f32[512,1024]{1,0:T(8,128)}, f32[512,1024]{1,0:T(8,128)}, bf16[512,1024]{1,0:T(8,128)(2,1)}...) custom-call(bf16[512,384]{1,0:T(8,128)(2,1)} %copy.82.refs_0_, ...), custom_call_target="tpu_custom_call" | custom-call | tf_op jit(solution)/shard_map/body/pallas_call | solution.py:941
  366.9 90.0 %back_first.1 = (f32[128,1536]{1,0:T(8,128)}, bf16[4,128,1536]{2,1,0:T(8,128)(2,1)}, bf16[512,2048]{1,0:T(8,128)(2,1)}, f32[128,1536]{1,0:T(8,128)}, f32[1,1536]...) custom-call(bf16[128,1536]{1,0:T(8,128)(2,1)} %get-tuple-element.77.refs_0_, ...), custom_call_target="tpu_custom_call" | custom-call | tf_op jit(solution)/shard_map/back_first/pallas_call | solution.py:1025
  456.9 1.2 copy.83
  458.2 3.8 fusion.5
  463.6 1.8 convolution_bitcast_fusion.3
  465.6 3.5 fusion.14
  469.5 4.6 convolution_convert_fusion.7
  474.1 2.0 convolution_convert_fusion.9
  476.1 3.5 convolution_convert_fusion.3
  479.6 3.7 convolution_convert_fusion.4
  483.3 3.5 convolution_convert_fusion.5
  486.8 134.3 %back_mid.1 = (f32[128,1536]{1,0:T(8,128)}, f32[1,1536]{1,0:T(1,128)}, bf16[4,128,1536]{2,1,0:T(8,128)(2,1)}, bf16[512,2048]{1,0:T(8,128)(2,1)}, f32[128,1536]{1...) custom-call(bf16[512,768]{1,0:T(8,128)(2,1)} %copy-done.2, ...), custom_call_target="tpu_custom_call" | custom-call | tf_op jit(solution)/shard_map/back_mid/pallas_call | solution.py:1025
  621.2 1.2 copy.90
  622.5 3.9 fusion.2
  627.8 1.9 copy.94
  629.7 1.8 convolution_bitcast_fusion.1
  631.8 3.5 fusion.15
  635.6 4.6 convolution_convert_fusion.6
  640.2 2.0 convolution_convert_fusion.8
  642.3 3.5 convolution_convert_fusion
  645.8 3.5 convolution_convert_fusion.1
  649.2 3.5 convolution_convert_fusion.2
  653.5 146.9 %back_last.1 = (f32[128,1536]{1,0:T(8,128)}, f32[16,128]{1,0:T(8,128)}, f32[128,1536]{1,0:T(8,128)}, f32[4,48,1024]{2,1,0:T(8,128)}, f32[4,48,1024]{2,1,0:T(8,12...) custom-call(bf16[512,768]{1,0:T(8,128)(2,1)} %copy-done.3, bf16[1536,896]{1,0:T(8,128)(2,1)} %bitcast.298, ...), custom_call_target="tpu_custom_call" | custom-call | tf_op jit(solution)/shard_map/back_last/pallas_call | solution.py:1025
  800.4 2.5 pad_maximum_fusion.1
  805.5 1.5 maximum_bitcast_fusion
  808.3 1.8 reshape.442
  810.7 1.5 maximum_bitcast_fusion.1
  812.3 3.3 pad_maximum_fusion
  818.4 1.1 pad_maximum_fusion.2
  819.5 1.3 slice.239
  (221 shorter events, 33.7 us)
Async XLA Ops:
  0.6 2.7 copy-start.45
  1.7 2.6 copy-start.37
  111.8 2.1 copy-start
  113.9 1.8 copy-start.1
  120.1 3.7 copy-start.29
  120.2 3.7 copy-start.31
  123.8 3.2 copy-start.5
  128.0 5.3 copy-start.17
  131.6 130.3 %copy-start.8 = (bf16[2,96,2,512]{3,1,2,0:T(8,128)(2,1)}, bf16[2,96,2,512]{3,1,2,0:T(8,128)(2,1)S(1)}, u32[]{:S(2)}) copy-start(bf16[2,96,2,512]{3,1,2,0:T(8,128)(2,1)S(1)} %convolution_convert_fusion.11) | copy-start | bytes 1179652
  267.1 3.9 copy-start.27
  267.1 3.8 copy-start.28
  268.0 3.0 copy-start.33
  268.0 3.0 copy-start.35
  271.0 3.2 copy-start.7
  274.5 3.6 copy-start.40
  274.5 4.5 copy-start.18
  278.1 180.0 %copy-start.10 = (bf16[2,96,2,512]{3,1,2,0:T(8,128)(2,1)}, bf16[2,96,2,512]{3,1,2,0:T(8,128)(2,1)S(1)}, u32[]{:S(2)}) copy-start(bf16[2,96,2,512]{3,1,2,0:T(8,128)(2,1)S(1)} %convolution_convert_fusion.10) | copy-start | bytes 1179652
  366.8 91.4 %copy-start.41 = (bf16[512,192]{0,1:T(8,128)(2,1)S(1)}, bf16[512,192]{0,1:T(8,128)(2,1)}, u32[]{:S(2)}) copy-start(bf16[512,192]{0,1:T(8,128)(2,1)} %copy-done.40) | copy-start | bytes 589828
  458.2 3.8 copy-start.34
  458.2 3.8 copy-start.36
  465.6 3.6 copy-start.14
  469.4 4.6 copy-start.2
  469.4 4.6 copy-start.11
  469.4 4.6 copy-start.53
  469.5 6.7 copy-start.51
  474.1 2.1 copy-start.47
  479.6 3.7 copy-start.52
  479.6 3.7 copy-start.55
  486.8 135.5 %copy-start.9 = (bf16[2,96,2,512]{3,1,2,0:T(8,128)(2,1)S(1)}, bf16[2,96,2,512]{3,1,2,0:T(8,128)(2,1)}, u32[]{:S(2)}) copy-start(bf16[2,96,2,512]{3,1,2,0:T(8,128)(2,1)} %copy-done.8) | copy-start | bytes 1179652
  622.5 3.9 copy-start.30
  622.5 3.9 copy-start.32
  631.8 3.6 copy-start.13
  635.5 4.7 copy-start.3
  635.6 4.6 copy-start.50
  635.6 6.7 copy-start.48
  640.2 2.1 copy-start.46
  645.8 3.5 copy-start.49
  645.8 3.5 copy-start.54
  649.2 3.5 copy-start.42
  649.2 3.5 copy-start.43
  649.2 3.5 copy-start.44
  653.5 146.9 %copy-start.24 = (f32[128,1536]{1,0:T(8,128)S(1)}, f32[128,1536]{1,0:T(8,128)}, u32[]{:S(2)}) copy-start(f32[128,1536]{1,0:T(8,128)} %get-tuple-element.115) | copy-start | bytes 2359300
  800.4 2.5 copy-start.23
  804.8 2.2 copy-start.20
  812.3 3.3 copy-start.39
  812.3 3.3 copy-start.38
  818.3 2.5 copy-start.19
  818.4 3.3 copy-start.21
  (10 other events, 11.6 us)

commit v3 on v2

--- a/solution.py
+++ b/solution.py
@@ -302,13 +302,49 @@
         target[index] = (target[index].astype(F32) + source[index].astype(F32)).astype(BF16)
 
 
-def spread(net, land):
-    mine = land.at[net.place.rank]
-    return [net.remote(mine, mine, device) for device, _ in net.place.peers]
-
-
-def push(net, out, land, i):
-    return net.remote(out.at[i], land.at[i], net.place.peers[i][0])
+class Spread:
+    def __init__(self, net, land):
+        self.net, self.land = net, land
+        self.peers = net.place.peers
+        mine = land.at[net.place.rank]
+        self.along_x = net.remote(mine, mine, self.peers[0][0])
+        self.along_zl = net.remote(mine, mine, self.peers[1][0])
+
+    def arrivals(self):
+        self.along_zl.wait_recv()
+        got = self.land.at[self.peers[1][1]]
+        relay = self.net.remote(got, got, self.peers[0][0])
+        yield 1, self.peers[1][1]
+        self.along_x.wait_recv()
+        yield 0, self.peers[0][1]
+        relay.wait_recv()
+        yield 2, self.peers[2][1]
+
+    def wait(self):
+        for _ in self.arrivals():
+            pass
+
+
+class Sum:
+    def __init__(self, net, out, land):
+        self.net, self.out, self.land = net, out, land
+        self.peers = net.place.peers
+
+    def ready(self, i):
+        if i == 2:
+            self.diagonal = self.net.remote(self.out.at[2], self.land.at[0], self.peers[0][0])
+        elif i == 0:
+            self.along_x = self.net.remote(self.out.at[0], self.land.at[1], self.peers[0][0])
+
+    def forward(self):
+        self.diagonal.wait_recv()
+        add_into(self.out.at[1], self.land.at[0])
+        self.along_zl = self.net.remote(self.out.at[1], self.land.at[2], self.peers[1][0])
+
+    def result(self, own):
+        self.along_x.wait_recv()
+        self.along_zl.wait_recv()
+        return own + self.land[1].astype(F32) + self.land[2].astype(F32)
 
 
 def products(x, w_ref, count, tile, transposed, use):
@@ -333,10 +369,6 @@
     inner = jnp.sum(z * h, axis=-1, keepdims=True)
     back = factor * z - h * (factor * factor * factor * inner / h.shape[-1])
     return back, jnp.sum(grad * h * factor, axis=0, keepdims=True)
-
-
-def landed_sum(first, land):
-    return first + land[0].astype(F32) + land[1].astype(F32) + land[2].astype(F32)
 
 
 def rows_of(rank, rows):
@@ -388,7 +420,7 @@
     shares[0].wait()
     gathers[0].begin()
     swap.wait()
-    spreads = spread(net, land)
+    spreads = Spread(net, land)
     shares[1].wait()
     gathers[1].begin()
     for share in shares[2:]:
@@ -400,8 +432,7 @@
         gathers[i - 1].middle()
         gathers[i - 2].final()
         if i == 2:
-            for copy in spreads:
-                copy.wait_recv()
+            spreads.wait()
             keep = net.here(land, all_tokens)
             for share in shares_later:
                 share.start()
@@ -470,7 +501,7 @@
     tick()
     load_out.wait()
 
-    sums = [None] * 3
+    sums = Sum(net, out_a, land_a)
     for i in (2, 0, 1):
         span = rows_of(peers[i][1], rows)
 
@@ -478,20 +509,19 @@
             out_a[i, :, cols] = y.astype(BF16)
 
         products(lambda: o_ref[span, :], wo, width, 512, True, use)
-        sums[i] = push(net, out_a, land_a, i)
+        sums.ready(i)
     span = rows_of(place.rank, rows)
 
     def use_own(cols, y):
         h1_ref[:, cols] = h_ref[:, cols].astype(F32) + y
 
     products(lambda: o_ref[span, :], wo, width, 512, True, use_own)
+    sums.forward()
     tick()
-    for copy in sums:
-        copy.wait_recv()
-    h1 = landed_sum(h1_ref[...], land_a)
+    h1 = sums.result(h1_ref[...])
     h1_ref[...] = h1
     land_n[place.rank] = norm_rows(h1, gain_ref[...])
-    gather = spread(net, land_n)
+    gather = Spread(net, land_n)
     tick()
     load_gate.wait()
     load_up.wait()
@@ -513,11 +543,10 @@
 
     span = inner_block(place.rank)
     tick()
-    second = []
-    for i, (_, rank) in enumerate(peers):
-        gather[i].wait_recv()
+    second = Sum(net, out_b, land_b)
+    for i, rank in gather.arrivals():
         span = inner_block(rank)
-        if i == 0:
+        if i == 1:
             down.done()
             keep_down = net.here(wd_blocks, wd_out)
 
@@ -525,7 +554,7 @@
             out_b[i, :, cols] = y.astype(BF16)
 
         products(lambda: u_ref[span, :], wd, width, 512, False, use)
-        second.append(push(net, out_b, land_b, i))
+        second.ready(i)
         tick()
     keep = net.here(land_n, ng_hbm)
     span = rows_of(place.rank, rows)
@@ -534,16 +563,14 @@
         hn_ref[:, cols] = h1_ref[:, cols] + y
 
     products(lambda: u_ref[span, :], wd, width, 512, False, use_down)
-    for copy in second:
-        copy.wait_recv()
-    hn = landed_sum(hn_ref[...], land_b)
+    second.forward()
+    hn = second.result(hn_ref[...])
     hn_ref[...] = hn
     if more:
         land_q[place.rank] = norm_rows(hn, gain_next[...])
-        third = spread(net, land_q)
+        third = Spread(net, land_q)
         tick()
-        for copy in third:
-            copy.wait_recv()
+        for _ in third.arrivals():
             tick()
         keep_next = net.here(land_q, nn_hbm)
         keep_next.wait()
@@ -581,7 +608,7 @@
     if not first:
         wq, out_a, land_a = refs.take(3)
     if last:
-        gnew_ref, gains_all, gains_part = refs.take(3)
+        gnew_ref, gsend_ref, gains_all, gains_part = refs.take(4)
         gains_scratch = refs.take(5)
     if not last:
         wd, wgu, wo, land_g, out_b, land_b, land_h = refs.take(7)
@@ -640,7 +667,7 @@
     if not first:
         load_q.wait()
         width = ghin_ref.shape[1]
-        total = [None] * 3
+        total = Sum(net, out_a, land_a)
         for i in (2, 0, 1):
             span = rows_of(peers[i][1], rows)
 
@@ -648,21 +675,20 @@
                 out_a[i, :, cols] = y.astype(BF16)
 
             products(lambda: dqkv_ref[span, :], wq, width, 512, True, use)
-            total[i] = push(net, out_a, land_a, i)
+            total.ready(i)
 
         def use_own(cols, y):
             gnew_ref[:, cols] = y
 
         products(lambda: dqkv_ref[own, :], wq, width, 512, True, use_own)
+        total.forward()
         tick()
-        for copy in total:
-            copy.wait_recv()
-        dn = landed_sum(gnew_ref[...], land_a)
+        dn = total.result(gnew_ref[...])
         back, ggain = norm_rows_back(hin_ref[...].astype(F32), gainin_ref[...], dn)
         gnew_ref[...] = ghin_ref[...] + back
         if last:
             finish_last(
-                place, net, jobs, gnew_ref, ggain, other_gains, gains_all, gains_part, gains_scratch,
+                place, net, jobs, gnew_ref, gsend_ref, ggain, other_gains, gains_all, gains_part, gains_scratch,
                 gains_out, swap_dst,
             )
             return
@@ -670,7 +696,7 @@
         g_ref = gnew_ref
     width = g_ref.shape[1]
     land_g[place.rank] = g_ref[...].astype(BF16)
-    gather = spread(net, land_g)
+    gather = Spread(net, land_g)
     tick()
     load_down.wait()
     load_gate.wait()
@@ -700,27 +726,25 @@
 
     products(lambda: dgu_ref[span, :], wgu, width, 512, True, use_mid)
     tick()
-    second = []
-    for i, (_, rank) in enumerate(peers):
-        gather[i].wait_recv()
+    second = Sum(net, out_b, land_b)
+    for i, rank in gather.arrivals():
         span = inner_block(rank)
 
         def use(cols, y, i=i):
             out_b[i, :, cols] = y.astype(BF16)
 
         products(lambda: dgu_ref[span, :], wgu, width, 512, True, use)
-        second.append(push(net, out_b, land_b, i))
+        second.ready(i)
         tick()
     keep = net.here(land_g, gbg_hbm)
-    for copy in second:
-        copy.wait_recv()
-    dn = landed_sum(gh_ref[...], land_b)
+    second.forward()
+    dn = second.result(gh_ref[...])
     back, ggain = norm_rows_back(h1_ref[...], gain_ref[...], dn)
     gh = g_ref[...].astype(F32) + back
     gh_ref[...] = gh
     gg_ref[...] = ggain
     land_h[place.rank] = gh.astype(BF16)
-    third = spread(net, land_h)
+    third = Spread(net, land_h)
     tick()
     load_out.wait()
 
@@ -733,9 +757,8 @@
         products(lambda: land_h[rank], wo, wo.shape[1], wo.shape[1], False, use)
 
     out_block(place.rank)
-    for i, (_, rank) in enumerate(peers):
+    for _, rank in third.arrivals():
         tick()
-        third[i].wait_recv()
         out_block(rank)
     keep_h = net.here(land_h, ghg_hbm)
     tick.rest()
@@ -746,8 +769,9 @@
     net.finish()
 
 
-def finish_last(place, net, jobs, gnew_ref, ggain, other_gains, gains_all, gains_part, scratch, gains_out, swap_dst):
-    swap = Swap(net, gnew_ref, swap_dst)
+def finish_last(place, net, jobs, gnew_ref, gsend_ref, ggain, other_gains, gains_all, gains_part, scratch, gains_out, swap_dst):
+    gsend_ref[...] = gnew_ref[...].astype(BF16)
+    swap = Swap(net, gsend_ref, swap_dst)
     swap.start()
     gains_all[...] = other_gains[...]
     gains_all[0:1, :] = ggain
@@ -992,13 +1016,14 @@
     elif not last:
         outs, out_specs = [like((rows, width), F32), like((1, width), F32)], [VM, VM]
     else:
-        outs, out_specs = [like((rows, width), F32), like((16, GAIN_COLS), F32)], [AN, VM]
+        outs, out_specs = [like((rows, width)), like((16, GAIN_COLS), F32)], [AN, VM]
     if not first:
         scratch += [pltpu.VMEM((width, start[0].shape[1]), BF16), three, three]
     if last:
         gains_shape = full_shape(count, (16, GAIN_COLS))
         scratch += [
             pltpu.VMEM((rows, width), F32),
+            pltpu.VMEM((rows, width), BF16),
             pltpu.VMEM((16, width), F32),
             pltpu.VMEM(gains_shape, BF16),
         ]
@@ -1079,7 +1104,7 @@
             g = ahead
 
     shape7 = lambda value: value.reshape(count, 2, 2, 2, 2, -1, value.shape[-1])
-    start, parts = (g, h), []
+    start, parts = (g, h.astype(BF16)), []
     grads = [None] * LAYERS
     gain_grads = [None] * (2 * LAYERS)
     for layer in reversed(range(LAYERS)):
@@ -1109,7 +1134,7 @@
     stacked = [unpack_grads(q, o, gate, up, count) for _, gate, up, o, q in grads]
     s_qkv, s_out, s_gu = (jnp.stack([s[i] for s in stacked]) for i in range(3))
     s_down = jnp.stack([g[0] for g in grads])
-    return (out_act, grad_tokens, s_qkv, s_out, s_gu, s_down, grad_gains)
+    return (out_act.astype(F32), grad_tokens.astype(F32), s_qkv, s_out, s_gu, s_down, grad_gains)
 
 
 def solution(mesh):

time: 834 us -> 781 us (0.936)
  Pallas kernels: 682 us -> 632 us
    pallas_call x3, Pallas kernels: 371 us -> 329 us  [call_back(): pl.pallas_call(functools.partial(back_kernel, count, rows, first, last, n...]
where the time goes in v3:
time: 781 us; the launch traced here: 774 us
  Pallas kernels  632 us (81%)
  matrix products  71.4 us (9%)
  local copies, waits for them, and re-layouts  39.7 us (5%)
  other arithmetic  29.1 us (4%)
    pallas_call x3, Pallas kernels, call_back(): pl.pallas_call(functools.partial(back_kernel, count, rows, first, last, n...  329 us
    pallas_call x2, Pallas kernels, call_body(): pl.pallas_call(functools.partial(body_kernel, count, rows, more), out_sha...  213 us
    pallas_call x1, Pallas kernels, call_start(): pl.pallas_call(functools.partial(start_kernel, count, n, ahead), out_shap...  89.8 us
    dot_general x10, matrix products, dot_t(): lax.dot_general(a, b, (((0,), (0,)), ((), ())), preferred_element_type=F32)  34.5 us

profile of v3, /device:TPU:0, one launch (start us, length us, event | category | flops | bytes accessed | tf_op | source)
XLA Modules:
  0.0 774.0 jit_solution(5422344300352194570)
XLA Ops:
  0.6 1.1 slice_bitcast_fusion.4
  5.1 2.9 fusion.35
  9.6 1.0 squeeze.36.refs_3_
  13.2 1.0 squeeze.40.refs_7_
  15.2 89.8 %start.1 = (bf16[4,128,1536]{2,1,0:T(8,128)(2,1)}, bf16[2,2,2,2,2,48,896]{6,5,4,3,2,1,0:T(8,128)(2,1)}, bf16[2,2,2,2,2,48,384]{6,5,4,3,2,1,0:T(8,128)(2,1)}, bf1...) custom-call(bf16[128,1536]{1,0:T(8,128)(2,1)} %refs_0_.1, ...), custom_call_target="tpu_custom_call" | custom-call | tf_op jit(solution)/shard_map/start/pallas_call | solution.py:939
  105.0 1.2 slice_convert_fusion.2
  108.9 1.4 fusion.12
  110.3 1.1 copy-done.4
  114.1 2.9 fusion.10
  117.0 3.2 exponential_reduce_fusion.1
  121.2 3.6 convolution_convert_fusion.11
  127.4 126.4 %body_more.1 = (f32[128,1536]{1,0:T(8,128)}, f32[128,1536]{1,0:T(8,128)}, f32[512,1024]{1,0:T(8,128)}, f32[512,1024]{1,0:T(8,128)}, bf16[512,1024]{1,0:T(8,128)(...) custom-call(bf16[512,384]{1,0:T(8,128)(2,1)} %copy.77.refs_0_, ...), custom_call_target="tpu_custom_call" | custom-call | tf_op jit(solution)/shard_map/body_more/pallas_call | solution.py:965
  253.9 3.5 fusion.42
  257.4 1.1 copy-done.6
  259.9 2.9 fusion.11
  262.9 3.2 exponential_reduce_fusion
  266.5 3.5 convolution_convert_fusion.10
  271.7 86.7 %body.1 = (f32[128,1536]{1,0:T(8,128)}, f32[128,1536]{1,0:T(8,128)}, f32[512,1024]{1,0:T(8,128)}, f32[512,1024]{1,0:T(8,128)}, bf16[512,1024]{1,0:T(8,128)(2,1)}...) custom-call(bf16[512,384]{1,0:T(8,128)(2,1)} %copy.82.refs_0_, ...), custom_call_target="tpu_custom_call" | custom-call | tf_op jit(solution)/shard_map/body/pallas_call | solution.py:965
  358.4 1.9 convert_element_type.258.refs_1_
  360.3 85.7 %back_first.1 = (bf16[128,1536]{1,0:T(8,128)(2,1)}, bf16[4,128,1536]{2,1,0:T(8,128)(2,1)}, bf16[512,2048]{1,0:T(8,128)(2,1)}, f32[128,1536]{1,0:T(8,128)}, f32[1...) custom-call(bf16[128,1536]{1,0:T(8,128)(2,1)} %get-tuple-element.77.refs_0_, ...), custom_call_target="tpu_custom_call" | custom-call | tf_op jit(solution)/shard_map/back_first/pallas_call | solution.py:1050
  446.1 1.2 copy.83
  447.4 3.8 fusion.5
  452.8 1.8 convolution_bitcast_fusion.3
  454.8 3.5 fusion.14
  458.7 4.6 convolution_convert_fusion.7
  463.2 2.0 convolution_convert_fusion.9
  465.3 3.5 convolution_convert_fusion.3
  468.8 3.7 convolution_convert_fusion.4
  472.5 3.5 convolution_convert_fusion.5
  476.0 121.2 %back_mid.1 = (f32[128,1536]{1,0:T(8,128)}, f32[1,1536]{1,0:T(1,128)}, bf16[4,128,1536]{2,1,0:T(8,128)(2,1)}, bf16[512,2048]{1,0:T(8,128)(2,1)}, f32[128,1536]{1...) custom-call(bf16[512,768]{1,0:T(8,128)(2,1)} %copy-done.2, ...), custom_call_target="tpu_custom_call" | custom-call | tf_op jit(solution)/shard_map/back_mid/pallas_call | solution.py:1050
  597.3 1.2 copy.90
  598.6 3.9 fusion.2
  603.9 1.9 copy.94
  605.8 1.8 convolution_bitcast_fusion.1
  607.8 3.5 fusion.15
  611.6 4.6 convolution_convert_fusion.6
  616.3 2.0 convolution_convert_fusion.8
  618.3 3.5 convolution_convert_fusion
  621.8 3.5 convolution_convert_fusion.1
  625.3 3.5 convolution_convert_fusion.2
  629.6 122.0 %back_last.1 = (bf16[128,1536]{1,0:T(8,128)(2,1)}, f32[16,128]{1,0:T(8,128)}, f32[128,1536]{1,0:T(8,128)}, f32[4,48,1024]{2,1,0:T(8,128)}, f32[4,48,1024]{2,1,0:...) custom-call(bf16[512,768]{1,0:T(8,128)(2,1)} %copy-done.3, bf16[1536,896]{1,0:T(8,128)(2,1)} %bitcast.298, ...), custom_call_target="tpu_custom_call" | custom-call | tf_op jit(solution)/shard_map/back_last/pallas_call | solution.py:1050
  751.6 2.5 pad_maximum_fusion.1
  756.6 1.5 maximum_bitcast_fusion
  759.5 1.8 reshape.442
  761.9 1.5 maximum_bitcast_fusion.1
  763.5 3.3 pad_maximum_fusion
  769.6 1.1 pad_maximum_fusion.2
  771.6 1.3 slice.239
  (222 shorter events, 34.7 us)
Async XLA Ops:
  0.6 2.7 copy-start.45
  1.7 2.6 copy-start.37
  105.0 2.1 copy-start
  107.1 1.8 copy-start.1
  108.9 1.4 copy-start.12
  113.3 3.7 copy-start.27
  113.3 3.7 copy-start.29
  117.0 3.2 copy-start.5
  121.2 5.3 copy-start.17
  124.8 129.1 %copy-start.8 = (bf16[2,96,2,512]{3,1,2,0:T(8,128)(2,1)}, bf16[2,96,2,512]{3,1,2,0:T(8,128)(2,1)S(1)}, u32[]{:S(2)}) copy-start(bf16[2,96,2,512]{3,1,2,0:T(8,128)(2,1)S(1)} %convolution_convert_fusion.11) | copy-start | bytes 1179652
  259.0 3.9 copy-start.25
  259.0 3.9 copy-start.26
  259.9 3.0 copy-start.31
  259.9 3.0 copy-start.33
  262.9 3.2 copy-start.7
  266.4 3.6 copy-start.40
  266.4 4.5 copy-start.18
  270.0 177.3 %copy-start.10 = (bf16[2,96,2,512]{3,1,2,0:T(8,128)(2,1)}, bf16[2,96,2,512]{3,1,2,0:T(8,128)(2,1)S(1)}, u32[]{:S(2)}) copy-start(bf16[2,96,2,512]{3,1,2,0:T(8,128)(2,1)S(1)} %convolution_convert_fusion.10) | copy-start | bytes 1179652
  360.3 87.1 %copy-start.41 = (bf16[512,192]{0,1:T(8,128)(2,1)S(1)}, bf16[512,192]{0,1:T(8,128)(2,1)}, u32[]{:S(2)}) copy-start(bf16[512,192]{0,1:T(8,128)(2,1)} %copy-done.40) | copy-start | bytes 589828
  447.4 3.8 copy-start.32
  447.4 3.8 copy-start.34
  454.8 3.6 copy-start.14
  458.6 4.6 copy-start.2
  458.6 4.6 copy-start.11
  458.6 4.6 copy-start.53
  458.6 6.7 copy-start.51
  463.2 2.1 copy-start.47
  468.8 3.7 copy-start.52
  468.8 3.7 copy-start.55
  476.0 122.4 %copy-start.9 = (bf16[2,96,2,512]{3,1,2,0:T(8,128)(2,1)S(1)}, bf16[2,96,2,512]{3,1,2,0:T(8,128)(2,1)}, u32[]{:S(2)}) copy-start(bf16[2,96,2,512]{3,1,2,0:T(8,128)(2,1)} %copy-done.8) | copy-start | bytes 1179652
  598.6 3.9 copy-start.28
  598.6 3.9 copy-start.30
  607.8 3.6 copy-start.13
  611.6 4.7 copy-start.3
  611.6 4.6 copy-start.50
  611.6 6.7 copy-start.48
  616.3 2.0 copy-start.46
  621.8 3.5 copy-start.49
  621.8 3.5 copy-start.54
  625.3 3.5 copy-start.42
  625.3 3.5 copy-start.43
  625.3 3.5 copy-start.44
  629.6 122.0 %copy-start.22 = (f32[128,1536]{1,0:T(8,128)S(1)}, f32[128,1536]{1,0:T(8,128)}, u32[]{:S(2)}) copy-start(f32[128,1536]{1,0:T(8,128)} %get-tuple-element.115) | copy-start | bytes 2359300
  751.6 2.5 copy-start.21
  756.0 2.2 copy-start.19
  763.4 3.3 copy-start.39
  763.4 3.3 copy-start.38
  769.5 3.4 copy-start.35
  (10 other events, 11.4 us)

commit v4 on v3

--- a/solution.py
+++ b/solution.py
@@ -2,6 +2,7 @@
 
 import jax
 import jax.numpy as jnp
+import numpy as np
 from jax import lax
 from jax.experimental import pallas as pl
 from jax.experimental.pallas import tpu as pltpu
@@ -348,14 +349,15 @@
 
 
 def products(x, w_ref, count, tile, transposed, use):
-    @pl.loop(0, count // tile)
-    def _(j):
-        cols = pl.ds(pl.multiple_of(j * tile, tile), tile)
+    def part(cols):
         if transposed:
             w, dims = w_ref[cols, :], (((1,), (1,)), ((), ()))
         else:
             w, dims = w_ref[:, cols], (((1,), (0,)), ((), ()))
         use(cols, lax.dot_general(x(), w, dims, preferred_element_type=F32))
+
+    for j in range(count // tile):
+        part(pl.ds(j * tile, tile))
 
 
 def norm_rows(h, gain):
@@ -398,47 +400,147 @@
             self()
 
 
-def start_kernel(count, n, ahead, *refs):
+def wide_tables(length):
+    steps = np.arange(HEAD_DIM // 2, dtype=np.float32)
+    inverse = np.exp(steps * np.float32(-2.0 * np.log(ROPE_BASE) / HEAD_DIM)).astype(np.float32)
+    angles = np.arange(length, dtype=np.float32)[:, None] * inverse[None, :]
+    cosine, sine = np.cos(angles), np.sin(angles)
+    turned = (HEADS + KV_HEADS) // RANKS
+    still = KV_HEADS // RANKS * HEAD_DIM
+    cos_all = np.concatenate([cosine] * (2 * turned) + [np.ones((length, still))], axis=1)
+    sin_all = np.concatenate([-sine, sine] * turned + [np.zeros((length, still))], axis=1)
+    return jnp.asarray(cos_all, F32), jnp.asarray(sin_all, F32)
+
+
+def turn(values, cosine, sine):
+    cols = values.shape[1]
+    half = HEAD_DIM // 2
+    lane = lax.broadcasted_iota(jnp.int32, values.shape, 1)
+    other = jnp.where(
+        lax.rem(lane, HEAD_DIM) < half,
+        pltpu.roll(values, cols - half, 1),
+        pltpu.roll(values, half, 1),
+    )
+    return values * cosine + other * sine
+
+
+def head_window(values, h):
+    offset = HEAD_DIM * h
+    start = offset // 128 * 128
+    size = 128 if offset - start + HEAD_DIM <= 128 else 256
+    window = values[:, start : start + size]
+    if offset > start:
+        window = pltpu.roll(window, size - (offset - start), 1)
+    window = window[:, :128]
+    lane = lax.broadcasted_iota(jnp.int32, window.shape, 1)
+    return jnp.where(lane < HEAD_DIM, window, 0.0)
+
+
+def heads_joined(parts):
+    rows = parts[0].shape[0]
+    columns = [jnp.zeros((rows, 128), F32) for _ in range(len(parts) * HEAD_DIM // 128 + 1)]
+    for h, part in enumerate(parts):
+        offset = HEAD_DIM * h
+        first = offset // 128
+        shift = offset - first * 128
+        if shift == 0:
+            columns[first] = columns[first] + part
+            continue
+        double = jnp.concatenate([part, jnp.zeros((rows, 128), F32)], axis=1)
+        double = pltpu.roll(double, shift, 1)
+        columns[first] = columns[first] + double[:, :128]
+        columns[first + 1] = columns[first + 1] + double[:, 128:]
+    return jnp.concatenate(columns[:-1], axis=1)
+
+
+def project_heads(rows, n1, wq, cos_ref, sin_ref, qkv_ref, heads):
+    count = heads.shape[0]
+
+    @pl.loop(0, RANKS)
+    def _(b):
+        span = rows_of(b, rows)
+        y = jnp.dot(n1[b], wq[...], preferred_element_type=F32)
+        y = turn(y, cos_ref[span, :], sin_ref[span, :])
+        qkv_ref[span, :] = y.astype(BF16)
+        for h in range(count):
+            heads[h, span, :] = head_window(y, h).astype(BF16)
+
+
+def causal_scores(rows, rank, query, key):
+    scores = lax.dot_general(query, key, (((1,), (1,)), ((), ())), preferred_element_type=F32)
+    row = lax.broadcasted_iota(jnp.int32, scores.shape, 0) + rank * rows
+    col = lax.broadcasted_iota(jnp.int32, scores.shape, 1)
+    return jnp.where(col <= row, scores * HEAD_DIM ** (-0.5), MASKED)
+
+
+def attend_rows(rows, rank, heads, o_ref, lse_ref):
+    span = rows_of(rank, rows)
+    queries = HEADS // RANKS
+    pairs = KV_HEADS // RANKS
+    groups = HEADS // KV_HEADS
+    mixed = []
+    lane = lax.broadcasted_iota(jnp.int32, (rows, 128), 1)
+    lse_all = jnp.zeros((rows, 128), F32)
+    for h in range(queries):
+        kv = h // groups
+        scores = causal_scores(rows, rank, heads[h, span, :], heads[queries + kv])
+        highest = jnp.max(scores, axis=-1, keepdims=True)
+        weights = jnp.exp(scores - highest)
+        total = jnp.sum(weights, axis=-1, keepdims=True)
+        lse = highest + jnp.log(total)
+        lse_all = jnp.where(lane == h, lse, lse_all)
+        weights = (weights * (1.0 / total)).astype(BF16)
+        mixed.append(
+            jnp.dot(weights, heads[queries + pairs + kv], preferred_element_type=F32)
+        )
+    lse_ref[span, :] = lse_all
+    o_ref[span, :] = heads_joined(mixed).astype(BF16)
+
+
+def start_kernel(count, n, ahead, n_down, *refs):
     refs = Refs(refs)
     (tokens,) = refs.take(1)
-    pieces, later = refs.take(n), refs.take(ahead)
+    pieces, later, downs = refs.take(n), refs.take(ahead), refs.take(n_down)
     (all_tokens,) = refs.take(1)
-    full, blocks_later = refs.take(n), refs.take(ahead)
+    full, blocks_later, downs_full = refs.take(n), refs.take(ahead), refs.take(n_down)
     (land,) = refs.take(1)
     blocks = refs.take(n)
     send, recv, local = refs.take(3)
     place = Place(count)
     net = Net(place, send, recv, local)
     shares = [Share(net, pieces[i], blocks[i]) for i in range(n)]
+    shares_later = [Share(net, later[i], blocks_later[i]) for i in range(ahead)]
     gathers = [Gather(net, blocks[i], full[i]) for i in range(n)]
-    shares_later = [Share(net, later[i], blocks_later[i]) for i in range(ahead)]
+    gathers += [Gather(net, downs[i], downs_full[i], ranks=False) for i in range(n_down)]
     swap = Swap(net, tokens, land.at[place.zh * 2 + place.zl])
     place.greet(True, True)
     shares[0].start()
     swap.start()
-    shares[1].start()
-    shares[0].wait()
-    gathers[0].begin()
+    for share in shares[1:]:
+        share.start()
+    for i in range(2):
+        shares[i].wait()
+        gathers[i].begin()
     swap.wait()
     spreads = Spread(net, land)
-    shares[1].wait()
-    gathers[1].begin()
-    for share in shares[2:]:
+    for i in range(2, len(gathers)):
+        if i < n:
+            shares[i].wait()
+        gathers[i].begin()
+    arrivals = spreads.arrivals()
+    next(arrivals)
+    for share in shares_later:
         share.start()
     gathers[0].middle()
-    for i in range(2, n):
-        shares[i].wait()
-        gathers[i].begin()
-        gathers[i - 1].middle()
-        gathers[i - 2].final()
-        if i == 2:
-            spreads.wait()
-            keep = net.here(land, all_tokens)
-            for share in shares_later:
-                share.start()
-    gathers[n - 1].middle()
-    gathers[n - 2].final()
-    gathers[n - 1].final()
+    gathers[1].middle()
+    for _ in arrivals:
+        pass
+    keep = net.here(land, all_tokens)
+    gathers[0].final()
+    for i in range(2, len(gathers)):
+        gathers[i].middle()
+        gathers[i - 1].final()
+    gathers[-1].final()
     for gather in gathers:
         gather.done()
     for share in shares_later:
@@ -447,75 +549,85 @@
     net.finish()
 
 
-def body_kernel(count, rows, more, *refs):
+def body_kernel(count, rows, late, n_next, plan, *refs):
     refs = Refs(refs)
-    o_ref, h_ref, gain_ref, wo_hbm, wgate_hbm, wup_hbm, down_hbm = refs.take(7)
-    if more:
+    n1_hbm, wq_hbm, cos_ref, sin_ref, h_ref, gain_ref, wo_hbm = refs.take(7)
+    inner_hbm = refs.take(3)
+    if n_next:
         (gain_next,) = refs.take(1)
-        blocks = refs.take(more)
+        blocks = refs.take(n_next)
     else:
         (swap_src,) = refs.take(1)
-    h1_ref, hn_ref, gate_ref, up_ref, u_ref, ng_hbm, wd_out = refs.take(7)
-    if more:
+    qkv_ref, o_ref, lse_ref, h1_ref, hn_ref, gate_ref, up_ref, u_ref, ng_hbm = refs.take(9)
+    late_out = [refs.take(1)[0] if late[i] else None for i in range(3)]
+    if n_next:
         (nn_hbm,) = refs.take(1)
-        full = refs.take(more)
+        full = refs.take(n_next)
     else:
         (swap_dst,) = refs.take(1)
-    wo, wgu, wd_blocks, out_a, land_a, land_n, out_b, land_b = refs.take(8)
-    if more:
+    n1, wq, heads, wo = refs.take(4)
+    inner = refs.take(3)
+    out_a, land_a, land_n, out_b, land_b = refs.take(5)
+    if n_next:
         (land_q,) = refs.take(1)
     send, recv, local = refs.take(3)
 
     place = Place(count)
     net = Net(place, send, recv, local)
     width = h_ref.shape[1]
-    hidden = wgate_hbm.shape[1]
+    hidden = u_ref.shape[1]
+    load_q = net.here(wq_hbm.at[:, pl.ds(0, wq.shape[1])], wq)
+    load_n = net.here(n1_hbm, n1)
     load_out = net.here(wo_hbm, wo)
-    load_gate = net.here(wgate_hbm, wgu.at[:, pl.ds(0, hidden)])
-    load_up = net.here(wup_hbm, wgu.at[:, pl.ds(hidden, hidden)])
+    jobs = {}
+    loads, weights = [], []
+    for i in range(3):
+        if late[i]:
+            jobs[("gate", "up", "down")[i]] = Gather(net, inner_hbm[i], inner[i], ranks=i < 2)
+            loads.append(None)
+        else:
+            loads.append(net.here(inner_hbm[i], inner[i]))
+        weights.append(inner[i].reshape((hidden, width) if i == 2 else (width, hidden)) if late[i] else inner[i])
+    wg, wu, wd = weights
+    for i in range(n_next):
+        jobs[i] = Gather(net, blocks[i], full[i])
+    if not n_next:
+        jobs["swap"] = Swap(net, swap_src, swap_dst)
     peers = place.peers
-    place.greet(True, not more)
-    down = Gather(net, down_hbm, wd_blocks, ranks=False)
-    wd = wd_blocks.reshape(hidden, width)
-    jobs = [Gather(net, blocks[i], full[i]) for i in range(more)]
-    if more:
-        j = jobs
-        tick = Ticks(
-            [
-                [down.begin],
-                [j[0].begin],
-                [down.middle],
-                [j[1].begin, down.final],
-                [j[0].middle, j[2].begin],
-                [j[0].final, j[1].middle],
-                [j[1].final],
-                [j[2].middle, j[3].begin],
-                [j[2].final],
-                [j[3].middle],
-                [j[3].final],
-            ]
-        )
-    else:
-        swap = Swap(net, swap_src, swap_dst)
-        tick = Ticks([[down.begin], [], [down.middle], [swap.start, down.final]])
+    place.greet(True, not n_next)
+    keeps = []
+
+    def ready(i):
+        if late[i]:
+            jobs[("gate", "up", "down")[i]].done()
+            keeps.append(net.here(inner[i], late_out[i]))
+        else:
+            loads[i].wait()
+
+    tick = Ticks(plan(jobs))
     tick()
+
+    load_q.wait()
+    load_n.wait()
+    project_heads(rows, n1, wq, cos_ref, sin_ref, qkv_ref, heads)
     load_out.wait()
-
     sums = Sum(net, out_a, land_a)
     for i in (2, 0, 1):
+        attend_rows(rows, peers[i][1], heads, o_ref, lse_ref)
         span = rows_of(peers[i][1], rows)
 
         def use(cols, y, i=i):
             out_a[i, :, cols] = y.astype(BF16)
 
-        products(lambda: o_ref[span, :], wo, width, 512, True, use)
+        products(lambda: o_ref[span, :], wo, width, width, True, use)
         sums.ready(i)
+    attend_rows(rows, place.rank, heads, o_ref, lse_ref)
     span = rows_of(place.rank, rows)
 
     def use_own(cols, y):
         h1_ref[:, cols] = h_ref[:, cols].astype(F32) + y
 
-    products(lambda: o_ref[span, :], wo, width, 512, True, use_own)
+    products(lambda: o_ref[span, :], wo, width, width, True, use_own)
     sums.forward()
     tick()
     h1 = sums.result(h1_ref[...])
@@ -523,37 +635,33 @@
     land_n[place.rank] = norm_rows(h1, gain_ref[...])
     gather = Spread(net, land_n)
     tick()
-    load_gate.wait()
-    load_up.wait()
+    ready(0)
+    ready(1)
 
     def inner_block(rank):
         span = rows_of(rank, rows)
 
-        @pl.loop(0, hidden // 256)
-        def _(j):
-            cols = pl.ds(pl.multiple_of(j * 256, 256), 256)
-            ups = pl.ds(pl.multiple_of(j * 256 + hidden, 256), 256)
-            gate = jnp.dot(land_n[rank], wgu[:, cols], preferred_element_type=F32)
-            up = jnp.dot(land_n[rank], wgu[:, ups], preferred_element_type=F32)
-            gate_ref[span, cols] = gate
-            up_ref[span, cols] = up
-            u_ref[span, cols] = (gate / (1.0 + jnp.exp(-gate)) * up).astype(BF16)
+        gate = jnp.dot(land_n[rank], wg[...], preferred_element_type=F32)
+        up = jnp.dot(land_n[rank], wu[...], preferred_element_type=F32)
+        gate_ref[span, :] = gate
+        up_ref[span, :] = up
+        u_ref[span, :] = (gate / (1.0 + jnp.exp(-gate)) * up).astype(BF16)
 
         return span
 
-    span = inner_block(place.rank)
+    inner_block(place.rank)
     tick()
     second = Sum(net, out_b, land_b)
     for i, rank in gather.arrivals():
         span = inner_block(rank)
         if i == 1:
-            down.done()
-            keep_down = net.here(wd_blocks, wd_out)
+            tick()
+            ready(2)
 
         def use(cols, y, i=i):
             out_b[i, :, cols] = y.astype(BF16)
 
-        products(lambda: u_ref[span, :], wd, width, 512, False, use)
+        products(lambda: u_ref[span, :], wd, width, width, False, use)
         second.ready(i)
         tick()
     keep = net.here(land_n, ng_hbm)
@@ -562,11 +670,12 @@
     def use_down(cols, y):
         hn_ref[:, cols] = h1_ref[:, cols] + y
 
-    products(lambda: u_ref[span, :], wd, width, 512, False, use_down)
+    products(lambda: u_ref[span, :], wd, width, width, False, use_down)
     second.forward()
+    tick()
     hn = second.result(hn_ref[...])
     hn_ref[...] = hn
-    if more:
+    if n_next:
         land_q[place.rank] = norm_rows(hn, gain_next[...])
         third = Spread(net, land_q)
         tick()
@@ -575,20 +684,87 @@
         keep_next = net.here(land_q, nn_hbm)
         keep_next.wait()
     tick.rest()
-    if more:
-        for job in jobs:
-            job.done()
-    else:
-        swap.wait()
+    for i in range(n_next):
+        jobs[i].done()
+    if not n_next:
+        jobs["swap"].wait()
     keep.wait()
-    keep_down.wait()
+    for copy in keeps:
+        copy.wait()
     net.finish()
+
+
+def plan_late(j):
+    gate, down = j["gate"], j["down"]
+    return [
+        [gate.begin],
+        [gate.middle, down.begin],
+        [gate.final],
+        [down.middle, j[0].begin, j[1].begin],
+        [down.final],
+        [],
+        [],
+        [j[0].middle],
+        [j[0].final, j[1].middle],
+        [j[2].begin, j[1].final],
+        [],
+        [],
+        [j[2].middle],
+        [j[2].final],
+    ]
+
+
+def plan_late_end(j):
+    up, down = j["up"], j["down"]
+    return [
+        [up.begin],
+        [up.middle, down.begin],
+        [up.final],
+        [down.middle],
+        [down.final],
+        [],
+        [],
+        [j["swap"].start],
+    ]
+
+
+def plan_early(j):
+    return [
+        [j[0].begin],
+        [j[1].begin],
+        [j[0].middle, j[1].middle, j[2].begin],
+        [],
+        [j[0].final],
+        [j[1].final],
+        [j[2].middle],
+        [],
+        [j[3].begin, j[2].final],
+        [],
+        [],
+        [],
+        [j[3].middle],
+        [j[3].final],
+    ]
+
+
+def plan_end(j):
+    down = j["down"]
+    return [
+        [down.begin],
+        [],
+        [down.middle],
+        [],
+        [down.final],
+        [],
+        [],
+        [j["swap"].start],
+    ]
 
 
 def back_kernel(count, rows, first, last, n_red, *refs):
     refs = Refs(refs)
     if first:
-        g_ref, swap_src = refs.take(2)
+        (g_ref,) = refs.take(1)
     else:
         dqkv_ref, wq_hbm, ghin_ref, hin_ref, gainin_ref = refs.take(5)
     if not last:
@@ -596,12 +772,10 @@
     else:
         (other_gains,) = refs.take(1)
     parts = refs.take(n_red)
-    if first:
-        (swap_dst,) = refs.take(1)
-    elif not last:
+    if last:
+        swap_dst, gains_out = refs.take(2)
+    elif not first:
         gnew_ref, ggin_ref = refs.take(2)
-    else:
-        swap_dst, gains_out = refs.take(2)
     if not last:
         gbg_hbm, dgu_ref, gh_ref, gg_ref, ghg_hbm, do_ref = refs.take(6)
     red_out = refs.take(n_red)
@@ -630,10 +804,9 @@
         load_gate = net.here(wgate_hbm, wgu.at[:, pl.ds(0, hidden)])
         load_up = net.here(wup_hbm, wgu.at[:, pl.ds(hidden, hidden)])
         load_out = net.here(wo_hbm, wo)
-    place.greet(n_red > 0, first or last)
+    place.greet(n_red > 0, last)
     if first:
-        swap = Swap(net, swap_src, swap_dst)
-        tick = Ticks([[swap.start]])
+        tick = Ticks([])
     elif not last:
         j = jobs
         tick = Ticks(
@@ -674,13 +847,13 @@
             def use(cols, y, i=i):
                 out_a[i, :, cols] = y.astype(BF16)
 
-            products(lambda: dqkv_ref[span, :], wq, width, 512, True, use)
+            products(lambda: dqkv_ref[span, :], wq, width, width, True, use)
             total.ready(i)
 
         def use_own(cols, y):
             gnew_ref[:, cols] = y
 
-        products(lambda: dqkv_ref[own, :], wq, width, 512, True, use_own)
+        products(lambda: dqkv_ref[own, :], wq, width, width, True, use_own)
         total.forward()
         tick()
         dn = total.result(gnew_ref[...])
@@ -705,17 +878,11 @@
     def inner_block(rank):
         span = rows_of(rank, rows)
 
-        @pl.loop(0, hidden // 256)
-        def _(j):
-            cols = pl.ds(pl.multiple_of(j * 256, 256), 256)
-            ups = pl.ds(pl.multiple_of(j * 256 + hidden, 256), 256)
-            du = lax.dot_general(
-                land_g[rank], wd[cols, :], (((1,), (1,)), ((), ())), preferred_element_type=F32
-            )
-            gate, up = gate_ref[span, cols], up_ref[span, cols]
-            sg = 1.0 / (1.0 + jnp.exp(-gate))
-            dgu_ref[span, cols] = (du * up * sg * (1.0 + gate * (1.0 - sg))).astype(BF16)
-            dgu_ref[span, ups] = (du * gate * sg).astype(BF16)
+        du = lax.dot_general(land_g[rank], wd[...], (((1,), (1,)), ((), ())), preferred_element_type=F32)
+        gate, up = gate_ref[span, :], up_ref[span, :]
+        sg = 1.0 / (1.0 + jnp.exp(-gate))
+        dgu_ref[span, pl.ds(0, hidden)] = (du * up * sg * (1.0 + gate * (1.0 - sg))).astype(BF16)
+        dgu_ref[span, pl.ds(hidden, hidden)] = (du * gate * sg).astype(BF16)
 
         return span
 
@@ -724,7 +891,7 @@
     def use_mid(cols, y):
         gh_ref[:, cols] = y
 
-    products(lambda: dgu_ref[span, :], wgu, width, 512, True, use_mid)
+    products(lambda: dgu_ref[span, :], wgu, width, width, True, use_mid)
     tick()
     second = Sum(net, out_b, land_b)
     for i, rank in gather.arrivals():
@@ -733,7 +900,7 @@
         def use(cols, y, i=i):
             out_b[i, :, cols] = y.astype(BF16)
 
-        products(lambda: dgu_ref[span, :], wgu, width, 512, True, use)
+        products(lambda: dgu_ref[span, :], wgu, width, width, True, use)
         second.ready(i)
         tick()
     keep = net.here(land_g, gbg_hbm)
@@ -764,8 +931,6 @@
     tick.rest()
     keep_h.wait()
     keep.wait()
-    if first:
-        swap.wait()
     net.finish()
 
 
@@ -869,25 +1034,16 @@
     return rotate(grads, cosine, -sine_tab)
 
 
-def attend(proj, cosine, sine_tab, causal):
-    length = proj.shape[0]
+def saved_heads(qkv, lse):
+    length = qkv.shape[0]
     kv = KV_HEADS // RANKS
     groups = HEADS // KV_HEADS
     q_cols = kv * groups * HEAD_DIM
     kv_cols = kv * HEAD_DIM
-    query = rotate(proj[:, :q_cols].reshape(length, kv * groups, HEAD_DIM), cosine, sine_tab)
-    query = query.astype(BF16).reshape(length, kv, groups, HEAD_DIM)
-    key = rotate(proj[:, q_cols : q_cols + kv_cols].reshape(length, kv, HEAD_DIM), cosine, sine_tab)
-    key = key.astype(BF16)
-    value = proj[:, q_cols + kv_cols :].astype(BF16).reshape(length, kv, HEAD_DIM)
-    scale = HEAD_DIM ** (-0.5)
-    scores = jnp.einsum("qkgd,skd->kgqs", query, key, preferred_element_type=F32) * scale
-    scores = jnp.where(causal[None, None], scores, MASKED)
-    highest = jnp.max(scores, axis=-1, keepdims=True)
-    lse = highest + jnp.log(jnp.sum(jnp.exp(scores - highest), axis=-1, keepdims=True))
-    weights = jnp.exp(scores - lse).astype(BF16)
-    mixed = jnp.einsum("kgqs,skd->qkgd", weights, value, preferred_element_type=F32).astype(BF16)
-    return mixed.reshape(length, q_cols), (query, key, value, lse)
+    query = qkv[:, :q_cols].reshape(length, kv, groups, HEAD_DIM)
+    key = qkv[:, q_cols : q_cols + kv_cols].reshape(length, kv, HEAD_DIM)
+    value = qkv[:, q_cols + kv_cols :].reshape(length, kv, HEAD_DIM)
+    return query, key, value, lse[:, : kv * groups].T.reshape(kv, groups, length, 1)
 
 
 def attend_back(saved, mixed, grad_mixed, cosine, sine_tab, causal):
@@ -933,90 +1089,106 @@
     return (count, 2, 2, 2, 2) + tuple(tail)
 
 
-def call_start(count, tokens, pieces, later):
+def call_start(count, tokens, pieces, later, downs):
     rows, width = tokens.shape
-    n, ahead = len(pieces), len(later)
+    n, ahead, n_down = len(pieces), len(later), len(downs)
+    outs = [like((RANKS, rows, width))]
+    outs += [like(full_shape(count, p.shape[1:])) for p in pieces]
+    outs += [like((2, 2) + p.shape[1:]) for p in later]
+    outs += [like((count, 2, 2) + d.shape) for d in downs]
     got = pl.pallas_call(
-        functools.partial(start_kernel, count, n, ahead),
-        out_shape=[like((RANKS, rows, width))]
-        + [like(full_shape(count, p.shape[1:])) for p in pieces]
-        + [like((2, 2) + p.shape[1:]) for p in later],
-        in_specs=[AN] * (1 + n + ahead),
-        out_specs=[AN] * (1 + n + ahead),
+        functools.partial(start_kernel, count, n, ahead, n_down),
+        out_shape=outs,
+        in_specs=[AN] * len(outs),
+        out_specs=[AN] * len(outs),
         scratch_shapes=[pltpu.VMEM((RANKS, rows, width), BF16)]
         + [pltpu.VMEM((2, 2) + p.shape[1:], BF16) for p in pieces]
         + sems(count),
         compiler_params=params(1),
         name="start",
-    )(tokens, *pieces, *later)
-    return got[0], [f.reshape(-1, f.shape[-1]) for f in got[1 : n + 1]], got[n + 1 :]
-
-
-def call_body(count, o, h, gain, weights, down, extra):
+    )(tokens, *pieces, *later, *downs)
+    cut = n + 1 + ahead
+    return got[0], [flat(f) for f in got[1 : n + 1]], got[n + 1 : cut], [flat(d) for d in got[cut:]]
+
+
+def flat(value):
+    return value.reshape(-1, value.shape[-1])
+
+
+def call_body(count, n1, wq, tables, h, gain, wo, inner, late, plan, gain_next=None, blocks=(), swap=None):
     rows, width = h.shape
     tall = RANKS * rows
-    wo, wgate, wup = weights
-    hidden = wgate.shape[1]
-    more = len(extra) - 1
-    blocks = extra[1:]
+    hidden = inner[0].shape[-1]
+    n_next = len(blocks)
+    heads = (HEADS + 2 * KV_HEADS) // RANKS
+    cols = heads * HEAD_DIM
+    o_cols = HEADS // RANKS * HEAD_DIM
     three = pltpu.VMEM((3, rows, width), BF16)
     four = pltpu.VMEM((RANKS, rows, width), BF16)
-    wd_shape = (count, 2, 2) + down.shape
+    shapes = []
+    for i in range(3):
+        shape = inner[i].shape
+        if late[i]:
+            shape = full_shape(count, shape[2:]) if i < 2 else (count, 2, 2) + shape
+        shapes.append(shape)
+    outs = [
+        like((tall, cols)),
+        like((tall, o_cols)),
+        like((tall, 128), F32),
+        like((rows, width), F32),
+        like((rows, width), F32),
+        like((tall, hidden), F32),
+        like((tall, hidden), F32),
+        like((tall, hidden)),
+        like((RANKS, rows, width)),
+    ]
+    n_state = len(outs)
+    outs += [like(shapes[i]) for i in range(3) if late[i]]
+    if n_next:
+        outs += [like((RANKS, rows, width))] + [like(full_shape(count, b.shape[2:])) for b in blocks]
+        extra = (gain_next, *blocks)
+    else:
+        outs += [like(swap.shape)]
+        extra = (swap,)
     got = pl.pallas_call(
-        functools.partial(body_kernel, count, rows, more),
-        out_shape=[
-            like((rows, width), F32),
-            like((rows, width), F32),
-            like((tall, hidden), F32),
-            like((tall, hidden), F32),
-            like((tall, hidden)),
-            like((RANKS, rows, width)),
-            like(wd_shape),
+        functools.partial(body_kernel, count, rows, late, n_next, plan),
+        out_shape=outs,
+        in_specs=[AN, AN, VM, VM, VM, VM, AN, AN, AN, AN] + ([VM] + [AN] * n_next if n_next else [AN]),
+        out_specs=[VM] * (n_state - 1) + [AN] * (len(outs) - n_state + 1),
+        scratch_shapes=[
+            four,
+            pltpu.VMEM((width, cols), BF16),
+            pltpu.VMEM((heads, tall, 128), BF16),
+            pltpu.VMEM(wo.shape, BF16),
         ]
-        + (
-            [like((RANKS, rows, width))] + [like(full_shape(count, b.shape[2:])) for b in blocks]
-            if more
-            else [like(extra[0].shape)]
-        ),
-        in_specs=[VM, VM, VM, AN, AN, AN, AN] + ([VM] + [AN] * more if more else [AN]),
-        out_specs=[VM] * 5 + [AN] * 2 + [AN] * (1 + more),
-        scratch_shapes=[
-            pltpu.VMEM(wo.shape, BF16),
-            pltpu.VMEM((width, 2 * hidden), BF16),
-            pltpu.VMEM(wd_shape, BF16),
-            three,
-            three,
-            four,
-            three,
-            three,
-        ]
-        + ([four] if more else [])
+        + [pltpu.VMEM(shape, BF16) for shape in shapes]
+        + [three, three, four, three, three]
+        + ([four] if n_next else [])
         + sems(count),
-        compiler_params=params(2 if more else 3),
-        name="body_more" if more else "body",
-    )(o, h, gain, wo, wgate, wup, down, *extra)
+        compiler_params=params(2 if n_next else 3),
+        name="body_more" if n_next else "body",
+    )(n1, wq, *tables, h, gain, wo, *inner, *extra)
     got = list(got)
-    got[6] = got[6].reshape(-1, width)
-    return got[:7], got[7], [f.reshape(-1, f.shape[-1]) for f in got[8:]]
+    state, rest = got[:n_state], got[n_state:]
+    inner = [flat(rest.pop(0)) if late[i] else inner[i] for i in range(3)]
+    return state, inner, rest[0], [flat(f) for f in rest[1:]]
 
 
 def call_back(count, start, rest, parts):
-    first, last = len(start) == 2, len(rest) == 1
+    first, last = len(start) == 1, len(rest) == 1
     rows, width = start[0].shape if first else start[2].shape
     tall = RANKS * rows
     three = pltpu.VMEM((3, rows, width), BF16)
     four = pltpu.VMEM((RANKS, rows, width), BF16)
-    in_specs = [VM, AN] if first else [VM, AN, VM, VM, VM]
+    in_specs = [VM] if first else [VM, AN, VM, VM, VM]
     in_specs += [VM] if last else [AN, AN, AN, AN, VM, VM, VM, VM]
     n_red = len(parts)
     in_specs += [AN] * n_red
     outs, out_specs, scratch = [], [], []
-    if first:
-        outs, out_specs = [like(start[1].shape, start[1].dtype)], [AN]
-    elif not last:
+    if last:
+        outs, out_specs = [like((rows, width)), like((16, GAIN_COLS), F32)], [AN, VM]
+    elif not first:
         outs, out_specs = [like((rows, width), F32), like((1, width), F32)], [VM, VM]
-    else:
-        outs, out_specs = [like((rows, width)), like((16, GAIN_COLS), F32)], [AN, VM]
     if not first:
         scratch += [pltpu.VMEM((width, start[0].shape[1]), BF16), three, three]
     if last:
@@ -1062,6 +1234,16 @@
     return lax.dot_general(a, b, (((0,), (0,)), ((), ())), preferred_element_type=F32).astype(BF16)
 
 
+def swap_pairs(dp_size, ctx_size):
+    pairs = []
+    for dp in range(dp_size):
+        for ctx in range(ctx_size):
+            a, x, core = dp // 4, dp // 2 % 2, dp % 2
+            zh, zl = ctx // 2, ctx % 2
+            pairs.append((dp * ctx_size + ctx, (a * 4 + zh * 2 + core) * ctx_size + x * 2 + zl))
+    return pairs
+
+
 def shards(dp_size, ctx_size, tokens, cotangent, w_qkv, w_out, w_gate_up, w_down, gains):
     count = dp_size // 4
     rows, width = tokens.shape
@@ -1073,50 +1255,72 @@
     tall = lambda value: value.reshape(length, width)
     rank = lax.rem(lax.div(lax.axis_index("dp"), 2), 2) * 2 + lax.rem(lax.axis_index("ctx"), 2)
 
+    swap = lambda value: lax.ppermute(value, ("dp", "ctx"), swap_pairs(dp_size, ctx_size))
+    tie = lax.optimization_barrier
+
+    swap = lambda value: lax.ppermute(value, ("dp", "ctx"), swap_pairs(dp_size, ctx_size))
+    tie = lax.optimization_barrier
+    tables = wide_tables(length)
+
     packed = [pack_weights(w_qkv, w_out, w_gate_up, gains, count, layer) for layer in range(LAYERS)]
-    all_tokens, full, blocks = call_start(count, tokens, packed[0], packed[1])
+    whole_rows = w_qkv.shape[1] % 16 == 0
+    if whole_rows:
+        head, out, gate, up = packed[0]
+        now, later, downs = (head, out, up), (gate, *packed[1]), ()
+    else:
+        now, later, downs = packed[0], packed[1], (w_down[0],)
+    all_tokens, full, blocks, downs = call_start(count, tokens, now, later, downs)
     gain_rows = full[0][:, -GAIN_COLS:][:, : 2 * LAYERS].astype(F32).T
     gain = lambda layer, which: gain_rows[2 * layer + which][None]
     h = lax.dynamic_index_in_dim(all_tokens, rank, 0, keepdims=False)
-    states = tall(all_tokens).astype(F32)
-    n1 = norm_rows(states, gain(0, 0))
+    n1 = norm_rows(all_tokens.astype(F32), gain(0, 0))
+    if whole_rows:
+        inner, late, plan = (blocks[0], full[2], w_down[0]), (True, False, True), plan_late
+        *blocks, last_up = blocks[1:]
+    else:
+        inner, late, plan = (*full[2:], *downs), (False, False, False), plan_early
 
     records = []
-    swapped = None
     for layer in range(LAYERS):
-        wq, wo, wgate, wup = full
-        wq_now = wq[:, : wq.shape[1] - GAIN_COLS] if layer == 0 else wq
-        proj = jnp.dot(tall(n1), wq_now, preferred_element_type=F32)
-        mixed, saved = attend(proj, cosine, sine_tab, causal)
+        wq, wo = full[:2]
         if layer + 1 < LAYERS:
-            extra = (gain(layer + 1, 0), *blocks)
+            state, inner, n1_next, full = call_body(
+                count, n1, wq, tables, h, gain(layer, 1), wo, inner, late, plan, gain(layer + 1, 0), blocks
+            )
+            if whole_rows:
+                late, plan = (False, True, True), plan_late_end
+                next_inner = (full[2], last_up, w_down[layer + 1])
+            else:
+                late, plan = (False, False, True), plan_end
+                next_inner = (*full[2:], w_down[layer + 1])
         else:
-            extra = (cotangent.astype(BF16),)
-        got, ahead, full = call_body(
-            count, mixed, h, gain(layer, 1), (wo, wgate, wup), w_down[layer], extra
-        )
-        h1, h_next, gate, up, u, n2, wd = got
-        records.append((h, n1, saved, mixed, h1, n2, gate, up, u, (wq, wo, wgate, wup, wd)))
-        h = h_next
-        if layer + 1 < LAYERS:
-            n1 = ahead
-        else:
-            g = ahead
+            state, inner, g, _ = call_body(
+                count, n1, wq, tables, h, gain(layer, 1), wo, inner, late, plan,
+                swap=cotangent.astype(BF16),
+            )
+            n1_next = None
+        qkv, mixed, lse, h1, h_next, gate, up, u, n2 = state
+        saved = saved_heads(qkv, lse)
+        records.append((h, n1, saved, mixed, h1, n2, gate, up, u, (wq, wo, *inner)))
+        h, n1, inner = h_next, n1_next, next_inner
 
     shape7 = lambda value: value.reshape(count, 2, 2, 2, 2, -1, value.shape[-1])
-    start, parts = (g, h.astype(BF16)), []
+    start, parts = (g,), []
     grads = [None] * LAYERS
     gain_grads = [None] * (2 * LAYERS)
     for layer in reversed(range(LAYERS)):
         h_in, n1, saved, mixed, h1, n2, gate, up, u, (wq, wo, wgate, wup, wd) = records[layer]
         got = call_back(count, start, (wd, wgate, wup, wo, gate, up, h1, gain(layer, 1)), parts)
-        if layer == LAYERS - 1:
-            out_act, *got = got
-        else:
+        if layer < LAYERS - 1:
             _, gain_grads[2 * layer + 2], *got = got
             grads[layer + 1] = got[6:]
         gbg, dgu, gh, gain_grads[2 * layer + 1], ghg, do = got[:6]
+        if layer == LAYERS - 1:
+            do, send = tie((do, h.astype(BF16)))
+            out_act = swap(send)
         dqkv = attend_back(saved, mixed, do, cosine, sine_tab, causal)
+        if layer == LAYERS - 1:
+            dqkv, out_act = tie((dqkv, out_act))
         parts = [
             dot_t(u, tall(gbg)).reshape(count, 2, 2, -1, width),
             shape7(dot_t(tall(n2), dgu[:, :hidden])),

time: 781 us -> 772 us (0.988)
  matrix products: 71.4 us -> 47.8 us
  local copies, waits for them, and re-layouts: 39.7 us -> 53.5 us
    dot_general x6 -> x2, matrix products: 17.9 us -> 3.49 us  [attend_back(): jnp.einsum('qkgd,skd->kgqs', query, key, preferred_element_type=F32) * scale]
    pallas_call x3, Pallas kernels: 329 us -> 320 us  [call_back(): pl.pallas_call(functools.partial(back_kernel, count, rows, first, last, n...]
    pallas_call x3, Pallas kernels: 303 us -> 311 us  [the longest x2 233 us: call_body(): pl.pallas_call(functools.partial(body_kernel, count, rows, late, n_next,...]
  transfers between devices with their start and end apart: 0 -> 1, of which waited for: 0 -> 0; matrix products, arithmetic and copies ran while one was open for 0% -> 4% of each run, Pallas kernels for 0% -> 0%
where the time goes in v4:
time: 772 us; the launch traced here: 763 us
  Pallas kernels  630 us (82%)
  local copies, waits for them, and re-layouts  53.5 us (7%)
  matrix products  47.8 us (6%)
  other arithmetic  24.1 us (3%)
    pallas_call x3, Pallas kernels, call_back(): pl.pallas_call(functools.partial(back_kernel, count, rows, first, last, n...  320 us
    pallas_call x2, Pallas kernels, call_body(): pl.pallas_call(functools.partial(body_kernel, count, rows, late, n_next,...  233 us
    pallas_call x1, Pallas kernels, call_start(): pl.pallas_call(functools.partial(start_kernel, count, n, ahead, n_down),...  77.2 us
    dot_general x10, matrix products, dot_t(): lax.dot_general(a, b, (((0,), (0,)), ((), ())), preferred_element_type=F32)  33.8 us
  transfers between devices with their start and end apart: 1, of which 0 were waited for; matrix products, arithmetic and copies ran while one was open for 4% of the time, Pallas kernels for 0%

profile of v4, /device:TPU:0, one launch (start us, length us, event | category | flops | bytes accessed | tf_op | source)
XLA Modules:
  0.0 762.7 jit_solution(15674282841587585172)
XLA Ops:
  0.7 1.1 slice_bitcast_fusion.4
  5.3 1.5 fusion.42
  16.6 77.2 %start.1 = (bf16[4,128,1536]{2,1,0:T(8,128)(2,1)}, bf16[2,2,2,2,2,48,896]{6,5,4,3,2,1,0:T(8,128)(2,1)}, bf16[2,2,2,2,2,48,384]{6,5,4,3,2,1,0:T(8,128)(2,1)}, bf1...) custom-call(bf16[128,1536]{1,0:T(8,128)(2,1)} %refs_0_.1, ...), custom_call_target="tpu_custom_call" | custom-call | tf_op jit(solution)/shard_map/start/pallas_call | solution.py:1099
  93.8 1.9 fusion.12
  95.7 1.8 dynamic-slice_bitcast_fusion.refs_4_.refs_3_
  97.5 1.0 slice_convert_fusion
  101.2 1.6 fusion.14.refs_0_
  102.7 139.8 %body_more.1 = (bf16[512,768]{1,0:T(8,128)(2,1)}, bf16[512,384]{1,0:T(8,128)(2,1)}, f32[512,128]{1,0:T(8,128)}, f32[128,1536]{1,0:T(8,128)}, f32[128,1536]{1,0:T...) custom-call(bf16[4,128,1536]{2,1,0:T(8,128)(2,1)} %fusion.14.refs_0_, ...), custom_call_target="tpu_custom_call" | custom-call | tf_op jit(solution)/shard_map/body_more/pallas_call | solution.py:1153
  242.5 93.7 %body.1 = (bf16[512,768]{1,0:T(8,128)(2,1)}, bf16[512,384]{1,0:T(8,128)(2,1)}, f32[512,128]{1,0:T(8,128)}, f32[128,1536]{1,0:T(8,128)}, f32[128,1536]{1,0:T(8,12...) custom-call(bf16[4,128,1536]{2,1,0:T(8,128)(2,1)} %get-tuple-element, ...), custom_call_target="tpu_custom_call" | custom-call | tf_op jit(solution)/shard_map/body/pallas_call | solution.py:1153
  336.2 1.9 convert_element_type.162
  338.2 78.3 %back_first.1 = (bf16[4,128,1536]{2,1,0:T(8,128)(2,1)}, bf16[512,2048]{1,0:T(8,128)(2,1)}, f32[128,1536]{1,0:T(8,128)}, f32[1,1536]{1,0:T(1,128)}, bf16[4,128,15...) custom-call(bf16[128,1536]{1,0:T(8,128)(2,1)} %get-tuple-element.88.refs_0_, bf16[1024,1536]{1,0:T(8,128)(2,1)} %bitcast.309, ...), custom_call_target="tpu_custom_call" | custom-call | tf_op jit(solution)/shard_map/back_first/pallas_call | solution.py:1222
  416.5 5.1 collective-permute-start
  424.7 1.7 fusion.7
  427.7 1.3 fusion.30
  429.7 3.5 convolution_convert_fusion.3
  433.2 3.5 convolution_convert_fusion.4
  439.0 3.5 convolution_convert_fusion.9
  444.9 2.7 fusion.53
  447.8 3.7 convolution_convert_fusion.5
  451.5 2.8 convolution_convert_fusion.7
  454.3 121.9 %back_mid.1 = (f32[128,1536]{1,0:T(8,128)}, f32[1,1536]{1,0:T(1,128)}, bf16[4,128,1536]{2,1,0:T(8,128)(2,1)}, bf16[512,2048]{1,0:T(8,128)(2,1)}, f32[128,1536]{1...) custom-call(bf16[512,768]{1,0:T(8,128)(2,1)} %copy-done.4, ...), custom_call_target="tpu_custom_call" | custom-call | tf_op jit(solution)/shard_map/back_mid/pallas_call | solution.py:1222
  576.3 1.2 copy.86
  577.6 3.8 fusion.2
  583.6 1.3 fusion.27
  585.6 3.5 convolution_convert_fusion
  589.1 3.5 convolution_convert_fusion.1
  593.7 3.6 convolution_convert_fusion.8
  598.2 2.9 convolution_convert_fusion.6
  601.1 3.5 convolution_convert_fusion.2
  604.6 119.4 %back_last.1 = (bf16[128,1536]{1,0:T(8,128)(2,1)}, f32[16,128]{1,0:T(8,128)}, f32[128,1536]{1,0:T(8,128)}, f32[4,48,1024]{2,1,0:T(8,128)}, f32[4,48,1024]{2,1,0:...) custom-call(bf16[512,768]{1,0:T(8,128)(2,1)} %copy-done.5, bf16[1536,896]{1,0:T(8,128)(2,1)} %bitcast.275, ...), custom_call_target="tpu_custom_call" | custom-call | tf_op jit(solution)/shard_map/back_last/pallas_call | solution.py:1222
  724.0 1.9 slice_bitcast_fusion.11
  725.9 1.7 slice_bitcast_fusion.3
  731.0 1.8 reshape.385
  733.4 1.8 reshape.386
  735.3 1.5 copy.105
  736.8 1.0 copy.127
  739.4 1.7 reshape.376
  741.1 1.7 copy.96
  742.8 1.7 reshape.377
  745.3 1.1 copy.98
  747.5 2.1 convert_element_type.186
  749.5 1.3 slice.209
  750.8 2.0 convert_element_type.170
  752.7 1.3 pad_maximum_fusion.1
  754.0 1.5 maximum_bitcast_fusion
  755.5 1.5 maximum_bitcast_fusion.1
  757.1 3.3 pad_maximum_fusion
  761.4 1.1 pad_maximum_fusion.2
  (218 shorter events, 38.9 us)
Async XLA Ops:
  0.6 3.8 copy-start.49
  0.7 3.9 copy-start.42
  1.8 3.5 copy-start.12
  11.1 3.1 copy-start.32
  11.1 3.1 copy-start.33
  11.5 3.4 copy-start.35
  11.5 4.2 copy-start.40
  11.5 4.2 copy-start.41
  93.8 5.6 copy-start.21
  98.5 2.6 copy-start
  338.1 83.4 %copy-start.18 = (bf16[512,768]{1,0:T(8,128)(2,1)S(1)}, bf16[512,768]{1,0:T(8,128)(2,1)}, u32[]{:S(2)}) copy-start(bf16[512,768]{1,0:T(8,128)(2,1)} %get-tuple-element.86) | copy-start | bytes 2359300
  416.5 5.4 copy-start.34
  416.5 5.6 copy-start.38
  416.5 35.0 %collective-permute-start = (bf16[128,1536]{1,0:T(8,128)(2,1)}, bf16[128,1536]{1,0:T(8,128)(2,1)}, u32[]{:S(2)}, u32[]{:S(2)}) collective-permute-start(bf16[128,1536]{1,0:T(8,128)(2,1)} %convert_element_type.162), channel_id=1, source_target_pairs={{0,0},{1,1},{2,8},{3,9},{4,4},{5,5},{6,12},{7,13},{8,2},{9,3},{10,... | collective-permute-start | bytes 1179656 | tf_op jit(solution)/shard_map/ppermute | solution.py:1261
  421.8 5.8 copy-start.44
  433.2 3.5 copy-start.17
  439.0 3.5 copy-start.36
  443.6 4.0 copy-start.10
  444.8 2.9 copy-start.53
  444.8 2.9 copy-start.57
  447.8 3.7 copy-start.4
  447.8 3.7 copy-start.13
  454.3 123.2 %copy-start.45 = (pred[512,512]{0,1:T(8,128)(4,1)S(1)}, pred[512,512]{0,1:T(8,128)(4,1)}, u32[]{:S(2)}) copy-start(pred[512,512]{0,1:T(8,128)(4,1)} %copy-done.44) | copy-start | bytes 786436
  577.6 3.8 copy-start.11
  581.4 2.2 copy-start.2
  583.6 2.0 copy-start.52
  589.1 3.5 copy-start.7
  589.1 3.5 copy-start.9
  593.7 3.6 copy-start.46
  593.7 3.6 copy-start.47
  593.7 3.6 copy-start.48
  593.7 4.5 copy-start.1
  598.2 2.9 copy-start.5
  598.2 2.9 copy-start.54
  598.2 2.9 copy-start.56
  604.6 123.0 %copy-start.20 = (f32[4,48,768]{2,1,0:T(8,128)S(1)}, f32[4,48,768]{2,1,0:T(8,128)}, u32[]{:S(2)}) copy-start(f32[4,48,768]{2,1,0:T(8,128)} %get-tuple-element.127) | copy-start | bytes 1769476
  724.0 4.4 copy-start.24
  727.6 2.1 copy-start.23
  735.2 2.6 copy-start.43
  735.3 3.3 copy-start.26
  736.8 7.8 %copy-start.14 = (f32[4,6,8,384]{3,2,1,0:T(8,128)S(1)}, f32[4,6,8,384]{3,2,1,0:T(8,128)}, u32[]{:S(2)}) copy-start(f32[4,6,8,384]{3,2,1,0:T(8,128)} %slice_bitcast_fusion.3) | copy-start | bytes 884740
  736.8 10.4 %copy-start.25 = (f32[48,4,192]{2,0,1:T(8,128)S(1)}, f32[48,4,192]{2,0,1:T(8,128)}, u32[]{:S(2)}) copy-start(f32[48,4,192]{2,0,1:T(8,128)} %get-tuple-element.156) | copy-start | bytes 442372
  747.4 5.3 copy-start.27
  747.4 5.3 copy-start.28
  757.1 3.3 copy-start.15
  757.1 4.2 copy-start.16
  757.1 4.2 copy-start.29
  757.1 4.2 copy-start.30
  (11 other events, 13.5 us)

commit v5 on v4

--- a/solution.py
+++ b/solution.py
@@ -104,7 +104,7 @@
             copy.wait_send()
 
 
-REMOTE_SEMS, LOCAL_SEMS = 128, 32
+REMOTE_SEMS, LOCAL_SEMS = 128, 48
 
 
 def sems(count=2):
@@ -400,11 +400,15 @@
             self()
 
 
-def wide_tables(length):
+def np_tables(length):
     steps = np.arange(HEAD_DIM // 2, dtype=np.float32)
     inverse = np.exp(steps * np.float32(-2.0 * np.log(ROPE_BASE) / HEAD_DIM)).astype(np.float32)
     angles = np.arange(length, dtype=np.float32)[:, None] * inverse[None, :]
-    cosine, sine = np.cos(angles), np.sin(angles)
+    return np.cos(angles), np.sin(angles)
+
+
+def wide_tables(length):
+    cosine, sine = np_tables(length)
     turned = (HEADS + KV_HEADS) // RANKS
     still = KV_HEADS // RANKS * HEAD_DIM
     cos_all = np.concatenate([cosine] * (2 * turned) + [np.ones((length, still))], axis=1)
@@ -453,7 +457,7 @@
     return jnp.concatenate(columns[:-1], axis=1)
 
 
-def project_heads(rows, n1, wq, cos_ref, sin_ref, qkv_ref, heads):
+def project_heads(rows, n1, wq, cos_ref, sin_ref, heads):
     count = heads.shape[0]
 
     @pl.loop(0, RANKS)
@@ -461,7 +465,6 @@
         span = rows_of(b, rows)
         y = jnp.dot(n1[b], wq[...], preferred_element_type=F32)
         y = turn(y, cos_ref[span, :], sin_ref[span, :])
-        qkv_ref[span, :] = y.astype(BF16)
         for h in range(count):
             heads[h, span, :] = head_window(y, h).astype(BF16)
 
@@ -495,6 +498,75 @@
         )
     lse_ref[span, :] = lse_all
     o_ref[span, :] = heads_joined(mixed).astype(BF16)
+
+
+def window_tables(length):
+    cosine, sine = np_tables(length)
+    none = np.zeros((length, 128 - HEAD_DIM))
+    cos_one = np.concatenate([cosine, cosine, none], axis=1)
+    sin_one = np.concatenate([-sine, sine, none], axis=1)
+    return jnp.asarray(cos_one, F32), jnp.asarray(sin_one, F32)
+
+
+def turn_window(values, cosine, sine):
+    half = HEAD_DIM // 2
+    lane = lax.broadcasted_iota(jnp.int32, values.shape, 1)
+    other = jnp.where(lane < half, pltpu.roll(values, 128 - half, 1), pltpu.roll(values, half, 1))
+    return values * cosine + other * sine
+
+
+def dot_tn(a, b):
+    return lax.dot_general(a, b, (((0,), (0,)), ((), ())), preferred_element_type=F32)
+
+
+def attend_rows_back(rows, rank, do_rows, heads, o_ref, lse_ref, cos_ref, sin_ref, dq_ref, dkv):
+    span = rows_of(rank, rows)
+    queries = HEADS // RANKS
+    pairs = KV_HEADS // RANKS
+    groups = HEADS // KV_HEADS
+    o_rows = o_ref[span, :].astype(F32)
+    parts = []
+    for h in range(queries):
+        kv = h // groups
+        do_h = head_window(do_rows, h)
+        delta = jnp.sum(do_h * head_window(o_rows, h), axis=-1, keepdims=True)
+        do_b = do_h.astype(BF16)
+        query, key, value = heads[h, span, :], heads[queries + kv], heads[queries + pairs + kv]
+        weights = jnp.exp(causal_scores(rows, rank, query, key) - lse_ref[span, h : h + 1])
+        grad_w = lax.dot_general(do_b, value, (((1,), (1,)), ((), ())), preferred_element_type=F32)
+        ds = (weights * (grad_w - delta) * HEAD_DIM ** (-0.5)).astype(BF16)
+        dq = jnp.dot(ds, key, preferred_element_type=F32)
+        parts.append(turn_window(dq, cos_ref[span, :], -sin_ref[span, :]))
+        dkv[kv] += dot_tn(ds, query)
+        dkv[pairs + kv] += dot_tn(weights.astype(BF16), do_b)
+    joined = heads_joined(parts)
+    dq_ref[span, pl.ds(0, joined.shape[1])] = joined.astype(BF16)
+
+
+def close_keys(rows, dkv, cos_ref, sin_ref, dqkv_ref):
+    pairs = KV_HEADS // RANKS
+    first = HEADS // RANKS * HEAD_DIM
+
+    @pl.loop(0, RANKS)
+    def _(b):
+        span = rows_of(b, rows)
+        parts = [turn_window(dkv[i, span, :], cos_ref[span, :], -sin_ref[span, :]) for i in range(pairs)]
+        parts += [dkv[pairs + i, span, :] for i in range(pairs)]
+        joined = heads_joined(parts)
+        dqkv_ref[span, pl.ds(first, joined.shape[1])] = joined.astype(BF16)
+
+
+def put_blocks(target, value):
+    *lead, rows, cols = target.shape
+    if rows % 16 == 0:
+        target.reshape(value.shape[0], cols)[...] = value.astype(BF16)
+        return
+    for block in range(value.shape[0] // rows):
+        index, left = [], block
+        for size in reversed(lead):
+            index.append(left % size)
+            left //= size
+        target[tuple(reversed(index))] = value[block * rows : (block + 1) * rows].astype(BF16)
 
 
 def start_kernel(count, n, ahead, n_down, *refs):
@@ -558,14 +630,14 @@
         blocks = refs.take(n_next)
     else:
         (swap_src,) = refs.take(1)
-    qkv_ref, o_ref, lse_ref, h1_ref, hn_ref, gate_ref, up_ref, u_ref, ng_hbm = refs.take(9)
+    heads, o_ref, lse_ref, h1_ref, hn_ref, gate_ref, up_ref, u_ref, ng_hbm = refs.take(9)
     late_out = [refs.take(1)[0] if late[i] else None for i in range(3)]
     if n_next:
         (nn_hbm,) = refs.take(1)
         full = refs.take(n_next)
     else:
         (swap_dst,) = refs.take(1)
-    n1, wq, heads, wo = refs.take(4)
+    n1, wq, wo = refs.take(3)
     inner = refs.take(3)
     out_a, land_a, land_n, out_b, land_b = refs.take(5)
     if n_next:
@@ -609,7 +681,7 @@
 
     load_q.wait()
     load_n.wait()
-    project_heads(rows, n1, wq, cos_ref, sin_ref, qkv_ref, heads)
+    project_heads(rows, n1, wq, cos_ref, sin_ref, heads)
     load_out.wait()
     sums = Sum(net, out_a, land_a)
     for i in (2, 0, 1):
@@ -761,184 +833,244 @@
     ]
 
 
-def back_kernel(count, rows, first, last, n_red, *refs):
+class Back:
+    def __init__(self, net, rows):
+        self.net, self.place, self.rows = net, net.place, rows
+        self.peers = net.place.peers
+
+    def enter(self, r, tick):
+        rows, place = self.rows, self.place
+        width = r["gnew"].shape[1]
+        total = Sum(self.net, r["out_a"], r["land_a"])
+        for i in (2, 0, 1):
+            span = rows_of(self.peers[i][1], rows)
+
+            def use(cols, y, i=i):
+                r["out_a"][i, :, cols] = y.astype(BF16)
+
+            products(lambda: r["dqkv"][span, :], r["wq"], width, width, True, use)
+            total.ready(i)
+        own = rows_of(place.rank, rows)
+
+        def use_own(cols, y):
+            r["gnew"][:, cols] = y
+
+        products(lambda: r["dqkv"][own, :], r["wq"], width, width, True, use_own)
+        total.forward()
+        tick()
+        dn = total.result(r["gnew"][...])
+        back, ggain = norm_rows_back(r["hin"][...].astype(F32), r["gain_in"][...], dn)
+        r["gnew"][...] = r["ghin"][...] + back
+        return ggain
+
+    def feed_forward(self, r, tick, ready, between):
+        net, rows, place = self.net, self.rows, self.place
+        land_g, dgu, out_b = r["land_g"], r["dgu"], r["out_b"]
+        width = land_g.shape[2]
+        hidden = r["gate"].shape[1]
+        land_g[place.rank] = r["g"][...].astype(BF16)
+        gather = Spread(net, land_g)
+        tick()
+        ready()
+
+        def inner_block(rank):
+            span = rows_of(rank, rows)
+            du = lax.dot_general(
+                land_g[rank], r["wd"][...], (((1,), (1,)), ((), ())), preferred_element_type=F32
+            )
+            gate, up = r["gate"][span, :], r["up"][span, :]
+            sg = 1.0 / (1.0 + jnp.exp(-gate))
+            dgu[span, pl.ds(0, hidden)] = (du * up * sg * (1.0 + gate * (1.0 - sg))).astype(BF16)
+            dgu[span, pl.ds(hidden, hidden)] = (du * gate * sg).astype(BF16)
+            return span
+
+        span = inner_block(place.rank)
+
+        def use_mid(cols, y):
+            r["gh"][:, cols] = y
+
+        products(lambda: dgu[span, :], r["wgu"], width, width, True, use_mid)
+        tick()
+        second = Sum(net, out_b, r["land_b"])
+        for i, rank in gather.arrivals():
+            span = inner_block(rank)
+
+            def use(cols, y, i=i):
+                out_b[i, :, cols] = y.astype(BF16)
+
+            products(lambda: dgu[span, :], r["wgu"], width, width, True, use)
+            second.ready(i)
+            tick()
+        second.forward()
+        tick()
+        between()
+        tick()
+        dn = second.result(r["gh"][...])
+        back, ggain = norm_rows_back(r["h1"][...], r["gain"][...], dn)
+        r["gh"][...] = r["g"][...].astype(F32) + back
+        r["gg"][...] = ggain
+
+    def weight_grads(self, r):
+        net = self.net
+        buffers, copies = r["buffers"], []
+        tile = buffers.shape[1]
+        tall, hidden = r["u"].shape
+        width = r["land_g"].shape[2]
+        g_all = r["land_g"][...].reshape(tall, width)
+
+        def emit(lhs, rhs, outs, m):
+            slot = len(copies) % 2
+            if len(copies) >= 2:
+                for copy in copies[-2]:
+                    copy.wait()
+            buffers[slot, :, pl.ds(0, rhs.shape[1])] = dot_tn(lhs, rhs).astype(BF16)
+            cols = rhs.shape[1] // len(outs)
+            copies.append([
+                net.here(buffers.at[slot, :, pl.ds(k * cols, cols)], out.at[pl.ds(m * tile, tile)])
+                for k, out in enumerate(outs)
+            ])
+
+        for m in range(hidden // tile):
+            emit(r["u"][:, m * tile : (m + 1) * tile], g_all, [r["g_down"]], m)
+        for m in range(width // tile):
+            emit(r["n2"][:, m * tile : (m + 1) * tile], r["dgu"][...], [r["g_gate"], r["g_up"]], m)
+        return copies[-2] + copies[-1]
+
+    def attention(self, r, tick, ready):
+        net, rows, place = self.net, self.rows, self.place
+        land_h = r["land_h"]
+        land_h[place.rank] = r["gh"][...].astype(BF16)
+        gather = Spread(net, land_h)
+        tick()
+        ready()
+        r["dkv"][...] = jnp.zeros(r["dkv"].shape, F32)
+
+        def block(rank):
+            do_rows = jnp.dot(land_h[rank], r["wo"][...], preferred_element_type=F32)
+            do_rows = do_rows.astype(BF16).astype(F32)
+            attend_rows_back(
+                rows, rank, do_rows, r["heads"], r["o"], r["lse"], r["cos"], r["sin"], r["dqkv"], r["dkv"]
+            )
+
+        block(place.rank)
+        tick()
+        for _, rank in gather.arrivals():
+            block(rank)
+            tick()
+        close_keys(rows, r["dkv"], r["cos"], r["sin"], r["dqkv"])
+
+
+ATTEND = ("wo", "heads", "o", "lse", "cos", "sin")
+
+
+def back_kernel(count, rows, names, out_names, scratch_names, n_parts, n_red, plan, *refs):
     refs = Refs(refs)
-    if first:
-        (g_ref,) = refs.take(1)
-    else:
-        dqkv_ref, wq_hbm, ghin_ref, hin_ref, gainin_ref = refs.take(5)
-    if not last:
-        wd_hbm, wgate_hbm, wup_hbm, wo_hbm, gate_ref, up_ref, h1_ref, gain_ref = refs.take(8)
-    else:
-        (other_gains,) = refs.take(1)
-    parts = refs.take(n_red)
-    if last:
-        swap_dst, gains_out = refs.take(2)
-    elif not first:
-        gnew_ref, ggin_ref = refs.take(2)
-    if not last:
-        gbg_hbm, dgu_ref, gh_ref, gg_ref, ghg_hbm, do_ref = refs.take(6)
+    r = dict(zip(names, refs.take(len(names))))
+    parts = refs.take(n_parts)
+    r.update(zip(out_names, refs.take(len(out_names))))
     red_out = refs.take(n_red)
-    if not first:
-        wq, out_a, land_a = refs.take(3)
-    if last:
-        gnew_ref, gsend_ref, gains_all, gains_part = refs.take(4)
-        gains_scratch = refs.take(5)
-    if not last:
-        wd, wgu, wo, land_g, out_b, land_b, land_h = refs.take(7)
+    r.update(zip(scratch_names, refs.take(len(scratch_names))))
     red_scratch = [refs.take(4 if i == 0 else 5) for i in range(n_red)]
+    gains_scratch = refs.take(5) if "gains_out" in r else None
     send, recv, local = refs.take(3)
 
     place = Place(count)
     net = Net(place, send, recv, local)
+    back = Back(net, rows)
+    entering, inner, attention = "hin" in r, "h1" in r, "heads_hbm" in r
+    last = "gains_out" in r
+    waits = {}
+
+    def load(name, source, target):
+        waits[name] = net.here(source, target)
+
+    if last:
+        parts = parts + [r["part_o"], r["part_q"]]
     jobs = []
-    for i in range(n_red):
+    for i, part in enumerate(parts):
         scratch = red_scratch[i] + ([None] if i == 0 else [])
-        jobs.append(Reduce(net, parts[i], red_out[i], *scratch, ranks=i > 0))
-    peers = place.peers
-    if not first:
-        load_q = net.here(wq_hbm.at[:, pl.ds(0, wq.shape[1])], wq)
-    if not last:
-        hidden = wd.shape[0]
-        load_down = net.here(wd_hbm, wd)
-        load_gate = net.here(wgate_hbm, wgu.at[:, pl.ds(0, hidden)])
-        load_up = net.here(wup_hbm, wgu.at[:, pl.ds(hidden, hidden)])
-        load_out = net.here(wo_hbm, wo)
-    place.greet(n_red > 0, last)
-    if first:
-        tick = Ticks([])
-    elif not last:
-        j = jobs
-        tick = Ticks(
-            [
-                [j[0].begin, j[1].begin],
-                [j[0].along_a, j[2].begin],
-                [j[1].along_a, j[3].begin],
-                [j[0].along_zh, j[4].begin],
-                [],
-                [j[2].along_a],
-                [j[1].along_zh],
-                [j[0].among_ranks, j[3].along_a],
-                [j[2].along_zh],
-                [j[1].among_ranks, j[4].along_a],
-                [j[3].along_zh],
-                [j[2].among_ranks, j[4].along_zh],
-                [j[1].done, j[2].done, j[3].among_ranks, j[4].among_ranks],
-                [j[3].done, j[4].done],
-            ]
-        )
-    else:
-        j = jobs
-        tick = Ticks(
-            [
-                [j[0].begin, j[1].begin, j[2].begin],
-                [j[0].along_a, j[3].begin, j[4].begin],
-            ]
-        )
+        jobs.append(Reduce(net, part, red_out[i], *scratch, ranks=i > 0))
+    if entering:
+        load("wq", r["wq_hbm"].at[:, pl.ds(0, r["wq"].shape[1])], r["wq"])
+    if inner:
+        hidden = r["wd"].shape[0]
+        load("wd", r["wd_hbm"], r["wd"])
+        load("wg", r["wgate_hbm"], r["wgu"].at[:, pl.ds(0, hidden)])
+        load("wu", r["wup_hbm"], r["wgu"].at[:, pl.ds(hidden, hidden)])
+        load("u", r["u_hbm"], r["u"])
+        load("n2", r["n2_hbm"], r["n2"])
+    if attention:
+        for name in ("wo", "heads", "o", "lse", "n1"):
+            load(name, r[name + "_hbm"], r[name])
+    place.greet(len(jobs) > 0, "swap_src" in r or last)
+    if "swap_src" in r:
+        jobs.append(Swap(net, r["swap_src"], r["swap_dst"]))
+    tick = Ticks(plan(jobs))
     tick()
-    own = rows_of(place.rank, rows)
-    if not first:
-        load_q.wait()
-        width = ghin_ref.shape[1]
-        total = Sum(net, out_a, land_a)
-        for i in (2, 0, 1):
-            span = rows_of(peers[i][1], rows)
-
-            def use(cols, y, i=i):
-                out_a[i, :, cols] = y.astype(BF16)
-
-            products(lambda: dqkv_ref[span, :], wq, width, width, True, use)
-            total.ready(i)
-
-        def use_own(cols, y):
-            gnew_ref[:, cols] = y
-
-        products(lambda: dqkv_ref[own, :], wq, width, width, True, use_own)
-        total.forward()
-        tick()
-        dn = total.result(gnew_ref[...])
-        back, ggain = norm_rows_back(hin_ref[...].astype(F32), gainin_ref[...], dn)
-        gnew_ref[...] = ghin_ref[...] + back
-        if last:
-            finish_last(
-                place, net, jobs, gnew_ref, gsend_ref, ggain, other_gains, gains_all, gains_part, gains_scratch,
-                gains_out, swap_dst,
-            )
+    ends = []
+
+    def ready_inner():
+        for name in ("wd", "wg", "wu"):
+            waits[name].wait()
+
+    def between():
+        waits["u"].wait()
+        waits["n2"].wait()
+        ends.extend(back.weight_grads(r))
+
+    def ready_attention():
+        for name in ("wo", "heads", "o", "lse"):
+            waits[name].wait()
+
+    if entering and inner:
+        waits["wq"].wait()
+        r["ggin"][...] = back.enter(r, tick)
+        r["g"] = r["gnew"]
+    if inner:
+        back.feed_forward(r, tick, ready_inner, between)
+    if attention:
+        back.attention(r, tick, ready_attention)
+        waits["n1"].wait()
+        width = r["land_h"].shape[2]
+        tall = r["o"].shape[0]
+
+        def grad_out():
+            return dot_tn(r["land_h"][...].reshape(tall, width), r["o"][...])
+
+        def grad_qkv():
+            return dot_tn(r["n1"][...].reshape(tall, width), r["dqkv"][...])
+
+        if not last:
+            r["g_out"][...] = grad_out().astype(BF16)
+            r["g_qkv"][...] = grad_qkv().astype(BF16)
+        else:
+            waits["wq"].wait()
+            made = Ticks([[lambda: put_blocks(r["part_q"], grad_qkv()), lambda: put_blocks(r["part_o"], grad_out())]])
+
+            def both():
+                made()
+                tick()
+
+            ggain = back.enter(r, both)
+            finish_last(net, r, jobs, ggain, gains_scratch)
+            for copy in ends:
+                copy.wait()
+            net.finish()
             return
-        ggin_ref[...] = ggain
-        g_ref = gnew_ref
-    width = g_ref.shape[1]
-    land_g[place.rank] = g_ref[...].astype(BF16)
-    gather = Spread(net, land_g)
-    tick()
-    load_down.wait()
-    load_gate.wait()
-    load_up.wait()
-
-    def inner_block(rank):
-        span = rows_of(rank, rows)
-
-        du = lax.dot_general(land_g[rank], wd[...], (((1,), (1,)), ((), ())), preferred_element_type=F32)
-        gate, up = gate_ref[span, :], up_ref[span, :]
-        sg = 1.0 / (1.0 + jnp.exp(-gate))
-        dgu_ref[span, pl.ds(0, hidden)] = (du * up * sg * (1.0 + gate * (1.0 - sg))).astype(BF16)
-        dgu_ref[span, pl.ds(hidden, hidden)] = (du * gate * sg).astype(BF16)
-
-        return span
-
-    span = inner_block(place.rank)
-
-    def use_mid(cols, y):
-        gh_ref[:, cols] = y
-
-    products(lambda: dgu_ref[span, :], wgu, width, width, True, use_mid)
-    tick()
-    second = Sum(net, out_b, land_b)
-    for i, rank in gather.arrivals():
-        span = inner_block(rank)
-
-        def use(cols, y, i=i):
-            out_b[i, :, cols] = y.astype(BF16)
-
-        products(lambda: dgu_ref[span, :], wgu, width, width, True, use)
-        second.ready(i)
-        tick()
-    keep = net.here(land_g, gbg_hbm)
-    second.forward()
-    dn = second.result(gh_ref[...])
-    back, ggain = norm_rows_back(h1_ref[...], gain_ref[...], dn)
-    gh = g_ref[...].astype(F32) + back
-    gh_ref[...] = gh
-    gg_ref[...] = ggain
-    land_h[place.rank] = gh.astype(BF16)
-    third = Spread(net, land_h)
-    tick()
-    load_out.wait()
-
-    def out_block(rank):
-        span = rows_of(rank, rows)
-
-        def use(cols, y):
-            do_ref[span, cols] = y.astype(BF16)
-
-        products(lambda: land_h[rank], wo, wo.shape[1], wo.shape[1], False, use)
-
-    out_block(place.rank)
-    for _, rank in third.arrivals():
-        tick()
-        out_block(rank)
-    keep_h = net.here(land_h, ghg_hbm)
     tick.rest()
-    keep_h.wait()
-    keep.wait()
+    if "swap_src" in r:
+        jobs[-1].wait()
+    for copy in ends:
+        copy.wait()
     net.finish()
 
 
-def finish_last(place, net, jobs, gnew_ref, gsend_ref, ggain, other_gains, gains_all, gains_part, scratch, gains_out, swap_dst):
-    gsend_ref[...] = gnew_ref[...].astype(BF16)
-    swap = Swap(net, gsend_ref, swap_dst)
+def finish_last(net, r, jobs, ggain, scratch):
+    r["gsend"][...] = r["gnew"][...].astype(BF16)
+    swap = Swap(net, r["gsend"], r["swap_dst"])
     swap.start()
-    gains_all[...] = other_gains[...]
+    gains_all, gains_part = r["gains_all"], r["gains_part"]
+    gains_all[...] = r["other_gains"][...]
     gains_all[0:1, :] = ggain
     gains_part[...] = jnp.zeros(gains_part.shape, BF16)
     count = gains_part.shape[0]
@@ -948,33 +1080,54 @@
         gains_part[index + (slice(None), slice(0, piece))] = gains_all[
             :, block * piece : (block + 1) * piece
         ].astype(BF16)
-    small = Reduce(net, gains_part, gains_out, *scratch, added=True)
+    small = Reduce(net, gains_part, r["gains_out"], *scratch, added=True)
     small.begin()
-    j = jobs
-    j[1].along_a()
-    j[0].along_zh()
-    small.along_a()
-    j[2].along_a()
-    j[1].along_zh()
-    small.along_zh()
-    j[0].among_ranks()
-    j[3].along_a()
-    j[2].along_zh()
-    small.among_ranks()
-    j[1].among_ranks()
-    j[4].along_a()
-    j[3].along_zh()
-    j[2].among_ranks()
-    j[1].done()
-    j[4].along_zh()
-    j[3].among_ranks()
-    j[2].done()
-    small.done()
-    j[4].among_ranks()
-    j[3].done()
-    j[4].done()
+    for step in plan_finish(jobs, small):
+        step()
     swap.wait()
-    net.finish()
+
+
+def plan_finish(j, s):
+    return [
+        s.along_a, j[1].along_zh, j[3].along_a, j[0].among_ranks, s.along_zh, j[4].along_a, j[2].along_zh,
+        j[1].among_ranks, s.among_ranks, j[3].along_zh, j[2].among_ranks, j[0].done, j[4].along_zh,
+        j[3].among_ranks, j[1].done, s.done, j[4].among_ranks, j[2].done, j[3].done, j[4].done,
+    ]
+
+
+def plan_first(j):
+    return [[], [], [], [], [], [], [j[-1].start]]
+
+
+def plan_middle(j):
+    return [
+        [j[0].begin, j[1].begin],
+        [j[0].along_a, j[2].begin],
+        [j[1].along_a, j[3].begin],
+        [j[0].along_zh, j[4].begin],
+        [],
+        [j[2].along_a],
+        [j[1].along_zh],
+        [j[0].among_ranks, j[3].along_a],
+        [j[2].along_zh],
+        [j[1].among_ranks, j[4].along_a],
+        [j[3].along_zh],
+        [j[2].among_ranks, j[4].along_zh],
+        [j[1].done, j[2].done, j[3].among_ranks, j[4].among_ranks],
+        [j[0].done, j[3].done, j[4].done],
+    ]
+
+
+def plan_last(j):
+    return [
+        [j[0].begin, j[1].begin, j[2].begin],
+        [j[0].along_a],
+        [j[1].along_a],
+        [],
+        [j[0].along_zh],
+        [j[2].along_a],
+        [j[3].begin, j[4].begin],
+    ]
 
 
 def pack_weights(w_qkv, w_out, w_gate_up, gains, count, layer):
@@ -1013,62 +1166,6 @@
         part.reshape(2, 2, rows, count, 2, 2, -1).transpose(2, 3, 0, 4, 5, 1, 6).reshape(rows, -1)
     )
     return qkv, wide(out).T, jnp.stack([order(gate), order(up)], axis=1)
-
-
-def rotary_tables(positions, head_size):
-    half_size = head_size // 2
-    freq_index = jnp.arange(half_size).astype(F32)
-    inverse = jnp.exp(freq_index * (-2.0 * jnp.log(ROPE_BASE) / head_size))
-    angles = positions.astype(F32)[:, None] * inverse[None, :]
-    return (jnp.cos(angles), jnp.sin(angles))
-
-
-def rotate(values, cosine, sine_tab):
-    half_size = values.shape[-1] // 2
-    first, second = values[..., :half_size], values[..., half_size:]
-    c, s = cosine[:, None, :], sine_tab[:, None, :]
-    return jnp.concatenate([first * c - second * s, second * c + first * s], axis=-1)
-
-
-def unrotate(grads, cosine, sine_tab):
-    return rotate(grads, cosine, -sine_tab)
-
-
-def saved_heads(qkv, lse):
-    length = qkv.shape[0]
-    kv = KV_HEADS // RANKS
-    groups = HEADS // KV_HEADS
-    q_cols = kv * groups * HEAD_DIM
-    kv_cols = kv * HEAD_DIM
-    query = qkv[:, :q_cols].reshape(length, kv, groups, HEAD_DIM)
-    key = qkv[:, q_cols : q_cols + kv_cols].reshape(length, kv, HEAD_DIM)
-    value = qkv[:, q_cols + kv_cols :].reshape(length, kv, HEAD_DIM)
-    return query, key, value, lse[:, : kv * groups].T.reshape(kv, groups, length, 1)
-
-
-def attend_back(saved, mixed, grad_mixed, cosine, sine_tab, causal):
-    query, key, value, lse = saved
-    length = query.shape[0]
-    grad_mixed = grad_mixed.reshape(query.shape)
-    mixed = mixed.reshape(query.shape)
-    scale = HEAD_DIM ** (-0.5)
-    scores = jnp.einsum("qkgd,skd->kgqs", query, key, preferred_element_type=F32) * scale
-    scores = jnp.where(causal[None, None], scores, MASKED)
-    weights = jnp.exp(scores - lse)
-    grad_weights = jnp.einsum("qkgd,skd->kgqs", grad_mixed, value, preferred_element_type=F32)
-    delta = jnp.sum(grad_mixed.astype(F32) * mixed.astype(F32), axis=-1)
-    delta = jnp.transpose(delta, (1, 2, 0))[..., None]
-    grad_scores = (weights * (grad_weights - delta) * scale).astype(BF16)
-    grad_query = jnp.einsum("kgqs,skd->qkgd", grad_scores, key, preferred_element_type=F32)
-    grad_key = jnp.einsum("kgqs,qkgd->skd", grad_scores, query, preferred_element_type=F32)
-    grad_value = jnp.einsum(
-        "kgqs,qkgd->skd", weights.astype(BF16), grad_mixed, preferred_element_type=F32
-    )
-    grad_query = unrotate(grad_query.reshape(length, -1, HEAD_DIM), cosine, sine_tab)
-    grad_key = unrotate(grad_key, cosine, sine_tab)
-    return jnp.concatenate(
-        [g.reshape(length, -1) for g in (grad_query, grad_key, grad_value)], axis=1
-    ).astype(BF16)
 
 
 VM = pl.BlockSpec(memory_space=pltpu.VMEM)
@@ -1132,7 +1229,7 @@
             shape = full_shape(count, shape[2:]) if i < 2 else (count, 2, 2) + shape
         shapes.append(shape)
     outs = [
-        like((tall, cols)),
+        like((heads, tall, 128)),
         like((tall, o_cols)),
         like((tall, 128), F32),
         like((rows, width), F32),
@@ -1158,7 +1255,6 @@
         scratch_shapes=[
             four,
             pltpu.VMEM((width, cols), BF16),
-            pltpu.VMEM((heads, tall, 128), BF16),
             pltpu.VMEM(wo.shape, BF16),
         ]
         + [pltpu.VMEM(shape, BF16) for shape in shapes]
@@ -1174,74 +1270,26 @@
     return state, inner, rest[0], [flat(f) for f in rest[1:]]
 
 
-def call_back(count, start, rest, parts):
-    first, last = len(start) == 1, len(rest) == 1
-    rows, width = start[0].shape if first else start[2].shape
-    tall = RANKS * rows
-    three = pltpu.VMEM((3, rows, width), BF16)
-    four = pltpu.VMEM((RANKS, rows, width), BF16)
-    in_specs = [VM] if first else [VM, AN, VM, VM, VM]
-    in_specs += [VM] if last else [AN, AN, AN, AN, VM, VM, VM, VM]
-    n_red = len(parts)
-    in_specs += [AN] * n_red
-    outs, out_specs, scratch = [], [], []
-    if last:
-        outs, out_specs = [like((rows, width)), like((16, GAIN_COLS), F32)], [AN, VM]
-    elif not first:
-        outs, out_specs = [like((rows, width), F32), like((1, width), F32)], [VM, VM]
-    if not first:
-        scratch += [pltpu.VMEM((width, start[0].shape[1]), BF16), three, three]
-    if last:
-        gains_shape = full_shape(count, (16, GAIN_COLS))
-        scratch += [
-            pltpu.VMEM((rows, width), F32),
-            pltpu.VMEM((rows, width), BF16),
-            pltpu.VMEM((16, width), F32),
-            pltpu.VMEM(gains_shape, BF16),
-        ]
-        scratch += Reduce.scratch(gains_shape)
-    else:
-        wd, wgate, wup, wo = rest[:4]
-        hidden = wgate.shape[1]
-        outs += [
-            like((RANKS, rows, width)),
-            like((tall, 2 * hidden)),
-            like((rows, width), F32),
-            like((1, width), F32),
-            like((RANKS, rows, width)),
-            like((tall, wo.shape[1])),
-        ]
-        out_specs += [AN, VM, VM, VM, AN, VM]
-        scratch += [pltpu.VMEM(s, BF16) for s in (wd.shape, (width, 2 * hidden), wo.shape)]
-        scratch += [four, three, three, four]
-    for i, part in enumerate(parts):
-        scratch += Reduce.scratch(part.shape, ranks=i > 0)
-        tail = part.shape[-2:]
-        outs.append(like(tail if i == 0 else (RANKS,) + tail, F32))
-        out_specs.append(VM)
-    return pl.pallas_call(
-        functools.partial(back_kernel, count, rows, first, last, n_red),
-        out_shape=outs,
-        in_specs=in_specs,
-        out_specs=out_specs,
-        scratch_shapes=scratch + sems(count),
-        compiler_params=params(4 if first else (6 if last else 5)),
-        name="back_first" if first else ("back_last" if last else "back_mid"),
-    )(*start, *rest, *parts)
-
-
-def dot_t(a, b):
-    return lax.dot_general(a, b, (((0,), (0,)), ((), ())), preferred_element_type=F32).astype(BF16)
-
-
-def swap_pairs(dp_size, ctx_size):
-    pairs = []
-    for dp in range(dp_size):
-        for ctx in range(ctx_size):
-            a, x, core = dp // 4, dp // 2 % 2, dp % 2
-            zh, zl = ctx // 2, ctx % 2
-            pairs.append((dp * ctx_size + ctx, (a * 4 + zh * 2 + core) * ctx_size + x * 2 + zl))
-    return pairs
+def call_back(name, count, rows, inputs, outputs, scratch, parts, made, plan, collective_id):
+    shapes = [p.shape for p in parts] + list(made)
+    red_out = [like(shape[-2:] if i == 0 else (RANKS,) + shape[-2:], F32) for i, shape in enumerate(shapes)]
+    scratch_shapes = [pltpu.VMEM(shape, dtype) for shape, dtype in scratch.values()]
+    for i, shape in enumerate(shapes):
+        scratch_shapes += Reduce.scratch(shape, ranks=i > 0)
+    if "gains_out" in outputs:
+        scratch_shapes += Reduce.scratch(scratch["gains_part"][0])
+    got = pl.pallas_call(
+        functools.partial(
+            back_kernel, count, rows, tuple(inputs), tuple(outputs), tuple(scratch), len(parts), len(shapes), plan
+        ),
+        out_shape=[shape for shape, _ in outputs.values()] + red_out,
+        in_specs=[spec for _, spec in inputs.values()] + [AN] * len(parts),
+        out_specs=[spec for _, spec in outputs.values()] + [VM] * len(red_out),
+        scratch_shapes=scratch_shapes + sems(count),
+        compiler_params=params(collective_id),
+        name=name,
+    )(*[value for value, _ in inputs.values()], *parts)
+    return dict(zip(outputs, got)), got[len(outputs) :]
 
 
 def shards(dp_size, ctx_size, tokens, cotangent, w_qkv, w_out, w_gate_up, w_down, gains):
@@ -1249,18 +1297,14 @@
     rows, width = tokens.shape
     length = RANKS * rows
     hidden = w_gate_up.shape[-1] // RANKS
-    positions = jnp.arange(length, dtype=jnp.int32)
-    cosine, sine_tab = rotary_tables(positions, HEAD_DIM)
-    causal = positions[None, :] <= positions[:, None]
     tall = lambda value: value.reshape(length, width)
     rank = lax.rem(lax.div(lax.axis_index("dp"), 2), 2) * 2 + lax.rem(lax.axis_index("ctx"), 2)
 
     swap = lambda value: lax.ppermute(value, ("dp", "ctx"), swap_pairs(dp_size, ctx_size))
     tie = lax.optimization_barrier
 
-    swap = lambda value: lax.ppermute(value, ("dp", "ctx"), swap_pairs(dp_size, ctx_size))
-    tie = lax.optimization_barrier
     tables = wide_tables(length)
+    windows = window_tables(length)
 
     packed = [pack_weights(w_qkv, w_out, w_gate_up, gains, count, layer) for layer in range(LAYERS)]
     whole_rows = w_qkv.shape[1] % 16 == 0
@@ -1299,40 +1343,116 @@
                 swap=cotangent.astype(BF16),
             )
             n1_next = None
-        qkv, mixed, lse, h1, h_next, gate, up, u, n2 = state
-        saved = saved_heads(qkv, lse)
-        records.append((h, n1, saved, mixed, h1, n2, gate, up, u, (wq, wo, *inner)))
+        heads, mixed, lse, h1, h_next, gate, up, u, n2 = state
+        records.append(dict(
+            hin=h, n1=n1, heads=heads, o=mixed, lse=lse, h1=h1, n2=tall(n2), gate=gate, up=up, u=u,
+            wq=wq, wo=wo, wgate=inner[0], wup=inner[1], wd=inner[2],
+        ))
         h, n1, inner = h_next, n1_next, next_inner
 
+    hidden = records[0]["u"].shape[1]
+    heads = (HEADS + 2 * KV_HEADS) // RANKS
+    cols = heads * HEAD_DIM
+    o_cols = HEADS // RANKS * HEAD_DIM
     shape7 = lambda value: value.reshape(count, 2, 2, 2, 2, -1, value.shape[-1])
-    start, parts = (g,), []
-    grads = [None] * LAYERS
-    gain_grads = [None] * (2 * LAYERS)
-    for layer in reversed(range(LAYERS)):
-        h_in, n1, saved, mixed, h1, n2, gate, up, u, (wq, wo, wgate, wup, wd) = records[layer]
-        got = call_back(count, start, (wd, wgate, wup, wo, gate, up, h1, gain(layer, 1)), parts)
-        if layer < LAYERS - 1:
-            _, gain_grads[2 * layer + 2], *got = got
-            grads[layer + 1] = got[6:]
-        gbg, dgu, gh, gain_grads[2 * layer + 1], ghg, do = got[:6]
-        if layer == LAYERS - 1:
-            do, send = tie((do, h.astype(BF16)))
-            out_act = swap(send)
-        dqkv = attend_back(saved, mixed, do, cosine, sine_tab, causal)
-        if layer == LAYERS - 1:
-            dqkv, out_act = tie((dqkv, out_act))
-        parts = [
-            dot_t(u, tall(gbg)).reshape(count, 2, 2, -1, width),
-            shape7(dot_t(tall(n2), dgu[:, :hidden])),
-            shape7(dot_t(tall(n2), dgu[:, hidden:])),
-            shape7(dot_t(tall(ghg), mixed)),
-            shape7(dot_t(tall(n1), dqkv)),
-        ]
-        start = (dqkv, wq, gh, h_in, gain(layer, 0))
-    others = jnp.concatenate([jnp.zeros((1, width), F32)] + gain_grads[1:], axis=0)
+    three, four = ((3, rows, width), BF16), ((RANKS, rows, width), BF16)
+    row_f32 = ((rows, width), F32)
+
+    def inner_in(layer):
+        rec = records[layer]
+        names = dict(wd="wd", wgate="wgate", wup="wup", u="u", n2="n2")
+        values = {key + "_hbm": (rec[name], AN) for key, name in names.items()}
+        return dict(
+            values, gate=(rec["gate"], VM), up=(rec["up"], VM), h1=(rec["h1"], VM), gain=(gain(layer, 1), VM)
+        )
+
+    inner_out = dict(
+        gh=(like((rows, width), F32), VM),
+        gg=(like((1, width), F32), VM),
+        g_down=(like((hidden, width)), AN),
+        g_gate=(like((width, hidden)), AN),
+        g_up=(like((width, hidden)), AN),
+    )
+    inner_scratch = dict(
+        wd=((hidden, width), BF16),
+        wgu=((width, 2 * hidden), BF16),
+        u=((length, hidden), BF16),
+        n2=((length, width), BF16),
+        dgu=((length, 2 * hidden), BF16),
+        buffers=((2, 256, 2 * hidden), BF16),
+        land_g=four,
+        out_b=three,
+        land_b=three,
+    )
+
+    def attention_in(layer):
+        rec = records[layer]
+        values = {name + "_hbm": (rec[name], AN) for name in ("wo", "heads", "o", "lse", "n1")}
+        return dict(values, cos=(windows[0], VM), sin=(windows[1], VM))
+
+    attention_scratch = dict(
+        wo=((width, o_cols), BF16),
+        heads=((heads, length, 128), BF16),
+        o=((length, o_cols), BF16),
+        lse=((length, 128), F32),
+        n1=four,
+        dkv=((2 * KV_HEADS // RANKS, length, 128), F32),
+        land_h=four,
+    )
+
+    def enter_in(layer):
+        rec = records[layer]
+        return dict(wq_hbm=(rec["wq"], AN), hin=(rec["hin"], VM), gain_in=(gain(layer, 0), VM))
+
+    enter_scratch = dict(wq=((width, cols), BF16), out_a=three, land_a=three)
+
+    first, _ = call_back(
+        "back_first", count, rows,
+        dict(g=(g, VM), swap_src=(h.astype(BF16), AN), **inner_in(1), **attention_in(1)),
+        dict(
+            inner_out,
+            dqkv=(like((length, cols)), VM),
+            g_out=(like((width, o_cols)), VM),
+            g_qkv=(like((width, cols)), VM),
+            swap_dst=(like((rows, width)), AN),
+        ),
+        dict(**inner_scratch, **attention_scratch), [], [], plan_first, 4,
+    )
+    parts_of = lambda got: [
+        got["g_down"].reshape(count, 2, 2, -1, width),
+        shape7(got["g_gate"]),
+        shape7(got["g_up"]),
+    ]
+    middle, grads_1 = call_back(
+        "back_mid", count, rows,
+        dict(dqkv=(first["dqkv"], VM), ghin=(first["gh"], VM), **enter_in(1), **inner_in(0)),
+        dict(ggin=(like((1, width), F32), VM), **inner_out),
+        dict(gnew=row_f32, **enter_scratch, **inner_scratch),
+        parts_of(first) + [shape7(first["g_out"]), shape7(first["g_qkv"])], [], plan_middle, 5,
+    )
+    others = jnp.concatenate([jnp.zeros((1, width), F32), middle["gg"], middle["ggin"], first["gg"]], axis=0)
     others = jnp.pad(others, ((0, 16 - 2 * LAYERS), (0, 0)))
-    grad_tokens, gains_sum, *last = call_back(count, start, (others,), parts)
-    grads[0] = last
+    shard_rows = w_qkv.shape[1]
+    shape_o, shape_q = (full_shape(count, (shard_rows, c)) for c in (o_cols, cols))
+    final, grads_0 = call_back(
+        "back_last", count, rows,
+        dict(gh=(middle["gh"], VM), ghin=(middle["gh"], VM), other_gains=(others, VM), **enter_in(0), **attention_in(0)),
+        dict(swap_dst=(like((rows, width)), AN), gains_out=(like((16, GAIN_COLS), F32), VM)),
+        dict(
+            gnew=row_f32,
+            gsend=((rows, width), BF16),
+            gains_all=((16, width), F32),
+            gains_part=(full_shape(count, (16, GAIN_COLS)), BF16),
+            part_o=(shape_o, BF16),
+            part_q=(shape_q, BF16),
+            dqkv=((length, cols), BF16),
+            **enter_scratch,
+            **attention_scratch,
+        ),
+        parts_of(middle), [shape_o, shape_q], plan_last, 6,
+    )
+    out_act, grad_tokens, gains_sum = first["swap_dst"], final["swap_dst"], final["gains_out"]
+    grads = (grads_0, grads_1)
     piece = gains.shape[-1]
     grad_gains = gains_sum[: 2 * LAYERS, :piece].reshape(LAYERS, 2, piece)
     stacked = [unpack_grads(q, o, gate, up, count) for _, gate, up, o, q in grads]

time: 772 us -> 710 us (0.920)
  matrix products: 47.8 us -> 0 us
  local copies, waits for them, and re-layouts: 53.5 us -> 26.8 us
  Pallas kernels: 630 us -> 649 us
    dot_general x20 -> x0, matrix products: 47.8 us -> none  [the longest x10 33.8 us: dot_t(): lax.dot_general(a, b, (((0,), (0,)), ((), ())), preferred_element_type=F32)]
    pallas_call x3, Pallas kernels: 320 us -> 337 us  [call_back(): pl.pallas_call(functools.partial(back_kernel, count, rows, tuple(inputs),...]
  transfers between devices with their start and end apart: 1 -> 0, of which waited for: 0 -> 0; matrix products, arithmetic and copies ran while one was open for 4% -> 0% of each run, Pallas kernels for 0% -> 0%
where the time goes in v5:
time: 710 us; the launch traced here: 698 us
  Pallas kernels  649 us (91%)
  local copies, waits for them, and re-layouts  26.8 us (4%)
  other arithmetic  20.9 us (3%)
    pallas_call x3, Pallas kernels, call_back(): pl.pallas_call(functools.partial(back_kernel, count, rows, tuple(inputs),...  337 us
    pallas_call x2, Pallas kernels, call_body(): pl.pallas_call(functools.partial(body_kernel, count, rows, late, n_next,...  234 us
    pallas_call x1, Pallas kernels, call_start(): pl.pallas_call(functools.partial(start_kernel, count, n, ahead, n_down),...  77.3 us

profile of v5, /device:TPU:0, one launch (start us, length us, event | category | flops | bytes accessed | tf_op | source)
XLA Modules:
  0.0 698.1 jit_solution(7220447908099050892)
XLA Ops:
  0.7 1.1 slice_bitcast_fusion.4
  2.2 0.8 maximum_bitcast_fusion.5.refs_5_
  3.5 0.8 maximum_bitcast_fusion.4.refs_1_
  4.4 0.7 bitcast_bitcast_fusion
  5.1 1.5 fusion.3
  6.6 0.6 reshape_squeeze.6
  7.2 0.4 copy.69
  7.6 0.6 fusion.5
  8.2 1.0 squeeze.36.refs_3_
  9.3 1.0 squeeze.37.refs_4_
  10.3 0.6 reshape_squeeze.7
  10.9 0.4 copy.68
  11.3 0.6 fusion.4
  11.9 1.0 squeeze.40.refs_7_
  12.9 1.0 squeeze.41.refs_8_
  13.9 77.3 %start.1 = (bf16[4,128,1536]{2,1,0:T(8,128)(2,1)}, bf16[2,2,2,2,2,48,896]{6,5,4,3,2,1,0:T(8,128)(2,1)}, bf16[2,2,2,2,2,48,384]{6,5,4,3,2,1,0:T(8,128)(2,1)}, bf1...) custom-call(bf16[128,1536]{1,0:T(8,128)(2,1)} %refs_0_.1, ...), custom_call_target="tpu_custom_call" | custom-call | tf_op jit(solution)/shard_map/start/pallas_call | solution.py:1196
  91.3 1.9 dynamic-slice_bitcast_fusion.refs_4_
  93.2 1.0 slice_convert_fusion
  94.5 0.6 fusion.9
  95.5 1.6 fusion.2.refs_0_.refs_10_
  97.1 0.9 slice_bitcast_fusion
  98.0 140.1 %body_more.1 = (bf16[8,512,128]{2,1,0:T(8,128)(2,1)}, bf16[512,384]{1,0:T(8,128)(2,1)}, f32[512,128]{1,0:T(8,128)}, f32[128,1536]{1,0:T(8,128)}, f32[128,1536]{1...) custom-call(bf16[4,128,1536]{2,1,0:T(8,128)(2,1)} %fusion.2.refs_0_., ...), custom_call_target="tpu_custom_call" | custom-call | tf_op jit(solution)/shard_map/body_more/pallas_call | solution.py:1250
  238.1 0.8 convert_element_type.25.refs_10_
  238.9 94.1 %body.1 = (bf16[8,512,128]{2,1,0:T(8,128)(2,1)}, bf16[512,384]{1,0:T(8,128)(2,1)}, f32[512,128]{1,0:T(8,128)}, f32[128,1536]{1,0:T(8,128)}, f32[128,1536]{1,0:T(...) custom-call(bf16[4,128,1536]{2,1,0:T(8,128)(2,1)} %get-tuple-element, ...), custom_call_target="tpu_custom_call" | custom-call | tf_op jit(solution)/shard_map/body/pallas_call | solution.py:1250
  333.0 1.9 convert_element_type.26.refs_1_
  334.9 87.5 %back_first.1 = (f32[128,1536]{1,0:T(8,128)}, f32[1,1536]{1,0:T(1,128)}, bf16[1024,1536]{1,0:T(8,128)(2,1)}, bf16[1536,1024]{1,0:T(8,128)(2,1)}, bf16[1536,1024]...) custom-call(bf16[128,1536]{1,0:T(8,128)(2,1)} %get-tuple-element.84., ...), custom_call_target="tpu_custom_call" | custom-call | tf_op jit(solution)/shard_map/back_first/pallas_call | solution.py:1281
  422.4 119.2 %back_mid.1 = (f32[1,1536]{1,0:T(1,128)}, f32[128,1536]{1,0:T(8,128)}, f32[1,1536]{1,0:T(1,128)}, bf16[1024,1536]{1,0:T(8,128)(2,1)}, bf16[1536,1024]{1,0:T(8,12...) custom-call(bf16[512,768]{1,0:T(8,128)(2,1)} %get-tuple-element.97.r, ...), custom_call_target="tpu_custom_call" | custom-call | tf_op jit(solution)/shard_map/back_mid/pallas_call | solution.py:1281
  541.7 0.8 pad_maximum_fusion.4
  542.5 0.6 pad.9.refs_2_
  543.2 130.4 %back_last.1 = (bf16[128,1536]{1,0:T(8,128)(2,1)}, f32[16,128]{1,0:T(8,128)}, f32[128,1536]{1,0:T(8,128)}, f32[4,48,1024]{2,1,0:T(8,128)}, f32[4,48,1024]{2,1,0:...) custom-call(f32[128,1536]{1,0:T(8,128)} %get-tuple-element.111.refs_0_.refs_1_, ...), custom_call_target="tpu_custom_call" | custom-call | tf_op jit(solution)/shard_map/back_last/pallas_call | solution.py:1281
  673.6 2.5 pad_maximum_fusion.1
  676.1 0.7 reshape.197
  676.8 0.6 copy.48
  677.4 0.7 reshape.198
  678.1 0.6 copy.49
  678.7 1.5 maximum_bitcast_fusion
  680.2 1.8 reshape.199
  682.0 0.6 copy.50
  682.6 1.8 reshape.200
  684.4 0.6 copy.51
  685.0 1.5 maximum_bitcast_fusion.1
  686.6 3.3 pad_maximum_fusion
  690.0 0.9 pad_maximum_fusion.3
  691.9 0.7 copy-done.2
  693.3 1.1 pad_maximum_fusion.2
  694.4 1.0 convert_element_type.28
  695.4 1.3 slice.129
  696.7 1.0 convert_element_type.27
  (70 shorter events, 3.3 us)
Async XLA Ops:
  1.9 1.5 copy-start.15
  2.1 2.2 copy-start.11
  3.1 2.0 copy-start.1
  91.3 3.8 copy-start
  95.5 1.6 copy-start.4
  98.0 140.1 %copy-start.5 = (f32[128,1536]{1,0:T(8,128)S(1)}, f32[128,1536]{1,0:T(8,128)}, u32[]{:S(2)}) copy-start(f32[128,1536]{1,0:T(8,128)} %param.12) | copy-start | bytes 2359300
  422.4 119.3 %copy-start.14 = (f32[1,1536]{1,0:T(1,128)S(1)}, f32[1,1536]{1,0:T(1,128)}, u32[]{:S(2)}) copy-start(f32[1,1536]{1,0:T(1,128)} %get-tuple-element.114) | copy-start | bytes 18436
  543.1 130.5 %copy-start.8 = (f32[128,1536]{1,0:T(8,128)S(1)}, f32[128,1536]{1,0:T(8,128)}, u32[]{:S(2)}) copy-start(f32[128,1536]{1,0:T(8,128)} %get-tuple-element.131) | copy-start | bytes 2359300
  673.6 2.5 copy-start.7
  676.1 1.3 copy-start.6
  686.6 3.3 copy-start.13
  686.6 3.3 copy-start.12
  689.9 1.2 copy-start.3
  691.5 1.1 copy-start.2
  693.3 1.2 copy-start.10
  693.3 3.3 copy-start.9

commit v6 on v5

--- a/solution.py
+++ b/solution.py
@@ -242,7 +242,8 @@
         net, p = self.net, self.net.place
         self.by_zh.wait_recv()
         if not self.ranks:
-            self.out[...] = self.held[p.a, p.zh].astype(F32) + self.from_zh[...].astype(F32)
+            total = self.held[p.a, p.zh].astype(F32) + self.from_zh[...].astype(F32)
+            self.out[...] = total.astype(self.out.dtype)
             return
         for x in range(2):
             for zl in range(2):
@@ -268,9 +269,9 @@
                 own = own + self.from_rank[j].astype(F32)
             self.out[...] = own
             return
-        self.out[p.rank] = own
+        self.out[p.rank] = own.astype(self.out.dtype)
         for j, (_, rank) in enumerate(p.peers):
-            self.out[rank] = self.from_rank[j].astype(F32)
+            self.out[rank] = self.from_rank[j].astype(self.out.dtype)
 
     @staticmethod
     def scratch(shape, ranks=True):
@@ -345,6 +346,72 @@
     def result(self, own):
         self.along_x.wait_recv()
         self.along_zl.wait_recv()
+        return own + self.land[1].astype(F32) + self.land[2].astype(F32)
+
+
+class EvenSpread:
+    def __init__(self, net, land):
+        self.net, self.land = net, land
+        self.peers = net.place.peers
+        self.half = land.shape[1] // 2
+        me = net.place.rank
+        self.x_high = self.go(me, 1, 0)
+        self.z_low = self.go(me, 0, 1)
+        self.x_low = self.go(me, 0, 0)
+        self.z_high = self.go(me, 1, 1)
+
+    def go(self, rank, part, i):
+        rows = self.land.at[rank, pl.ds(part * self.half, self.half)]
+        return self.net.remote(rows, rows, self.peers[i][0])
+
+    def arrivals(self):
+        self.x_high.wait_recv()
+        on_z = self.go(self.peers[0][1], 1, 1)
+        self.z_low.wait_recv()
+        on_x = self.go(self.peers[1][1], 0, 0)
+        self.x_low.wait_recv()
+        yield 0, self.peers[0][1]
+        self.z_high.wait_recv()
+        yield 1, self.peers[1][1]
+        on_z.wait_recv()
+        on_x.wait_recv()
+        yield 2, self.peers[2][1]
+
+    def wait(self):
+        for _ in self.arrivals():
+            pass
+
+
+class EvenSum:
+    def __init__(self, net, out, land):
+        self.net, self.out, self.land = net, out, land
+        self.peers = net.place.peers
+        self.half = out.shape[1] // 2
+
+    def go(self, i, part, slot, peer):
+        rows = pl.ds(part * self.half, self.half)
+        return self.net.remote(self.out.at[i, rows], self.land.at[slot, rows], self.peers[peer][0])
+
+    def ready(self, i):
+        if i == 2:
+            self.low, self.high = self.go(2, 0, 0, 0), self.go(2, 1, 0, 1)
+        elif i == 0:
+            self.x_low = self.go(0, 0, 1, 0)
+        else:
+            self.z_high = self.go(1, 1, 2, 1)
+
+    def forward(self):
+        low, high = pl.ds(0, self.half), pl.ds(self.half, self.half)
+        self.high.wait_recv()
+        add_into(self.out.at[0, high], self.land.at[0, high])
+        self.x_high = self.go(0, 1, 1, 0)
+        self.low.wait_recv()
+        add_into(self.out.at[1, low], self.land.at[0, low])
+        self.z_low = self.go(1, 0, 2, 1)
+
+    def result(self, own):
+        for copy in (self.x_low, self.x_high, self.z_low, self.z_high):
+            copy.wait_recv()
         return own + self.land[1].astype(F32) + self.land[2].astype(F32)
 
 
@@ -683,7 +750,7 @@
     load_n.wait()
     project_heads(rows, n1, wq, cos_ref, sin_ref, heads)
     load_out.wait()
-    sums = Sum(net, out_a, land_a)
+    sums = EvenSum(net, out_a, land_a)
     for i in (2, 0, 1):
         attend_rows(rows, peers[i][1], heads, o_ref, lse_ref)
         span = rows_of(peers[i][1], rows)
@@ -705,7 +772,7 @@
     h1 = sums.result(h1_ref[...])
     h1_ref[...] = h1
     land_n[place.rank] = norm_rows(h1, gain_ref[...])
-    gather = Spread(net, land_n)
+    gather = EvenSpread(net, land_n)
     tick()
     ready(0)
     ready(1)
@@ -715,20 +782,22 @@
 
         gate = jnp.dot(land_n[rank], wg[...], preferred_element_type=F32)
         up = jnp.dot(land_n[rank], wu[...], preferred_element_type=F32)
-        gate_ref[span, :] = gate
-        up_ref[span, :] = up
+        gate_ref[span, :] = gate.astype(BF16)
+        up_ref[span, :] = up.astype(BF16)
         u_ref[span, :] = (gate / (1.0 + jnp.exp(-gate)) * up).astype(BF16)
 
         return span
 
     inner_block(place.rank)
     tick()
-    second = Sum(net, out_b, land_b)
+    second = EvenSum(net, out_b, land_b)
+    got_down = False
     for i, rank in gather.arrivals():
         span = inner_block(rank)
-        if i == 1:
+        if not got_down:
             tick()
             ready(2)
+            got_down = True
 
         def use(cols, y, i=i):
             out_b[i, :, cols] = y.astype(BF16)
@@ -749,7 +818,7 @@
     hn_ref[...] = hn
     if n_next:
         land_q[place.rank] = norm_rows(hn, gain_next[...])
-        third = Spread(net, land_q)
+        third = EvenSpread(net, land_q)
         tick()
         for _ in third.arrivals():
             tick()
@@ -841,7 +910,7 @@
     def enter(self, r, tick):
         rows, place = self.rows, self.place
         width = r["gnew"].shape[1]
-        total = Sum(self.net, r["out_a"], r["land_a"])
+        total = EvenSum(self.net, r["out_a"], r["land_a"])
         for i in (2, 0, 1):
             span = rows_of(self.peers[i][1], rows)
 
@@ -850,6 +919,7 @@
 
             products(lambda: r["dqkv"][span, :], r["wq"], width, width, True, use)
             total.ready(i)
+        tick()
         own = rows_of(place.rank, rows)
 
         def use_own(cols, y):
@@ -869,7 +939,7 @@
         width = land_g.shape[2]
         hidden = r["gate"].shape[1]
         land_g[place.rank] = r["g"][...].astype(BF16)
-        gather = Spread(net, land_g)
+        gather = EvenSpread(net, land_g)
         tick()
         ready()
 
@@ -878,7 +948,7 @@
             du = lax.dot_general(
                 land_g[rank], r["wd"][...], (((1,), (1,)), ((), ())), preferred_element_type=F32
             )
-            gate, up = r["gate"][span, :], r["up"][span, :]
+            gate, up = r["gate"][span, :].astype(F32), r["up"][span, :].astype(F32)
             sg = 1.0 / (1.0 + jnp.exp(-gate))
             dgu[span, pl.ds(0, hidden)] = (du * up * sg * (1.0 + gate * (1.0 - sg))).astype(BF16)
             dgu[span, pl.ds(hidden, hidden)] = (du * gate * sg).astype(BF16)
@@ -891,7 +961,7 @@
 
         products(lambda: dgu[span, :], r["wgu"], width, width, True, use_mid)
         tick()
-        second = Sum(net, out_b, r["land_b"])
+        second = EvenSum(net, out_b, r["land_b"])
         for i, rank in gather.arrivals():
             span = inner_block(rank)
 
@@ -910,7 +980,7 @@
         r["gh"][...] = r["g"][...].astype(F32) + back
         r["gg"][...] = ggain
 
-    def weight_grads(self, r):
+    def weight_grads(self, r, down_made):
         net = self.net
         buffers, copies = r["buffers"], []
         tile = buffers.shape[1]
@@ -930,8 +1000,11 @@
                 for k, out in enumerate(outs)
             ])
 
-        for m in range(hidden // tile):
-            emit(r["u"][:, m * tile : (m + 1) * tile], g_all, [r["g_down"]], m)
+        for k, part in enumerate((r["part_da"], r["part_db"])):
+            cols = part.shape[-1]
+            made = dot_tn(r["u"][...], g_all[:, k * cols : (k + 1) * cols])
+            part.reshape(hidden, cols)[...] = made.astype(BF16)
+        down_made()
         for m in range(width // tile):
             emit(r["n2"][:, m * tile : (m + 1) * tile], r["dgu"][...], [r["g_gate"], r["g_up"]], m)
         return copies[-2] + copies[-1]
@@ -940,7 +1013,7 @@
         net, rows, place = self.net, self.rows, self.place
         land_h = r["land_h"]
         land_h[place.rank] = r["gh"][...].astype(BF16)
-        gather = Spread(net, land_h)
+        gather = EvenSpread(net, land_h)
         tick()
         ready()
         r["dkv"][...] = jnp.zeros(r["dkv"].shape, F32)
@@ -963,14 +1036,14 @@
 ATTEND = ("wo", "heads", "o", "lse", "cos", "sin")
 
 
-def back_kernel(count, rows, names, out_names, scratch_names, n_parts, n_red, plan, *refs):
+def back_kernel(count, rows, names, out_names, scratch_names, n_parts, kinds, plan, *refs):
     refs = Refs(refs)
     r = dict(zip(names, refs.take(len(names))))
     parts = refs.take(n_parts)
     r.update(zip(out_names, refs.take(len(out_names))))
-    red_out = refs.take(n_red)
+    red_out = refs.take(len(kinds))
     r.update(zip(scratch_names, refs.take(len(scratch_names))))
-    red_scratch = [refs.take(4 if i == 0 else 5) for i in range(n_red)]
+    red_scratch = [refs.take(5 if ranks else 4) for ranks in kinds]
     gains_scratch = refs.take(5) if "gains_out" in r else None
     send, recv, local = refs.take(3)
 
@@ -984,12 +1057,10 @@
     def load(name, source, target):
         waits[name] = net.here(source, target)
 
-    if last:
-        parts = parts + [r["part_o"], r["part_q"]]
+    parts = parts + ([r["part_o"], r["part_q"]] if last else [r["part_da"], r["part_db"]])
     jobs = []
-    for i, part in enumerate(parts):
-        scratch = red_scratch[i] + ([None] if i == 0 else [])
-        jobs.append(Reduce(net, part, red_out[i], *scratch, ranks=i > 0))
+    for part, out, scratch, ranks in zip(parts, red_out, red_scratch, kinds):
+        jobs.append(Reduce(net, part, out, *scratch, *([] if ranks else [None]), ranks=ranks))
     if entering:
         load("wq", r["wq_hbm"].at[:, pl.ds(0, r["wq"].shape[1])], r["wq"])
     if inner:
@@ -1016,7 +1087,7 @@
     def between():
         waits["u"].wait()
         waits["n2"].wait()
-        ends.extend(back.weight_grads(r))
+        ends.extend(back.weight_grads(r, tick))
 
     def ready_attention():
         for name in ("wo", "heads", "o", "lse"):
@@ -1045,7 +1116,10 @@
             r["g_qkv"][...] = grad_qkv().astype(BF16)
         else:
             waits["wq"].wait()
-            made = Ticks([[lambda: put_blocks(r["part_q"], grad_qkv()), lambda: put_blocks(r["part_o"], grad_out())]])
+            made = Ticks([
+                [],
+                [lambda: put_blocks(r["part_q"], grad_qkv()), lambda: put_blocks(r["part_o"], grad_out())],
+            ])
 
             def both():
                 made()
@@ -1068,7 +1142,6 @@
 def finish_last(net, r, jobs, ggain, scratch):
     r["gsend"][...] = r["gnew"][...].astype(BF16)
     swap = Swap(net, r["gsend"], r["swap_dst"])
-    swap.start()
     gains_all, gains_part = r["gains_all"], r["gains_part"]
     gains_all[...] = r["other_gains"][...]
     gains_all[0:1, :] = ggain
@@ -1082,51 +1155,70 @@
         ].astype(BF16)
     small = Reduce(net, gains_part, r["gains_out"], *scratch, added=True)
     small.begin()
-    for step in plan_finish(jobs, small):
+    for step in plan_finish(jobs, small, swap):
         step()
     swap.wait()
 
 
-def plan_finish(j, s):
+def plan_finish(j, s, swap):
     return [
-        s.along_a, j[1].along_zh, j[3].along_a, j[0].among_ranks, s.along_zh, j[4].along_a, j[2].along_zh,
-        j[1].among_ranks, s.among_ranks, j[3].along_zh, j[2].among_ranks, j[0].done, j[4].along_zh,
-        j[3].among_ranks, j[1].done, s.done, j[4].among_ranks, j[2].done, j[3].done, j[4].done,
+        s.along_a, j[2].along_a, j[3].along_a, j[1].along_zh, j[0].among_ranks, s.along_zh, j[2].along_zh,
+        s.among_ranks, j[3].along_zh, swap.start, j[1].among_ranks, j[0].done, j[2].among_ranks, s.done, j[1].done,
+        j[3].among_ranks, j[2].done, j[3].done,
     ]
 
 
 def plan_first(j):
-    return [[], [], [], [], [], [], [j[-1].start]]
+    da, db, swap = j
+    return [
+        [],
+        [],
+        [],
+        [],
+        [],
+        [],
+        [swap.start],
+        [da.begin, db.begin],
+        [da.along_a],
+        [db.along_a],
+        [],
+        [da.along_zh],
+        [db.along_zh],
+        [],
+        [da.among_ranks, db.among_ranks],
+    ]
 
 
 def plan_middle(j):
+    gate, up, out, qkv, da, db = j
     return [
-        [j[0].begin, j[1].begin],
-        [j[0].along_a, j[2].begin],
-        [j[1].along_a, j[3].begin],
-        [j[0].along_zh, j[4].begin],
-        [],
-        [j[2].along_a],
-        [j[1].along_zh],
-        [j[0].among_ranks, j[3].along_a],
-        [j[2].along_zh],
-        [j[1].among_ranks, j[4].along_a],
-        [j[3].along_zh],
-        [j[2].among_ranks, j[4].along_zh],
-        [j[1].done, j[2].done, j[3].among_ranks, j[4].among_ranks],
-        [j[0].done, j[3].done, j[4].done],
+        [gate.begin, up.begin, out.begin, qkv.begin],
+        [gate.along_a],
+        [up.along_a],
+        [],
+        [out.along_a],
+        [gate.along_zh],
+        [qkv.along_a],
+        [],
+        [up.along_zh],
+        [da.begin, db.begin],
+        [gate.among_ranks, da.along_a],
+        [out.along_zh, db.along_a, qkv.along_zh, up.among_ranks, out.among_ranks, gate.done, da.along_zh, up.done],
+        [qkv.among_ranks, db.along_zh, out.done, qkv.done, da.among_ranks, db.among_ranks],
     ]
 
 
 def plan_last(j):
+    gate, up, out, qkv = j
     return [
-        [j[0].begin, j[1].begin, j[2].begin],
-        [j[0].along_a],
-        [j[1].along_a],
-        [],
-        [j[0].along_zh],
-        [j[2].along_a],
-        [j[3].begin, j[4].begin],
+        [gate.begin, up.begin],
+        [gate.along_a],
+        [],
+        [up.along_a],
+        [],
+        [gate.along_zh],
+        [],
+        [out.begin, qkv.begin],
     ]
 
 
@@ -1234,8 +1326,8 @@
         like((tall, 128), F32),
         like((rows, width), F32),
         like((rows, width), F32),
-        like((tall, hidden), F32),
-        like((tall, hidden), F32),
+        like((tall, hidden)),
+        like((tall, hidden)),
         like((tall, hidden)),
         like((RANKS, rows, width)),
     ]
@@ -1270,17 +1362,17 @@
     return state, inner, rest[0], [flat(f) for f in rest[1:]]
 
 
-def call_back(name, count, rows, inputs, outputs, scratch, parts, made, plan, collective_id):
+def call_back(name, count, rows, inputs, outputs, scratch, parts, made, kinds, plan, collective_id):
     shapes = [p.shape for p in parts] + list(made)
-    red_out = [like(shape[-2:] if i == 0 else (RANKS,) + shape[-2:], F32) for i, shape in enumerate(shapes)]
+    red_out = [like(((RANKS,) if ranks else ()) + shape[-2:]) for shape, ranks in zip(shapes, kinds)]
     scratch_shapes = [pltpu.VMEM(shape, dtype) for shape, dtype in scratch.values()]
-    for i, shape in enumerate(shapes):
-        scratch_shapes += Reduce.scratch(shape, ranks=i > 0)
+    for shape, ranks in zip(shapes, kinds):
+        scratch_shapes += Reduce.scratch(shape, ranks=ranks)
     if "gains_out" in outputs:
         scratch_shapes += Reduce.scratch(scratch["gains_part"][0])
     got = pl.pallas_call(
         functools.partial(
-            back_kernel, count, rows, tuple(inputs), tuple(outputs), tuple(scratch), len(parts), len(shapes), plan
+            back_kernel, count, rows, tuple(inputs), tuple(outputs), tuple(scratch), len(parts), kinds, plan
         ),
         out_shape=[shape for shape, _ in outputs.values()] + red_out,
         in_specs=[spec for _, spec in inputs.values()] + [AN] * len(parts),
@@ -1369,11 +1461,13 @@
     inner_out = dict(
         gh=(like((rows, width), F32), VM),
         gg=(like((1, width), F32), VM),
-        g_down=(like((hidden, width)), AN),
         g_gate=(like((width, hidden)), AN),
         g_up=(like((width, hidden)), AN),
     )
+    shape_d = (count, 2, 2, w_down.shape[1], width // 2)
     inner_scratch = dict(
+        part_da=(shape_d, BF16),
+        part_db=(shape_d, BF16),
         wd=((hidden, width), BF16),
         wgu=((width, 2 * hidden), BF16),
         u=((length, hidden), BF16),
@@ -1406,7 +1500,7 @@
 
     enter_scratch = dict(wq=((width, cols), BF16), out_a=three, land_a=three)
 
-    first, _ = call_back(
+    first, down_1 = call_back(
         "back_first", count, rows,
         dict(g=(g, VM), swap_src=(h.astype(BF16), AN), **inner_in(1), **attention_in(1)),
         dict(
@@ -1416,19 +1510,16 @@
             g_qkv=(like((width, cols)), VM),
             swap_dst=(like((rows, width)), AN),
         ),
-        dict(**inner_scratch, **attention_scratch), [], [], plan_first, 4,
+        dict(**inner_scratch, **attention_scratch), [], [shape_d] * 2, (False,) * 2, plan_first, 4,
     )
-    parts_of = lambda got: [
-        got["g_down"].reshape(count, 2, 2, -1, width),
-        shape7(got["g_gate"]),
-        shape7(got["g_up"]),
-    ]
+    parts_of = lambda got: [shape7(got["g_gate"]), shape7(got["g_up"])]
     middle, grads_1 = call_back(
         "back_mid", count, rows,
         dict(dqkv=(first["dqkv"], VM), ghin=(first["gh"], VM), **enter_in(1), **inner_in(0)),
         dict(ggin=(like((1, width), F32), VM), **inner_out),
         dict(gnew=row_f32, **enter_scratch, **inner_scratch),
-        parts_of(first) + [shape7(first["g_out"]), shape7(first["g_qkv"])], [], plan_middle, 5,
+        parts_of(first) + [shape7(first["g_out"]), shape7(first["g_qkv"])],
+        [shape_d] * 2, (True,) * 4 + (False,) * 2, plan_middle, 5,
     )
     others = jnp.concatenate([jnp.zeros((1, width), F32), middle["gg"], middle["ggin"], first["gg"]], axis=0)
     others = jnp.pad(others, ((0, 16 - 2 * LAYERS), (0, 0)))
@@ -1449,16 +1540,18 @@
             **enter_scratch,
             **attention_scratch,
         ),
-        parts_of(middle), [shape_o, shape_q], plan_last, 6,
+        parts_of(middle), [shape_o, shape_q], (True,) * 4, plan_last, 6,
     )
     out_act, grad_tokens, gains_sum = first["swap_dst"], final["swap_dst"], final["gains_out"]
-    grads = (grads_0, grads_1)
+    grads = (grads_0, grads_1[:4])
+    downs = (grads_1[4:], down_1)
     piece = gains.shape[-1]
     grad_gains = gains_sum[: 2 * LAYERS, :piece].reshape(LAYERS, 2, piece)
-    stacked = [unpack_grads(q, o, gate, up, count) for _, gate, up, o, q in grads]
+    stacked = [unpack_grads(q, o, gate, up, count) for gate, up, o, q in grads]
     s_qkv, s_out, s_gu = (jnp.stack([s[i] for s in stacked]) for i in range(3))
-    s_down = jnp.stack([g[0] for g in grads])
-    return (out_act.astype(F32), grad_tokens.astype(F32), s_qkv, s_out, s_gu, s_down, grad_gains)
+    s_down = jnp.stack([jnp.concatenate(d, axis=1) for d in downs])
+    wide = lambda value: value.astype(F32)
+    return (wide(out_act), wide(grad_tokens), wide(s_qkv), wide(s_out), wide(s_gu), wide(s_down), grad_gains)
 
 
 def solution(mesh):

time: 710 us -> 640 us (0.901)
  Pallas kernels: 649 us -> 586 us
    pallas_call x3, Pallas kernels: 337 us -> 302 us  [call_back(): pl.pallas_call(functools.partial(back_kernel, count, rows, tuple(inputs),...]
    pallas_call x2, Pallas kernels: 234 us -> 207 us  [call_body(): pl.pallas_call(functools.partial(body_kernel, count, rows, late, n_next,...]
    another operation x7 -> x4, other arithmetic: 8.4 us -> 0.19 us  [shards(): s_qkv, s_out, s_gu = (jnp.stack([s[i] for s in stacked]) for i in range(3))]
where the time goes in v6:
time: 640 us; the launch traced here: 630 us
  Pallas kernels  586 us (92%)
  local copies, waits for them, and re-layouts  27.9 us (4%)
  other arithmetic  14.1 us (2%)
    pallas_call x3, Pallas kernels, call_back(): pl.pallas_call(functools.partial(back_kernel, count, rows, tuple(inputs),...  302 us
    pallas_call x2, Pallas kernels, call_body(): pl.pallas_call(functools.partial(body_kernel, count, rows, late, n_next,...  207 us
    pallas_call x1, Pallas kernels, call_start(): pl.pallas_call(functools.partial(start_kernel, count, n, ahead, n_down),...  77.3 us

profile of v6, /device:TPU:0, one launch (start us, length us, event | category | flops | bytes accessed | tf_op | source)
XLA Modules:
  0.0 629.6 jit_solution(4109203932861744766)
XLA Ops:
  0.7 1.1 slice_bitcast_fusion.2
  2.2 0.8 maximum_bitcast_fusion.5.refs_5_
  3.5 0.8 maximum_bitcast_fusion.4.refs_1_
  4.4 0.7 bitcast_bitcast_fusion
  5.1 1.5 fusion.3
  6.6 0.6 reshape_squeeze.6
  7.2 0.4 copy.74
  7.6 0.6 fusion.5
  8.2 1.0 squeeze.36.refs_3_
  9.3 1.0 squeeze.37.refs_4_
  10.3 0.6 reshape_squeeze.7
  10.9 0.4 copy.73
  11.3 0.6 fusion.4
  11.9 1.0 squeeze.40.refs_7_
  12.9 1.0 squeeze.41.refs_8_
  13.9 77.3 %start.1 = (bf16[4,128,1536]{2,1,0:T(8,128)(2,1)}, bf16[2,2,2,2,2,48,896]{6,5,4,3,2,1,0:T(8,128)(2,1)}, bf16[2,2,2,2,2,48,384]{6,5,4,3,2,1,0:T(8,128)(2,1)}, bf1...) custom-call(bf16[128,1536]{1,0:T(8,128)(2,1)} %refs_0_.1, ...), custom_call_target="tpu_custom_call" | custom-call | tf_op jit(solution)/shard_map/start/pallas_call | solution.py:1288
  91.3 1.9 dynamic-slice_bitcast_fusion.refs_4_
  93.2 1.0 slice_convert_fusion
  94.5 0.6 fusion.9
  95.1 0.4 fusion
  95.5 1.6 fusion.2.refs_0_.refs_10_
  97.1 0.9 slice_bitcast_fusion
  98.0 117.2 %body_more.1 = (bf16[8,512,128]{2,1,0:T(8,128)(2,1)}, bf16[512,384]{1,0:T(8,128)(2,1)}, f32[512,128]{1,0:T(8,128)}, f32[128,1536]{1,0:T(8,128)}, f32[128,1536]{1...) custom-call(bf16[4,128,1536]{2,1,0:T(8,128)(2,1)} %fusion.2.refs_0_., ...), custom_call_target="tpu_custom_call" | custom-call | tf_op jit(solution)/shard_map/body_more/pallas_call | solution.py:1342
  215.3 0.8 convert_element_type.37.refs_10_
  216.0 89.7 %body.1 = (bf16[8,512,128]{2,1,0:T(8,128)(2,1)}, bf16[512,384]{1,0:T(8,128)(2,1)}, f32[512,128]{1,0:T(8,128)}, f32[128,1536]{1,0:T(8,128)}, f32[128,1536]{1,0:T(...) custom-call(bf16[4,128,1536]{2,1,0:T(8,128)(2,1)} %get-tuple-element, ...), custom_call_target="tpu_custom_call" | custom-call | tf_op jit(solution)/shard_map/body/pallas_call | solution.py:1342
  305.8 1.9 convert_element_type.38.refs_1_
  307.7 84.2 %back_first.1 = (f32[128,1536]{1,0:T(8,128)}, f32[1,1536]{1,0:T(1,128)}, bf16[1536,1024]{1,0:T(8,128)(2,1)}, bf16[1536,1024]{1,0:T(8,128)(2,1)}, bf16[512,768]{1...) custom-call(bf16[128,1536]{1,0:T(8,128)(2,1)} %get-tuple-element.84., ...), custom_call_target="tpu_custom_call" | custom-call | tf_op jit(solution)/shard_map/back_first/pallas_call | solution.py:1373
  392.0 110.4 %back_mid.1 = (f32[1,1536]{1,0:T(1,128)}, f32[128,1536]{1,0:T(8,128)}, f32[1,1536]{1,0:T(1,128)}, bf16[1536,1024]{1,0:T(8,128)(2,1)}, bf16[1536,1024]{1,0:T(8,12...) custom-call(bf16[512,768]{1,0:T(8,128)(2,1)} %get-tuple-element.97.r, ...), custom_call_target="tpu_custom_call" | custom-call | tf_op jit(solution)/shard_map/back_mid/pallas_call | solution.py:1373
  502.4 1.1 maximum_bitcast_fusion.2
  503.6 1.2 maximum_convert_fusion.1
  504.9 0.6 pad.9.refs_2_
  505.5 107.0 %back_last.1 = (bf16[128,1536]{1,0:T(8,128)(2,1)}, f32[16,128]{1,0:T(8,128)}, bf16[4,48,1024]{2,1,0:T(8,128)(2,1)}, bf16[4,48,1024]{2,1,0:T(8,128)(2,1)}, bf16[4...) custom-call(f32[128,1536]{1,0:T(8,128)} %get-tuple-element.110.refs_0_.refs_1_, ...), custom_call_target="tpu_custom_call" | custom-call | tf_op jit(solution)/shard_map/back_last/pallas_call | solution.py:1373
  612.5 1.3 reshape.189
  613.8 0.6 copy.78
  614.5 0.3 stack_reshape.12
  615.0 0.6 copy.77
  615.7 0.3 stack_reshape.13
  616.1 0.3 reshape.191
  616.3 0.6 copy.76
  616.9 0.3 stack_reshape.14
  617.5 0.6 copy.75
  618.1 0.3 stack_reshape.15
  618.8 4.1 copy.52
  622.9 0.9 maximum_convert_fusion.3
  624.9 1.1 maximum_convert_fusion.2
  626.0 1.0 convert_element_type.40
  626.9 1.2 slice.129
  628.2 1.0 convert_element_type.39
  (85 shorter events, 3.2 us)
Async XLA Ops:
  0.7 2.7 copy-start.19
  1.8 2.6 copy-start.11
  2.1 3.0 copy-start.1
  91.3 3.8 copy-start
  95.1 2.0 copy-start.2
  98.0 117.2 %copy-start.3 = (f32[128,1536]{1,0:T(8,128)S(1)}, f32[128,1536]{1,0:T(8,128)}, u32[]{:S(2)}) copy-start(f32[128,1536]{1,0:T(8,128)} %param.12) | copy-start | bytes 2359300
  391.9 111.6 %copy-start.12 = (bf16[128,768]{1,0:T(8,128)(2,1)S(1)}, bf16[128,768]{1,0:T(8,128)(2,1)}, u32[]{:S(2)}) copy-start(bf16[128,768]{1,0:T(8,128)(2,1)} %get-tuple-element.130) | copy-start | bytes 589828
  391.9 111.6 %copy-start.13 = (bf16[128,768]{1,0:T(8,128)(2,1)S(1)}, bf16[128,768]{1,0:T(8,128)(2,1)}, u32[]{:S(2)}) copy-start(bf16[128,768]{1,0:T(8,128)(2,1)} %get-tuple-element.131) | copy-start | bytes 589828
  502.4 2.4 copy-start.16
  502.4 2.4 copy-start.17
  502.4 2.4 copy-start.18
  612.5 2.2 copy-start.8
  614.5 1.6 copy-start.7
  615.7 1.6 copy-start.6
  618.7 4.1 copy-start.15
  618.7 4.1 copy-start.14
  618.7 5.0 copy-start.5
  622.8 1.5 copy-start.4
  624.3 1.7 copy-start.10
  624.5 3.7 copy-start.9

commit v7 on v6

--- a/solution.py
+++ b/solution.py
@@ -162,8 +162,8 @@
 
 
 class Gather:
-    def __init__(self, net, block, full, ranks=True):
-        self.net, self.block, self.full, self.ranks = net, block, full, ranks
+    def __init__(self, net, block, full, ranks=True, ahead=None):
+        self.net, self.block, self.full, self.ranks, self.ahead = net, block, full, ranks, ahead
 
     def slot(self, a, core, zh):
         if self.ranks:
@@ -178,10 +178,18 @@
     def begin(self):
         net, p = self.net, self.net.place
         mine = self.slot(p.a, p.core, p.zh)
-        self.across = net.remote(self.block, mine, p.zh_peer)
-        self.near = [net.remote(self.block, mine, o[0]) for o in p.others]
+        self.own = [net.here(self.block, mine)]
         self.cores = [net.remote(self.block, mine, p.core_peer)]
-        self.own = net.here(self.block, mine)
+        if self.ahead is None:
+            self.across = net.remote(self.block, mine, p.zh_peer)
+            self.near = [net.remote(self.block, mine, o[0]) for o in p.others]
+            return
+        got = self.slot(p.a, p.core, 1 - p.zh)
+        self.far = [net.remote(self.ahead.at[0], got, o[0]) for o in p.others]
+        self.cores.append(net.remote(self.ahead.at[0], got, p.core_peer))
+        self.own.append(net.here(self.ahead.at[0], got))
+        for k, other in enumerate(p.others):
+            self.own.append(net.here(self.ahead.at[k + 1], self.slot(other[2], p.core, p.zh)))
 
     def middle(self):
         net, p = self.net, self.net.place
@@ -192,15 +200,31 @@
 
     def final(self):
         net, p = self.net, self.net.place
+        for copy in self.own:
+            copy.wait()
         for k, other in enumerate(p.others):
-            self.near[k].wait_recv()
+            if self.ahead is None:
+                self.near[k].wait_recv()
             self.far[k].wait_recv()
             got = self.column(other[2], p.core)
             self.cores.append(net.remote(got, got, p.core_peer))
 
     def done(self):
-        self.own.wait()
         for copy in self.cores:
+            copy.wait_recv()
+
+
+class Ahead:
+    def __init__(self, net, block, got):
+        self.net, self.block, self.got = net, block, got
+
+    def begin(self):
+        net, p = self.net, self.net.place
+        self.copies = [net.remote(self.block, self.got.at[0], p.zh_peer)]
+        self.copies += [net.remote(self.block, self.got.at[k + 1], o[0]) for k, o in enumerate(p.others)]
+
+    def done(self):
+        for copy in self.copies:
             copy.wait_recv()
 
 
@@ -636,39 +660,41 @@
         target[tuple(reversed(index))] = value[block * rows : (block + 1) * rows].astype(BF16)
 
 
-def start_kernel(count, n, ahead, n_down, *refs):
+def start_kernel(count, n, n_later, n_ahead, *refs):
     refs = Refs(refs)
     (tokens,) = refs.take(1)
-    pieces, later, downs = refs.take(n), refs.take(ahead), refs.take(n_down)
+    pieces, later = refs.take(n), refs.take(n_later)
     (all_tokens,) = refs.take(1)
-    full, blocks_later, downs_full = refs.take(n), refs.take(ahead), refs.take(n_down)
+    full, blocks_later, got_ahead = refs.take(n), refs.take(n_later), refs.take(n_ahead)
     (land,) = refs.take(1)
     blocks = refs.take(n)
     send, recv, local = refs.take(3)
     place = Place(count)
     net = Net(place, send, recv, local)
     shares = [Share(net, pieces[i], blocks[i]) for i in range(n)]
-    shares_later = [Share(net, later[i], blocks_later[i]) for i in range(ahead)]
+    shares_later = [Share(net, later[i], blocks_later[i]) for i in range(n_later)]
     gathers = [Gather(net, blocks[i], full[i]) for i in range(n)]
-    gathers += [Gather(net, downs[i], downs_full[i], ranks=False) for i in range(n_down)]
+    aheads = [Ahead(net, blocks_later[i], got_ahead[i]) for i in range(n_ahead)]
     swap = Swap(net, tokens, land.at[place.zh * 2 + place.zl])
     place.greet(True, True)
     shares[0].start()
     swap.start()
-    for share in shares[1:]:
+    for share in shares[1:] + shares_later[:n_ahead]:
         share.start()
     for i in range(2):
         shares[i].wait()
         gathers[i].begin()
     swap.wait()
     spreads = Spread(net, land)
-    for i in range(2, len(gathers)):
-        if i < n:
-            shares[i].wait()
+    for i in range(2, n):
+        shares[i].wait()
         gathers[i].begin()
+    for i in range(n_ahead):
+        shares_later[i].wait()
+        aheads[i].begin()
     arrivals = spreads.arrivals()
     next(arrivals)
-    for share in shares_later:
+    for share in shares_later[n_ahead:]:
         share.start()
     gathers[0].middle()
     gathers[1].middle()
@@ -676,22 +702,23 @@
         pass
     keep = net.here(land, all_tokens)
     gathers[0].final()
-    for i in range(2, len(gathers)):
+    for i in range(2, n):
         gathers[i].middle()
         gathers[i - 1].final()
     gathers[-1].final()
-    for gather in gathers:
+    for gather in gathers + aheads:
         gather.done()
-    for share in shares_later:
+    for share in shares_later[n_ahead:]:
         share.wait()
     keep.wait()
     net.finish()
 
 
-def body_kernel(count, rows, late, n_next, plan, *refs):
+def body_kernel(count, rows, late, started, n_next, n_ahead, plan, *refs):
     refs = Refs(refs)
     n1_hbm, wq_hbm, cos_ref, sin_ref, h_ref, gain_ref, wo_hbm = refs.take(7)
     inner_hbm = refs.take(3)
+    ahead_hbm = [refs.take(1)[0] if started[i] else None for i in range(3)]
     if n_next:
         (gain_next,) = refs.take(1)
         blocks = refs.take(n_next)
@@ -722,14 +749,14 @@
     loads, weights = [], []
     for i in range(3):
         if late[i]:
-            jobs[("gate", "up", "down")[i]] = Gather(net, inner_hbm[i], inner[i], ranks=i < 2)
+            jobs[("gate", "up", "down")[i]] = Gather(net, inner_hbm[i], inner[i], i < 2, ahead_hbm[i])
             loads.append(None)
         else:
             loads.append(net.here(inner_hbm[i], inner[i]))
         weights.append(inner[i].reshape((hidden, width) if i == 2 else (width, hidden)) if late[i] else inner[i])
     wg, wu, wd = weights
     for i in range(n_next):
-        jobs[i] = Gather(net, blocks[i], full[i])
+        jobs[i] = (Ahead if i >= n_next - n_ahead else Gather)(net, blocks[i], full[i])
     if not n_next:
         jobs["swap"] = Swap(net, swap_src, swap_dst)
     peers = place.peers
@@ -836,11 +863,11 @@
 
 
 def plan_late(j):
-    gate, down = j["gate"], j["down"]
+    gate, up, down = j["gate"], j["up"], j["down"]
     return [
-        [gate.begin],
+        [gate.begin, up.begin],
         [gate.middle, down.begin],
-        [gate.final],
+        [up.final, gate.final],
         [down.middle, j[0].begin, j[1].begin],
         [down.final],
         [],
@@ -848,19 +875,15 @@
         [j[0].middle],
         [j[0].final, j[1].middle],
         [j[2].begin, j[1].final],
-        [],
-        [],
-        [j[2].middle],
-        [j[2].final],
     ]
 
 
 def plan_late_end(j):
-    up, down = j["up"], j["down"]
+    gate, up, down = j["gate"], j["up"], j["down"]
     return [
-        [up.begin],
+        [up.begin, gate.begin],
         [up.middle, down.begin],
-        [up.final],
+        [gate.final, up.final],
         [down.middle],
         [down.final],
         [],
@@ -870,17 +893,18 @@
 
 
 def plan_early(j):
+    down = j["down"]
     return [
-        [j[0].begin],
-        [j[1].begin],
-        [j[0].middle, j[1].middle, j[2].begin],
+        [down.begin],
+        [down.middle, j[0].begin],
+        [],
+        [down.final, j[1].begin, j[2].begin],
+        [j[0].middle],
+        [],
         [],
         [j[0].final],
-        [j[1].final],
-        [j[2].middle],
-        [],
-        [j[3].begin, j[2].final],
-        [],
+        [j[1].middle, j[2].middle],
+        [j[3].begin, j[1].final, j[2].final],
         [],
         [],
         [j[3].middle],
@@ -1278,33 +1302,36 @@
     return (count, 2, 2, 2, 2) + tuple(tail)
 
 
-def call_start(count, tokens, pieces, later, downs):
+def call_start(count, tokens, pieces, later, n_ahead):
     rows, width = tokens.shape
-    n, ahead, n_down = len(pieces), len(later), len(downs)
+    n, n_later = len(pieces), len(later)
     outs = [like((RANKS, rows, width))]
     outs += [like(full_shape(count, p.shape[1:])) for p in pieces]
     outs += [like((2, 2) + p.shape[1:]) for p in later]
-    outs += [like((count, 2, 2) + d.shape) for d in downs]
+    outs += [like((count, 2, 2) + p.shape[1:]) for p in later[:n_ahead]]
     got = pl.pallas_call(
-        functools.partial(start_kernel, count, n, ahead, n_down),
+        functools.partial(start_kernel, count, n, n_later, n_ahead),
         out_shape=outs,
-        in_specs=[AN] * len(outs),
+        in_specs=[AN] * (1 + n + n_later),
         out_specs=[AN] * len(outs),
         scratch_shapes=[pltpu.VMEM((RANKS, rows, width), BF16)]
         + [pltpu.VMEM((2, 2) + p.shape[1:], BF16) for p in pieces]
         + sems(count),
         compiler_params=params(1),
         name="start",
-    )(tokens, *pieces, *later, *downs)
-    cut = n + 1 + ahead
-    return got[0], [flat(f) for f in got[1 : n + 1]], got[n + 1 : cut], [flat(d) for d in got[cut:]]
+    )(tokens, *pieces, *later)
+    cut = n + 1 + n_later
+    return got[0], [flat(f) for f in got[1 : n + 1]], got[n + 1 : cut], got[cut:]
 
 
 def flat(value):
     return value.reshape(-1, value.shape[-1])
 
 
-def call_body(count, n1, wq, tables, h, gain, wo, inner, late, plan, gain_next=None, blocks=(), swap=None):
+def call_body(
+    count, n1, wq, tables, h, gain, wo, inner, late, ahead, plan, gain_next=None, blocks=(), n_ahead=0, swap=None
+):
+    started = tuple(value is not None for value in ahead)
     rows, width = h.shape
     tall = RANKS * rows
     hidden = inner[0].shape[-1]
@@ -1334,15 +1361,19 @@
     n_state = len(outs)
     outs += [like(shapes[i]) for i in range(3) if late[i]]
     if n_next:
-        outs += [like((RANKS, rows, width))] + [like(full_shape(count, b.shape[2:])) for b in blocks]
+        outs += [like((RANKS, rows, width))]
+        outs += [like(full_shape(count, b.shape[2:])) for b in blocks[: n_next - n_ahead]]
+        outs += [like((count,) + b.shape) for b in blocks[n_next - n_ahead :]]
         extra = (gain_next, *blocks)
     else:
         outs += [like(swap.shape)]
         extra = (swap,)
     got = pl.pallas_call(
-        functools.partial(body_kernel, count, rows, late, n_next, plan),
+        functools.partial(body_kernel, count, rows, late, started, n_next, n_ahead, plan),
         out_shape=outs,
-        in_specs=[AN, AN, VM, VM, VM, VM, AN, AN, AN, AN] + ([VM] + [AN] * n_next if n_next else [AN]),
+        in_specs=[AN, AN, VM, VM, VM, VM, AN, AN, AN, AN]
+        + [AN] * sum(started)
+        + ([VM] + [AN] * n_next if n_next else [AN]),
         out_specs=[VM] * (n_state - 1) + [AN] * (len(outs) - n_state + 1),
         scratch_shapes=[
             four,
@@ -1355,11 +1386,12 @@
         + sems(count),
         compiler_params=params(2 if n_next else 3),
         name="body_more" if n_next else "body",
-    )(n1, wq, *tables, h, gain, wo, *inner, *extra)
+    )(n1, wq, *tables, h, gain, wo, *inner, *[value for value in ahead if value is not None], *extra)
     got = list(got)
     state, rest = got[:n_state], got[n_state:]
     inner = [flat(rest.pop(0)) if late[i] else inner[i] for i in range(3)]
-    return state, inner, rest[0], [flat(f) for f in rest[1:]]
+    rest, last = rest[: len(rest) - n_ahead], rest[len(rest) - n_ahead :]
+    return state, inner, rest[0], [flat(f) for f in rest[1:]], last
 
 
 def call_back(name, count, rows, inputs, outputs, scratch, parts, made, kinds, plan, collective_id):
@@ -1400,38 +1432,40 @@
 
     packed = [pack_weights(w_qkv, w_out, w_gate_up, gains, count, layer) for layer in range(LAYERS)]
     whole_rows = w_qkv.shape[1] % 16 == 0
+    none = (None, None, None)
     if whole_rows:
         head, out, gate, up = packed[0]
-        now, later, downs = (head, out, up), (gate, *packed[1]), ()
+        now, later, n_ahead = (head, out), (up, gate, *packed[1]), 1
     else:
-        now, later, downs = packed[0], packed[1], (w_down[0],)
-    all_tokens, full, blocks, downs = call_start(count, tokens, now, later, downs)
+        now, later, n_ahead = packed[0], packed[1], 0
+    all_tokens, full, blocks, ahead = call_start(count, tokens, now, later, n_ahead)
     gain_rows = full[0][:, -GAIN_COLS:][:, : 2 * LAYERS].astype(F32).T
     gain = lambda layer, which: gain_rows[2 * layer + which][None]
     h = lax.dynamic_index_in_dim(all_tokens, rank, 0, keepdims=False)
     n1 = norm_rows(all_tokens.astype(F32), gain(0, 0))
     if whole_rows:
-        inner, late, plan = (blocks[0], full[2], w_down[0]), (True, False, True), plan_late
-        *blocks, last_up = blocks[1:]
+        up, gate, *blocks, last_up = blocks
+        inner, late, ahead, plan = (gate, up, w_down[0]), (True, True, True), (None, ahead[0], None), plan_late
     else:
-        inner, late, plan = (*full[2:], *downs), (False, False, False), plan_early
+        inner, late, ahead, plan = (*full[2:], w_down[0]), (False, False, True), none, plan_early
 
     records = []
     for layer in range(LAYERS):
         wq, wo = full[:2]
         if layer + 1 < LAYERS:
-            state, inner, n1_next, full = call_body(
-                count, n1, wq, tables, h, gain(layer, 1), wo, inner, late, plan, gain(layer + 1, 0), blocks
+            state, inner, n1_next, full, last_got = call_body(
+                count, n1, wq, tables, h, gain(layer, 1), wo, inner, late, ahead, plan,
+                gain(layer + 1, 0), blocks, n_ahead,
             )
             if whole_rows:
-                late, plan = (False, True, True), plan_late_end
-                next_inner = (full[2], last_up, w_down[layer + 1])
+                late, ahead, plan = (True, True, True), (last_got[0], None, None), plan_late_end
+                next_inner = (blocks[-1], last_up, w_down[layer + 1])
             else:
                 late, plan = (False, False, True), plan_end
                 next_inner = (*full[2:], w_down[layer + 1])
         else:
-            state, inner, g, _ = call_body(
-                count, n1, wq, tables, h, gain(layer, 1), wo, inner, late, plan,
+            state, inner, g, _, _ = call_body(
+                count, n1, wq, tables, h, gain(layer, 1), wo, inner, late, ahead, plan,
                 swap=cotangent.astype(BF16),
             )
             n1_next = None

time: 640 us -> 615 us (0.961)
  Pallas kernels: 586 us -> 564 us
    pallas_call x3, Pallas kernels: 284 us -> 267 us  [the longest x2 197 us: call_body(): pl.pallas_call(functools.partial(body_kernel, count, rows, late, started,...]
where the time goes in v7:
time: 615 us; the launch traced here: 608 us
  Pallas kernels  564 us (92%)
  local copies, waits for them, and re-layouts  27.9 us (5%)
  other arithmetic  14.1 us (2%)
    pallas_call x3, Pallas kernels, call_back(): pl.pallas_call(functools.partial(back_kernel, count, rows, tuple(inputs),...  297 us
    pallas_call x2, Pallas kernels, call_body(): pl.pallas_call(functools.partial(body_kernel, count, rows, late, started,...  197 us
    pallas_call x1, Pallas kernels, call_start(): pl.pallas_call(functools.partial(start_kernel, count, n, n_later, n_ahead...  70.8 us

profile of v7, /device:TPU:0, one launch (start us, length us, event | category | flops | bytes accessed | tf_op | source)
XLA Modules:
  0.0 607.7 jit_solution(4359496523083529758)
XLA Ops:
  0.7 1.1 slice_bitcast_fusion.2
  2.2 0.8 maximum_bitcast_fusion.5.refs_5_
  3.5 0.8 maximum_bitcast_fusion.4.refs_1_
  4.4 0.8 bitcast_bitcast_fusion
  5.1 1.5 fusion.3
  6.6 0.6 reshape_squeeze.6
  7.2 0.4 copy.74
  7.7 0.6 fusion.5
  8.3 1.0 squeeze.36.refs_3_
  9.3 1.0 squeeze.37.refs_4_
  10.3 0.6 reshape_squeeze.7
  10.9 0.4 copy.73
  11.3 0.6 fusion.4
  11.9 1.0 squeeze.40.refs_7_
  12.9 1.0 squeeze.41.refs_8_
  13.9 70.8 %start.1 = (bf16[4,128,1536]{2,1,0:T(8,128)(2,1)}, bf16[2,2,2,2,2,48,896]{6,5,4,3,2,1,0:T(8,128)(2,1)}, bf16[2,2,2,2,2,48,384]{6,5,4,3,2,1,0:T(8,128)(2,1)}, bf1...) custom-call(bf16[128,1536]{1,0:T(8,128)(2,1)} %refs_0_.1, ...), custom_call_target="tpu_custom_call" | custom-call | tf_op jit(solution)/shard_map/start/pallas_call | solution.py:1312
  84.7 1.9 dynamic-slice_bitcast_fusion.refs_4_
  86.6 1.0 slice_convert_fusion
  87.9 0.6 fusion.9
  88.6 0.4 fusion
  89.0 1.6 fusion.2.refs_0_.refs_10_
  90.5 0.9 slice_bitcast_fusion
  91.5 116.8 %body_more.1 = (bf16[8,512,128]{2,1,0:T(8,128)(2,1)}, bf16[512,384]{1,0:T(8,128)(2,1)}, f32[512,128]{1,0:T(8,128)}, f32[128,1536]{1,0:T(8,128)}, f32[128,1536]{1...) custom-call(bf16[4,128,1536]{2,1,0:T(8,128)(2,1)} %fusion.2.refs_0_., ...), custom_call_target="tpu_custom_call" | custom-call | tf_op jit(solution)/shard_map/body_more/pallas_call | solution.py:1371
  208.3 0.8 convert_element_type.37.refs_11_
  209.1 79.9 %body.1 = (bf16[8,512,128]{2,1,0:T(8,128)(2,1)}, bf16[512,384]{1,0:T(8,128)(2,1)}, f32[512,128]{1,0:T(8,128)}, f32[128,1536]{1,0:T(8,128)}, f32[128,1536]{1,0:T(...) custom-call(bf16[4,128,1536]{2,1,0:T(8,128)(2,1)} %get-tuple-element, ...), custom_call_target="tpu_custom_call" | custom-call | tf_op jit(solution)/shard_map/body/pallas_call | solution.py:1371
  289.0 1.9 convert_element_type.38.refs_1_
  290.9 78.2 %back_first.1 = (f32[128,1536]{1,0:T(8,128)}, f32[1,1536]{1,0:T(1,128)}, bf16[1536,1024]{1,0:T(8,128)(2,1)}, bf16[1536,1024]{1,0:T(8,128)(2,1)}, bf16[512,768]{1...) custom-call(bf16[128,1536]{1,0:T(8,128)(2,1)} %get-tuple-element.88., ...), custom_call_target="tpu_custom_call" | custom-call | tf_op jit(solution)/shard_map/back_first/pallas_call | solution.py:1405
  369.1 106.1 %back_mid.1 = (f32[1,1536]{1,0:T(1,128)}, f32[128,1536]{1,0:T(8,128)}, f32[1,1536]{1,0:T(1,128)}, bf16[1536,1024]{1,0:T(8,128)(2,1)}, bf16[1536,1024]{1,0:T(8,12...) custom-call(bf16[512,768]{1,0:T(8,128)(2,1)} %get-tuple-element.102., ...), custom_call_target="tpu_custom_call" | custom-call | tf_op jit(solution)/shard_map/back_mid/pallas_call | solution.py:1405
  475.3 1.1 maximum_bitcast_fusion.2
  476.4 1.2 maximum_convert_fusion.1
  477.8 0.6 pad.9.refs_2_
  478.4 112.2 %back_last.1 = (bf16[128,1536]{1,0:T(8,128)(2,1)}, f32[16,128]{1,0:T(8,128)}, bf16[4,48,1024]{2,1,0:T(8,128)(2,1)}, bf16[4,48,1024]{2,1,0:T(8,128)(2,1)}, bf16[4...) custom-call(f32[128,1536]{1,0:T(8,128)} %get-tuple-element.116.refs_0_.refs_1_, ...), custom_call_target="tpu_custom_call" | custom-call | tf_op jit(solution)/shard_map/back_last/pallas_call | solution.py:1405
  590.7 1.3 reshape.189
  592.0 0.6 copy.78
  592.6 0.3 stack_reshape.12
  593.2 0.6 copy.77
  593.8 0.3 stack_reshape.13
  594.2 0.3 reshape.191
  594.4 0.6 copy.76
  595.1 0.3 stack_reshape.14
  595.6 0.6 copy.75
  596.3 0.3 stack_reshape.15
  596.9 4.1 copy.52
  601.0 0.9 maximum_convert_fusion.3
  603.0 1.1 maximum_convert_fusion.2
  604.1 1.0 convert_element_type.40
  605.1 1.3 slice.129
  606.3 1.0 convert_element_type.39
  (85 shorter events, 3.2 us)
Async XLA Ops:
  0.7 2.7 copy-start.19
  1.8 2.6 copy-start.11
  2.1 3.0 copy-start.1
  84.7 3.8 copy-start
  88.6 2.0 copy-start.2
  91.5 116.9 %copy-start.3 = (f32[128,1536]{1,0:T(8,128)S(1)}, f32[128,1536]{1,0:T(8,128)}, u32[]{:S(2)}) copy-start(f32[128,1536]{1,0:T(8,128)} %param.12) | copy-start | bytes 2359300
  369.1 107.2 %copy-start.12 = (bf16[128,768]{1,0:T(8,128)(2,1)S(1)}, bf16[128,768]{1,0:T(8,128)(2,1)}, u32[]{:S(2)}) copy-start(bf16[128,768]{1,0:T(8,128)(2,1)} %get-tuple-element.136) | copy-start | bytes 589828
  369.1 107.2 %copy-start.13 = (bf16[128,768]{1,0:T(8,128)(2,1)S(1)}, bf16[128,768]{1,0:T(8,128)(2,1)}, u32[]{:S(2)}) copy-start(bf16[128,768]{1,0:T(8,128)(2,1)} %get-tuple-element.137) | copy-start | bytes 589828
  475.3 2.4 copy-start.16
  475.3 2.4 copy-start.17
  475.3 2.4 copy-start.18
  590.6 2.2 copy-start.8
  592.6 1.6 copy-start.7
  593.8 1.6 copy-start.6
  596.8 4.1 copy-start.15
  596.9 4.1 copy-start.14
  596.9 5.0 copy-start.5
  601.0 1.5 copy-start.4
  602.4 1.7 copy-start.10
  602.6 3.7 copy-start.9

commit v8 on v7

--- a/solution.py
+++ b/solution.py
@@ -104,7 +104,7 @@
             copy.wait_send()
 
 
-REMOTE_SEMS, LOCAL_SEMS = 128, 48
+REMOTE_SEMS, LOCAL_SEMS = 128, 64
 
 
 def sems(count=2):
@@ -666,7 +666,7 @@
     pieces, later = refs.take(n), refs.take(n_later)
     (all_tokens,) = refs.take(1)
     full, blocks_later, got_ahead = refs.take(n), refs.take(n_later), refs.take(n_ahead)
-    (land,) = refs.take(1)
+    own_tokens, land = refs.take(2)
     blocks = refs.take(n)
     send, recv, local = refs.take(3)
     place = Place(count)
@@ -686,6 +686,7 @@
         gathers[i].begin()
     swap.wait()
     spreads = Spread(net, land)
+    keep_own = net.here(land.at[place.rank], own_tokens)
     for i in range(2, n):
         shares[i].wait()
         gathers[i].begin()
@@ -710,6 +711,7 @@
         gather.done()
     for share in shares_later[n_ahead:]:
         share.wait()
+    keep_own.wait()
     keep.wait()
     net.finish()
 
@@ -724,7 +726,7 @@
         blocks = refs.take(n_next)
     else:
         (swap_src,) = refs.take(1)
-    heads, o_ref, lse_ref, h1_ref, hn_ref, gate_ref, up_ref, u_ref, ng_hbm = refs.take(9)
+    heads, o_ref, lse_ref, h1_ref, hn_ref, hb_ref, gate_ref, up_ref, u_ref, ng_hbm = refs.take(10)
     late_out = [refs.take(1)[0] if late[i] else None for i in range(3)]
     if n_next:
         (nn_hbm,) = refs.take(1)
@@ -843,6 +845,7 @@
     tick()
     hn = second.result(hn_ref[...])
     hn_ref[...] = hn
+    hb_ref[...] = hn.astype(BF16)
     if n_next:
         land_q[place.rank] = norm_rows(hn, gain_next[...])
         third = EvenSpread(net, land_q)
@@ -1030,7 +1033,7 @@
             part.reshape(hidden, cols)[...] = made.astype(BF16)
         down_made()
         for m in range(width // tile):
-            emit(r["n2"][:, m * tile : (m + 1) * tile], r["dgu"][...], [r["g_gate"], r["g_up"]], m)
+            emit(r["n2"][:, m * tile : (m + 1) * tile], r["dgu"][...], [r[name] for name in INNER_GRADS], m)
         return copies[-2] + copies[-1]
 
     def attention(self, r, tick, ready):
@@ -1057,7 +1060,7 @@
         close_keys(rows, r["dkv"], r["cos"], r["sin"], r["dqkv"])
 
 
-ATTEND = ("wo", "heads", "o", "lse", "cos", "sin")
+INNER_GRADS = ("g_gate_a", "g_gate_b", "g_up_a", "g_up_b")
 
 
 def back_kernel(count, rows, names, out_names, scratch_names, n_parts, kinds, plan, *refs):
@@ -1185,10 +1188,11 @@
 
 
 def plan_finish(j, s, swap):
+    ga, gb, ua, ub, out, qkv = j
     return [
-        s.along_a, j[2].along_a, j[3].along_a, j[1].along_zh, j[0].among_ranks, s.along_zh, j[2].along_zh,
-        s.among_ranks, j[3].along_zh, swap.start, j[1].among_ranks, j[0].done, j[2].among_ranks, s.done, j[1].done,
-        j[3].among_ranks, j[2].done, j[3].done,
+        s.along_a, ub.along_zh, out.along_a, qkv.along_a, ga.among_ranks, s.along_zh, out.along_zh, gb.among_ranks,
+        s.among_ranks, ua.among_ranks, swap.start, ub.among_ranks, ga.done, qkv.along_zh, gb.done, out.among_ranks,
+        s.done, ua.done, ub.done, out.done, qkv.among_ranks, qkv.done,
     ]
 
 
@@ -1214,35 +1218,35 @@
 
 
 def plan_middle(j):
-    gate, up, out, qkv, da, db = j
+    ga, gb, ua, ub, out, qkv, da, db = j
     return [
-        [gate.begin, up.begin, out.begin, qkv.begin],
-        [gate.along_a],
-        [up.along_a],
-        [],
+        [ga.begin, gb.begin, ua.begin, ub.begin, out.begin, qkv.begin],
+        [ga.along_a],
+        [gb.along_a, ga.along_zh],
+        [ua.along_a],
+        [gb.along_zh],
+        [ub.along_a, ua.along_zh],
         [out.along_a],
-        [gate.along_zh],
-        [qkv.along_a],
-        [],
-        [up.along_zh],
-        [da.begin, db.begin],
-        [gate.among_ranks, da.along_a],
-        [out.along_zh, db.along_a, qkv.along_zh, up.among_ranks, out.among_ranks, gate.done, da.along_zh, up.done],
+        [ga.among_ranks],
+        [ub.along_zh, qkv.along_a],
+        [da.begin, db.begin, gb.among_ranks],
+        [out.along_zh, ua.among_ranks, da.along_a],
+        [db.along_a, ub.among_ranks, qkv.along_zh, out.among_ranks, ga.done, gb.done, da.along_zh, ua.done, ub.done],
         [qkv.among_ranks, db.along_zh, out.done, qkv.done, da.among_ranks, db.among_ranks],
     ]
 
 
 def plan_last(j):
-    gate, up, out, qkv = j
+    ga, gb, ua, ub, out, qkv = j
     return [
-        [gate.begin, up.begin],
-        [gate.along_a],
-        [],
-        [up.along_a],
-        [],
-        [gate.along_zh],
-        [],
-        [out.begin, qkv.begin],
+        [ga.begin, gb.begin, ua.begin, ub.begin],
+        [ga.along_a],
+        [gb.along_a],
+        [ga.along_zh, ua.along_a],
+        [],
+        [gb.along_zh, ub.along_a],
+        [],
+        [out.begin, qkv.begin, ua.along_zh],
     ]
 
 
@@ -1309,6 +1313,7 @@
     outs += [like(full_shape(count, p.shape[1:])) for p in pieces]
     outs += [like((2, 2) + p.shape[1:]) for p in later]
     outs += [like((count, 2, 2) + p.shape[1:]) for p in later[:n_ahead]]
+    outs += [like((rows, width))]
     got = pl.pallas_call(
         functools.partial(start_kernel, count, n, n_later, n_ahead),
         out_shape=outs,
@@ -1321,7 +1326,7 @@
         name="start",
     )(tokens, *pieces, *later)
     cut = n + 1 + n_later
-    return got[0], [flat(f) for f in got[1 : n + 1]], got[n + 1 : cut], got[cut:]
+    return got[0], got[-1], [flat(f) for f in got[1 : n + 1]], got[n + 1 : cut], got[cut:-1]
 
 
 def flat(value):
@@ -1353,6 +1358,7 @@
         like((tall, 128), F32),
         like((rows, width), F32),
         like((rows, width), F32),
+        like((rows, width)),
         like((tall, hidden)),
         like((tall, hidden)),
         like((tall, hidden)),
@@ -1422,7 +1428,6 @@
     length = RANKS * rows
     hidden = w_gate_up.shape[-1] // RANKS
     tall = lambda value: value.reshape(length, width)
-    rank = lax.rem(lax.div(lax.axis_index("dp"), 2), 2) * 2 + lax.rem(lax.axis_index("ctx"), 2)
 
     swap = lambda value: lax.ppermute(value, ("dp", "ctx"), swap_pairs(dp_size, ctx_size))
     tie = lax.optimization_barrier
@@ -1438,10 +1443,9 @@
         now, later, n_ahead = (head, out), (up, gate, *packed[1]), 1
     else:
         now, later, n_ahead = packed[0], packed[1], 0
-    all_tokens, full, blocks, ahead = call_start(count, tokens, now, later, n_ahead)
+    all_tokens, h, full, blocks, ahead = call_start(count, tokens, now, later, n_ahead)
     gain_rows = full[0][:, -GAIN_COLS:][:, : 2 * LAYERS].astype(F32).T
     gain = lambda layer, which: gain_rows[2 * layer + which][None]
-    h = lax.dynamic_index_in_dim(all_tokens, rank, 0, keepdims=False)
     n1 = norm_rows(all_tokens.astype(F32), gain(0, 0))
     if whole_rows:
         up, gate, *blocks, last_up = blocks
@@ -1469,7 +1473,7 @@
                 swap=cotangent.astype(BF16),
             )
             n1_next = None
-        heads, mixed, lse, h1, h_next, gate, up, u, n2 = state
+        heads, mixed, lse, h1, h_next, h_round, gate, up, u, n2 = state
         records.append(dict(
             hin=h, n1=n1, heads=heads, o=mixed, lse=lse, h1=h1, n2=tall(n2), gate=gate, up=up, u=u,
             wq=wq, wo=wo, wgate=inner[0], wup=inner[1], wd=inner[2],
@@ -1495,8 +1499,7 @@
     inner_out = dict(
         gh=(like((rows, width), F32), VM),
         gg=(like((1, width), F32), VM),
-        g_gate=(like((width, hidden)), AN),
-        g_up=(like((width, hidden)), AN),
+        **{name: (like((width, hidden // 2)), AN) for name in INNER_GRADS},
     )
     shape_d = (count, 2, 2, w_down.shape[1], width // 2)
     inner_scratch = dict(
@@ -1536,7 +1539,7 @@
 
     first, down_1 = call_back(
         "back_first", count, rows,
-        dict(g=(g, VM), swap_src=(h.astype(BF16), AN), **inner_in(1), **attention_in(1)),
+        dict(g=(g, VM), swap_src=(h_round, AN), **inner_in(1), **attention_in(1)),
         dict(
             inner_out,
             dqkv=(like((length, cols)), VM),
@@ -1546,14 +1549,14 @@
         ),
         dict(**inner_scratch, **attention_scratch), [], [shape_d] * 2, (False,) * 2, plan_first, 4,
     )
-    parts_of = lambda got: [shape7(got["g_gate"]), shape7(got["g_up"])]
+    parts_of = lambda got: [shape7(got[name]) for name in INNER_GRADS]
     middle, grads_1 = call_back(
         "back_mid", count, rows,
         dict(dqkv=(first["dqkv"], VM), ghin=(first["gh"], VM), **enter_in(1), **inner_in(0)),
         dict(ggin=(like((1, width), F32), VM), **inner_out),
         dict(gnew=row_f32, **enter_scratch, **inner_scratch),
         parts_of(first) + [shape7(first["g_out"]), shape7(first["g_qkv"])],
-        [shape_d] * 2, (True,) * 4 + (False,) * 2, plan_middle, 5,
+        [shape_d] * 2, (True,) * 6 + (False,) * 2, plan_middle, 5,
     )
     others = jnp.concatenate([jnp.zeros((1, width), F32), middle["gg"], middle["ggin"], first["gg"]], axis=0)
     others = jnp.pad(others, ((0, 16 - 2 * LAYERS), (0, 0)))
@@ -1574,14 +1577,15 @@
             **enter_scratch,
             **attention_scratch,
         ),
-        parts_of(middle), [shape_o, shape_q], (True,) * 4, plan_last, 6,
+        parts_of(middle), [shape_o, shape_q], (True,) * 6, plan_last, 6,
     )
     out_act, grad_tokens, gains_sum = first["swap_dst"], final["swap_dst"], final["gains_out"]
-    grads = (grads_0, grads_1[:4])
-    downs = (grads_1[4:], down_1)
+    grads = (grads_0, grads_1[:6])
+    downs = (grads_1[6:], down_1)
     piece = gains.shape[-1]
     grad_gains = gains_sum[: 2 * LAYERS, :piece].reshape(LAYERS, 2, piece)
-    stacked = [unpack_grads(q, o, gate, up, count) for gate, up, o, q in grads]
+    beside = lambda *halves: jnp.concatenate(halves, axis=2)
+    stacked = [unpack_grads(q, o, beside(ga, gb), beside(ua, ub), count) for ga, gb, ua, ub, o, q in grads]
     s_qkv, s_out, s_gu = (jnp.stack([s[i] for s in stacked]) for i in range(3))
     s_down = jnp.stack([jnp.concatenate(d, axis=1) for d in downs])
     wide = lambda value: value.astype(F32)

time: 615 us -> 607 us (0.987)
  no operation moved by 1% of the time
where the time goes in v8:
time: 607 us; the launch traced here: 599 us
  Pallas kernels  559 us (92%)
  local copies, waits for them, and re-layouts  25 us (4%)
  other arithmetic  13.4 us (2%)
    pallas_call x3, Pallas kernels, call_back(): pl.pallas_call(functools.partial(back_kernel, count, rows, tuple(inputs),...  291 us
    pallas_call x2, Pallas kernels, call_body(): pl.pallas_call(functools.partial(body_kernel, count, rows, late, started,...  197 us
    pallas_call x1, Pallas kernels, call_start(): pl.pallas_call(functools.partial(start_kernel, count, n, n_later, n_ahead...  70.9 us

profile of v8, /device:TPU:0, one launch (start us, length us, event | category | flops | bytes accessed | tf_op | source)
XLA Modules:
  0.0 599.2 jit_solution(7394737183421079999)
XLA Ops:
  0.6 1.1 slice_bitcast_fusion.2
  2.2 0.8 maximum_bitcast_fusion.5.refs_5_
  3.5 0.8 maximum_bitcast_fusion.4.refs_1_
  4.4 0.7 bitcast_bitcast_fusion
  5.1 1.5 fusion.3
  6.6 0.6 reshape_squeeze.6
  7.2 0.4 copy.74
  7.6 0.6 fusion.5
  8.2 1.0 squeeze.32.refs_3_
  9.2 1.0 squeeze.33.refs_4_
  10.3 0.6 reshape_squeeze.7
  10.8 0.4 copy.73
  11.3 0.6 fusion.4
  11.9 1.0 squeeze.36.refs_7_
  12.9 1.0 squeeze.37.refs_8_
  13.9 70.9 %start.1 = (bf16[4,128,1536]{2,1,0:T(8,128)(2,1)}, bf16[2,2,2,2,2,48,896]{6,5,4,3,2,1,0:T(8,128)(2,1)}, bf16[2,2,2,2,2,48,384]{6,5,4,3,2,1,0:T(8,128)(2,1)}, bf1...) custom-call(bf16[128,1536]{1,0:T(8,128)(2,1)} %refs_0_.1, ...), custom_call_target="tpu_custom_call" | custom-call | tf_op jit(solution)/shard_map/start/pallas_call | solution.py:1317
  84.8 1.2 slice_convert_fusion
  86.3 0.6 fusion.9
  86.9 0.4 fusion
  87.3 1.6 fusion.2.refs_0_.refs_10_
  88.9 0.9 slice_bitcast_fusion
  89.8 117.2 %body_more.1 = (bf16[8,512,128]{2,1,0:T(8,128)(2,1)}, bf16[512,384]{1,0:T(8,128)(2,1)}, f32[512,128]{1,0:T(8,128)}, f32[128,1536]{1,0:T(8,128)}, f32[128,1536]{1...) custom-call(bf16[4,128,1536]{2,1,0:T(8,128)(2,1)} %fusion.2.refs_0_., ...), custom_call_target="tpu_custom_call" | custom-call | tf_op jit(solution)/shard_map/body_more/pallas_call | solution.py:1377
  207.0 0.8 convert_element_type.34.refs_11_
  207.8 80.2 %body.1 = (bf16[8,512,128]{2,1,0:T(8,128)(2,1)}, bf16[512,384]{1,0:T(8,128)(2,1)}, f32[512,128]{1,0:T(8,128)}, f32[128,1536]{1,0:T(8,128)}, f32[128,1536]{1,0:T(...) custom-call(bf16[4,128,1536]{2,1,0:T(8,128)(2,1)} %get-tuple-element, ...), custom_call_target="tpu_custom_call" | custom-call | tf_op jit(solution)/shard_map/body/pallas_call | solution.py:1377
  288.0 78.9 %back_first.1 = (f32[128,1536]{1,0:T(8,128)}, f32[1,1536]{1,0:T(1,128)}, bf16[1536,512]{1,0:T(8,128)(2,1)}, bf16[1536,512]{1,0:T(8,128)(2,1)}, bf16[1536,512]{1,...) custom-call(bf16[128,1536]{1,0:T(8,128)(2,1)} %get-tuple-element.98., ...), custom_call_target="tpu_custom_call" | custom-call | tf_op jit(solution)/shard_map/back_first/pallas_call | solution.py:1411
  366.9 101.9 %back_mid.1 = (f32[1,1536]{1,0:T(1,128)}, f32[128,1536]{1,0:T(8,128)}, f32[1,1536]{1,0:T(1,128)}, bf16[1536,512]{1,0:T(8,128)(2,1)}, bf16[1536,512]{1,0:T(8,128)...) custom-call(bf16[512,768]{1,0:T(8,128)(2,1)} %get-tuple-element.112., ...), custom_call_target="tpu_custom_call" | custom-call | tf_op jit(solution)/shard_map/back_mid/pallas_call | solution.py:1411
  468.8 1.1 maximum_bitcast_fusion.2
  469.9 1.2 maximum_convert_fusion.1
  471.3 0.6 pad.9.refs_2_
  471.9 109.8 %back_last.1 = (bf16[128,1536]{1,0:T(8,128)(2,1)}, f32[16,128]{1,0:T(8,128)}, bf16[4,48,512]{2,1,0:T(8,128)(2,1)}, bf16[4,48,512]{2,1,0:T(8,128)(2,1)}, bf16[4,4...) custom-call(f32[128,1536]{1,0:T(8,128)} %get-tuple-element.128.refs_, ...), custom_call_target="tpu_custom_call" | custom-call | tf_op jit(solution)/shard_map/back_last/pallas_call | solution.py:1411
  581.8 1.1 pad_maximum_fusion
  583.2 0.6 copy.78
  583.8 0.3 stack_reshape.12
  584.1 0.3 reshape.206
  584.4 0.6 copy.77
  585.1 0.3 stack_reshape.13
  585.5 0.3 reshape.207
  585.8 0.6 copy.76
  586.4 0.3 stack_reshape.14
  586.8 0.3 reshape.208
  587.1 0.6 copy.75
  587.7 0.3 stack_reshape.15
  588.3 4.1 copy.52
  592.4 0.9 maximum_convert_fusion.3
  594.4 1.1 maximum_convert_fusion.2
  595.5 1.0 convert_element_type.36
  596.5 1.3 slice.129
  597.8 1.0 convert_element_type.35
  (93 shorter events, 3.1 us)
Async XLA Ops:
  1.9 1.5 copy-start.22
  2.1 2.2 copy-start.8
  3.1 2.0 copy-start.1
  84.8 2.1 copy-start
  87.3 1.6 copy-start.2
  89.8 117.2 %copy-start.3 = (f32[128,1536]{1,0:T(8,128)S(1)}, f32[128,1536]{1,0:T(8,128)}, u32[]{:S(2)}) copy-start(f32[128,1536]{1,0:T(8,128)} %param.12) | copy-start | bytes 2359300
  366.9 103.0 %copy-start.13 = (bf16[128,768]{1,0:T(8,128)(2,1)S(1)}, bf16[128,768]{1,0:T(8,128)(2,1)}, u32[]{:S(2)}) copy-start(bf16[128,768]{1,0:T(8,128)(2,1)} %get-tuple-element.154) | copy-start | bytes 589828
  366.9 103.0 %copy-start.14 = (bf16[128,768]{1,0:T(8,128)(2,1)S(1)}, bf16[128,768]{1,0:T(8,128)(2,1)}, u32[]{:S(2)}) copy-start(bf16[128,768]{1,0:T(8,128)(2,1)} %get-tuple-element.155) | copy-start | bytes 589828
  469.9 1.3 copy-start.19
  469.9 1.3 copy-start.20
  469.9 1.3 copy-start.21
  581.8 2.3 copy-start.15
  581.8 2.3 copy-start.16
  584.4 1.0 copy-start.11
  584.4 1.0 copy-start.12
  585.4 1.3 copy-start.9
  585.5 1.3 copy-start.10
  588.3 4.1 copy-start.18
  588.3 4.1 copy-start.17
  592.4 1.0 copy-start.5
  592.4 1.4 copy-start.4
  594.2 1.3 copy-start.7
  594.4 3.3 copy-start.6

commit v9 on v8

--- a/solution.py
+++ b/solution.py
@@ -726,13 +726,16 @@
         blocks = refs.take(n_next)
     else:
         (swap_src,) = refs.take(1)
-    heads, o_ref, lse_ref, h1_ref, hn_ref, hb_ref, gate_ref, up_ref, u_ref, ng_hbm = refs.take(10)
+    early_out = refs.take(6)
+    h1_ref, hn_ref, hb_ref, ng_hbm = refs.take(4)
     late_out = [refs.take(1)[0] if late[i] else None for i in range(3)]
     if n_next:
         (nn_hbm,) = refs.take(1)
         full = refs.take(n_next)
     else:
         (swap_dst,) = refs.take(1)
+    early = refs.take(6)
+    heads, o_ref, lse_ref, gate_ref, up_ref, u_ref = early
     n1, wq, wo = refs.take(3)
     inner = refs.take(3)
     out_a, land_a, land_n, out_b, land_b = refs.take(5)
@@ -835,6 +838,8 @@
         second.ready(i)
         tick()
     keep = net.here(land_n, ng_hbm)
+    for ref, out in zip(early, early_out):
+        keeps.append(net.here(ref, out))
     span = rows_of(place.rank, rows)
 
     def use_down(cols, y):
@@ -1356,12 +1361,12 @@
         like((heads, tall, 128)),
         like((tall, o_cols)),
         like((tall, 128), F32),
+        like((tall, hidden)),
+        like((tall, hidden)),
+        like((tall, hidden)),
         like((rows, width), F32),
         like((rows, width), F32),
         like((rows, width)),
-        like((tall, hidden)),
-        like((tall, hidden)),
-        like((tall, hidden)),
         like((RANKS, rows, width)),
     ]
     n_state = len(outs)
@@ -1380,8 +1385,9 @@
         in_specs=[AN, AN, VM, VM, VM, VM, AN, AN, AN, AN]
         + [AN] * sum(started)
         + ([VM] + [AN] * n_next if n_next else [AN]),
-        out_specs=[VM] * (n_state - 1) + [AN] * (len(outs) - n_state + 1),
-        scratch_shapes=[
+        out_specs=[AN] * 6 + [VM] * 3 + [AN] * (len(outs) - n_state + 1),
+        scratch_shapes=[pltpu.VMEM(out.shape, out.dtype) for out in outs[:6]]
+        + [
             four,
             pltpu.VMEM((width, cols), BF16),
             pltpu.VMEM(wo.shape, BF16),
@@ -1473,7 +1479,7 @@
                 swap=cotangent.astype(BF16),
             )
             n1_next = None
-        heads, mixed, lse, h1, h_next, h_round, gate, up, u, n2 = state
+        heads, mixed, lse, gate, up, u, h1, h_next, h_round, n2 = state
         records.append(dict(
             hin=h, n1=n1, heads=heads, o=mixed, lse=lse, h1=h1, n2=tall(n2), gate=gate, up=up, u=u,
             wq=wq, wo=wo, wgate=inner[0], wup=inner[1], wd=inner[2],

time: 607 us -> 603 us (level)
  no operation moved by 1% of the time
where the time goes in v9:
time: 603 us; the launch traced here: 595 us
  Pallas kernels  554 us (92%)
  local copies, waits for them, and re-layouts  25 us (4%)
  other arithmetic  13.4 us (2%)
    pallas_call x3, Pallas kernels, call_back(): pl.pallas_call(functools.partial(back_kernel, count, rows, tuple(inputs),...  289 us
    pallas_call x2, Pallas kernels, call_body(): pl.pallas_call(functools.partial(body_kernel, count, rows, late, started,...  194 us
    pallas_call x1, Pallas kernels, call_start(): pl.pallas_call(functools.partial(start_kernel, count, n, n_later, n_ahead...  70.9 us

profile of v9, /device:TPU:0, one launch (start us, length us, event | category | flops | bytes accessed | tf_op | source)
XLA Modules:
  0.0 594.6 jit_solution(10919916769027203456)
XLA Ops:
  0.6 1.1 slice_bitcast_fusion.2
  2.2 0.8 maximum_bitcast_fusion.5.refs_5_
  3.5 0.8 maximum_bitcast_fusion.4.refs_1_
  4.4 0.7 bitcast_bitcast_fusion
  5.1 1.5 fusion.3
  6.6 0.6 reshape_squeeze.6
  7.2 0.4 copy.74
  7.6 0.6 fusion.5
  8.2 1.0 squeeze.32.refs_3_
  9.2 1.0 squeeze.33.refs_4_
  10.3 0.6 reshape_squeeze.7
  10.8 0.4 copy.73
  11.3 0.6 fusion.4
  11.9 1.0 squeeze.36.refs_7_
  12.9 1.0 squeeze.37.refs_8_
  13.9 70.9 %start.1 = (bf16[4,128,1536]{2,1,0:T(8,128)(2,1)}, bf16[2,2,2,2,2,48,896]{6,5,4,3,2,1,0:T(8,128)(2,1)}, bf16[2,2,2,2,2,48,384]{6,5,4,3,2,1,0:T(8,128)(2,1)}, bf1...) custom-call(bf16[128,1536]{1,0:T(8,128)(2,1)} %refs_0_.1, ...), custom_call_target="tpu_custom_call" | custom-call | tf_op jit(solution)/shard_map/start/pallas_call | solution.py:1322
  84.8 1.2 slice_convert_fusion
  86.3 0.6 fusion.9
  86.9 0.4 fusion
  87.3 1.6 fusion.2.refs_0_.refs_10_
  88.9 0.9 slice_bitcast_fusion
  89.8 115.6 %body_more.1 = (bf16[8,512,128]{2,1,0:T(8,128)(2,1)}, bf16[512,384]{1,0:T(8,128)(2,1)}, f32[512,128]{1,0:T(8,128)}, bf16[512,1024]{1,0:T(8,128)(2,1)}, bf16[512,...) custom-call(bf16[4,128,1536]{2,1,0:T(8,128)(2,1)} %fusion.2.refs_0_., ...), custom_call_target="tpu_custom_call" | custom-call | tf_op jit(solution)/shard_map/body_more/pallas_call | solution.py:1382
  205.5 0.8 convert_element_type.34.refs_11_
  206.3 78.6 %body.1 = (bf16[8,512,128]{2,1,0:T(8,128)(2,1)}, bf16[512,384]{1,0:T(8,128)(2,1)}, f32[512,128]{1,0:T(8,128)}, bf16[512,1024]{1,0:T(8,128)(2,1)}, bf16[512,1024]...) custom-call(bf16[4,128,1536]{2,1,0:T(8,128)(2,1)} %get-tuple-element, ...), custom_call_target="tpu_custom_call" | custom-call | tf_op jit(solution)/shard_map/body/pallas_call | solution.py:1382
  284.9 79.6 %back_first.1 = (f32[128,1536]{1,0:T(8,128)}, f32[1,1536]{1,0:T(1,128)}, bf16[1536,512]{1,0:T(8,128)(2,1)}, bf16[1536,512]{1,0:T(8,128)(2,1)}, bf16[1536,512]{1,...) custom-call(bf16[128,1536]{1,0:T(8,128)(2,1)} %get-tuple-element.98., ...), custom_call_target="tpu_custom_call" | custom-call | tf_op jit(solution)/shard_map/back_first/pallas_call | solution.py:1417
  364.5 100.9 %back_mid.1 = (f32[1,1536]{1,0:T(1,128)}, f32[128,1536]{1,0:T(8,128)}, f32[1,1536]{1,0:T(1,128)}, bf16[1536,512]{1,0:T(8,128)(2,1)}, bf16[1536,512]{1,0:T(8,128)...) custom-call(bf16[512,768]{1,0:T(8,128)(2,1)} %get-tuple-element.112., ...), custom_call_target="tpu_custom_call" | custom-call | tf_op jit(solution)/shard_map/back_mid/pallas_call | solution.py:1417
  465.4 1.1 maximum_bitcast_fusion.2
  466.6 1.2 maximum_convert_fusion.1
  467.9 0.6 pad.9.refs_2_
  468.6 108.6 %back_last.1 = (bf16[128,1536]{1,0:T(8,128)(2,1)}, f32[16,128]{1,0:T(8,128)}, bf16[4,48,512]{2,1,0:T(8,128)(2,1)}, bf16[4,48,512]{2,1,0:T(8,128)(2,1)}, bf16[4,4...) custom-call(f32[128,1536]{1,0:T(8,128)} %get-tuple-element.128.refs_, ...), custom_call_target="tpu_custom_call" | custom-call | tf_op jit(solution)/shard_map/back_last/pallas_call | solution.py:1417
  577.2 1.1 pad_maximum_fusion
  578.6 0.6 copy.78
  579.2 0.3 stack_reshape.12
  579.5 0.3 reshape.206
  579.8 0.6 copy.77
  580.5 0.3 stack_reshape.13
  580.9 0.3 reshape.207
  581.2 0.6 copy.76
  581.8 0.3 stack_reshape.14
  582.2 0.3 reshape.208
  582.5 0.6 copy.75
  583.1 0.3 stack_reshape.15
  583.7 4.1 copy.52
  587.8 0.9 maximum_convert_fusion.3
  589.9 1.1 maximum_convert_fusion.2
  591.0 1.0 convert_element_type.36
  591.9 1.3 slice.129
  593.2 1.0 convert_element_type.35
  (93 shorter events, 3.1 us)
Async XLA Ops:
  1.9 1.5 copy-start.22
  2.1 2.2 copy-start.8
  3.1 2.0 copy-start.1
  84.8 2.1 copy-start
  87.3 1.6 copy-start.2
  89.8 115.7 %copy-start.3 = (f32[128,1536]{1,0:T(8,128)S(1)}, f32[128,1536]{1,0:T(8,128)}, u32[]{:S(2)}) copy-start(f32[128,1536]{1,0:T(8,128)} %param.12) | copy-start | bytes 2359300
  364.5 102.0 %copy-start.13 = (bf16[128,768]{1,0:T(8,128)(2,1)S(1)}, bf16[128,768]{1,0:T(8,128)(2,1)}, u32[]{:S(2)}) copy-start(bf16[128,768]{1,0:T(8,128)(2,1)} %get-tuple-element.154) | copy-start | bytes 589828
  364.5 102.0 %copy-start.14 = (bf16[128,768]{1,0:T(8,128)(2,1)S(1)}, bf16[128,768]{1,0:T(8,128)(2,1)}, u32[]{:S(2)}) copy-start(bf16[128,768]{1,0:T(8,128)(2,1)} %get-tuple-element.155) | copy-start | bytes 589828
  466.5 1.3 copy-start.19
  466.5 1.3 copy-start.20
  466.5 1.3 copy-start.21
  577.2 2.3 copy-start.15
  577.2 2.3 copy-start.16
  579.8 1.0 copy-start.11
  579.8 1.0 copy-start.12
  580.9 1.3 copy-start.9
  580.9 1.3 copy-start.10
  583.7 4.1 copy-start.18
  583.7 4.1 copy-start.17
  587.8 1.0 copy-start.5
  587.8 1.4 copy-start.4
  589.6 1.3 copy-start.7
  589.8 3.3 copy-start.6

commit v10 on v9

--- a/solution.py
+++ b/solution.py
@@ -1100,6 +1100,8 @@
         load("wd", r["wd_hbm"], r["wd"])
         load("wg", r["wgate_hbm"], r["wgu"].at[:, pl.ds(0, hidden)])
         load("wu", r["wup_hbm"], r["wgu"].at[:, pl.ds(hidden, hidden)])
+        load("gate", r["gate_hbm"], r["gate"])
+        load("up", r["up_hbm"], r["up"])
         load("u", r["u_hbm"], r["u"])
         load("n2", r["n2_hbm"], r["n2"])
     if attention:
@@ -1113,7 +1115,7 @@
     ends = []
 
     def ready_inner():
-        for name in ("wd", "wg", "wu"):
+        for name in ("wd", "wg", "wu", "gate", "up"):
             waits[name].wait()
 
     def between():
@@ -1496,10 +1498,10 @@
 
     def inner_in(layer):
         rec = records[layer]
-        names = dict(wd="wd", wgate="wgate", wup="wup", u="u", n2="n2")
+        names = dict(wd="wd", wgate="wgate", wup="wup", u="u", n2="n2", gate="gate", up="up")
         values = {key + "_hbm": (rec[name], AN) for key, name in names.items()}
         return dict(
-            values, gate=(rec["gate"], VM), up=(rec["up"], VM), h1=(rec["h1"], VM), gain=(gain(layer, 1), VM)
+            values, h1=(rec["h1"], VM), gain=(gain(layer, 1), VM)
         )
 
     inner_out = dict(
@@ -1514,6 +1516,8 @@
         wd=((hidden, width), BF16),
         wgu=((width, 2 * hidden), BF16),
         u=((length, hidden), BF16),
+        gate=((length, hidden), BF16),
+        up=((length, hidden), BF16),
         n2=((length, width), BF16),
         dgu=((length, 2 * hidden), BF16),
         buffers=((2, 256, 2 * hidden), BF16),

time: 603 us -> 603 us (level)
  no operation moved by 1% of the time
where the time goes in v10:
time: 603 us; the launch traced here: 593 us
  Pallas kernels  553 us (92%)
  local copies, waits for them, and re-layouts  25 us (4%)
  other arithmetic  13.4 us (2%)
    pallas_call x3, Pallas kernels, call_back(): pl.pallas_call(functools.partial(back_kernel, count, rows, tuple(inputs),...  288 us
    pallas_call x2, Pallas kernels, call_body(): pl.pallas_call(functools.partial(body_kernel, count, rows, late, started,...  194 us
    pallas_call x1, Pallas kernels, call_start(): pl.pallas_call(functools.partial(start_kernel, count, n, n_later, n_ahead...  70.9 us

profile of v10, /device:TPU:0, one launch (start us, length us, event | category | flops | bytes accessed | tf_op | source)
XLA Modules:
  0.0 593.2 jit_solution(4158366890410961015)
XLA Ops:
  0.6 1.1 slice_bitcast_fusion.2
  2.2 0.8 maximum_bitcast_fusion.5.refs_5_
  3.5 0.8 maximum_bitcast_fusion.4.refs_1_
  4.4 0.7 bitcast_bitcast_fusion
  5.1 1.5 fusion.3
  6.6 0.6 reshape_squeeze.6
  7.2 0.4 copy.74
  7.6 0.6 fusion.5
  8.2 1.0 squeeze.32.refs_3_
  9.2 1.0 squeeze.33.refs_4_
  10.3 0.6 reshape_squeeze.7
  10.8 0.4 copy.73
  11.3 0.6 fusion.4
  11.9 1.0 squeeze.36.refs_7_
  12.9 1.0 squeeze.37.refs_8_
  13.9 70.9 %start.1 = (bf16[4,128,1536]{2,1,0:T(8,128)(2,1)}, bf16[2,2,2,2,2,48,896]{6,5,4,3,2,1,0:T(8,128)(2,1)}, bf16[2,2,2,2,2,48,384]{6,5,4,3,2,1,0:T(8,128)(2,1)}, bf1...) custom-call(bf16[128,1536]{1,0:T(8,128)(2,1)} %refs_0_.1, ...), custom_call_target="tpu_custom_call" | custom-call | tf_op jit(solution)/shard_map/start/pallas_call | solution.py:1324
  84.8 1.2 slice_convert_fusion
  86.3 0.6 fusion.9
  86.9 0.4 fusion
  87.3 1.6 fusion.2.refs_0_.refs_10_
  88.9 0.9 slice_bitcast_fusion
  89.8 115.6 %body_more.1 = (bf16[8,512,128]{2,1,0:T(8,128)(2,1)}, bf16[512,384]{1,0:T(8,128)(2,1)}, f32[512,128]{1,0:T(8,128)}, bf16[512,1024]{1,0:T(8,128)(2,1)}, bf16[512,...) custom-call(bf16[4,128,1536]{2,1,0:T(8,128)(2,1)} %fusion.2.refs_0_., ...), custom_call_target="tpu_custom_call" | custom-call | tf_op jit(solution)/shard_map/body_more/pallas_call | solution.py:1384
  205.5 0.8 convert_element_type.34.refs_11_
  206.3 78.6 %body.1 = (bf16[8,512,128]{2,1,0:T(8,128)(2,1)}, bf16[512,384]{1,0:T(8,128)(2,1)}, f32[512,128]{1,0:T(8,128)}, bf16[512,1024]{1,0:T(8,128)(2,1)}, bf16[512,1024]...) custom-call(bf16[4,128,1536]{2,1,0:T(8,128)(2,1)} %get-tuple-element, ...), custom_call_target="tpu_custom_call" | custom-call | tf_op jit(solution)/shard_map/body/pallas_call | solution.py:1384
  284.9 78.9 %back_first.1 = (f32[128,1536]{1,0:T(8,128)}, f32[1,1536]{1,0:T(1,128)}, bf16[1536,512]{1,0:T(8,128)(2,1)}, bf16[1536,512]{1,0:T(8,128)(2,1)}, bf16[1536,512]{1,...) custom-call(bf16[128,1536]{1,0:T(8,128)(2,1)} %get-tuple-element.98., ...), custom_call_target="tpu_custom_call" | custom-call | tf_op jit(solution)/shard_map/back_first/pallas_call | solution.py:1419
  363.8 100.1 %back_mid.1 = (f32[1,1536]{1,0:T(1,128)}, f32[128,1536]{1,0:T(8,128)}, f32[1,1536]{1,0:T(1,128)}, bf16[1536,512]{1,0:T(8,128)(2,1)}, bf16[1536,512]{1,0:T(8,128)...) custom-call(bf16[512,768]{1,0:T(8,128)(2,1)} %get-tuple-element.112., ...), custom_call_target="tpu_custom_call" | custom-call | tf_op jit(solution)/shard_map/back_mid/pallas_call | solution.py:1419
  463.9 1.1 maximum_bitcast_fusion.2
  465.1 1.2 maximum_convert_fusion.1
  466.4 0.6 pad.9.refs_2_
  467.1 108.7 %back_last.1 = (bf16[128,1536]{1,0:T(8,128)(2,1)}, f32[16,128]{1,0:T(8,128)}, bf16[4,48,512]{2,1,0:T(8,128)(2,1)}, bf16[4,48,512]{2,1,0:T(8,128)(2,1)}, bf16[4,4...) custom-call(f32[128,1536]{1,0:T(8,128)} %get-tuple-element.128.refs_, ...), custom_call_target="tpu_custom_call" | custom-call | tf_op jit(solution)/shard_map/back_last/pallas_call | solution.py:1419
  575.8 1.1 pad_maximum_fusion
  577.2 0.6 copy.78
  577.8 0.3 stack_reshape.12
  578.2 0.3 reshape.206
  578.5 0.6 copy.77
  579.1 0.3 stack_reshape.13
  579.5 0.3 reshape.207
  579.8 0.6 copy.76
  580.4 0.3 stack_reshape.14
  580.8 0.3 reshape.208
  581.1 0.6 copy.75
  581.7 0.3 stack_reshape.15
  582.3 4.1 copy.52
  586.5 0.9 maximum_convert_fusion.3
  588.5 1.1 maximum_convert_fusion.2
  589.6 1.0 convert_element_type.36
  590.5 1.3 slice.129
  591.8 1.0 convert_element_type.35
  (93 shorter events, 3.1 us)
Async XLA Ops:
  1.9 1.5 copy-start.22
  2.1 2.2 copy-start.8
  3.1 2.0 copy-start.1
  84.8 2.1 copy-start
  87.3 1.6 copy-start.2
  89.8 115.7 %copy-start.3 = (f32[128,1536]{1,0:T(8,128)S(1)}, f32[128,1536]{1,0:T(8,128)}, u32[]{:S(2)}) copy-start(f32[128,1536]{1,0:T(8,128)} %param.12) | copy-start | bytes 2359300
  363.8 101.2 %copy-start.13 = (bf16[128,768]{1,0:T(8,128)(2,1)S(1)}, bf16[128,768]{1,0:T(8,128)(2,1)}, u32[]{:S(2)}) copy-start(bf16[128,768]{1,0:T(8,128)(2,1)} %get-tuple-element.154) | copy-start | bytes 589828
  363.8 101.2 %copy-start.14 = (bf16[128,768]{1,0:T(8,128)(2,1)S(1)}, bf16[128,768]{1,0:T(8,128)(2,1)}, u32[]{:S(2)}) copy-start(bf16[128,768]{1,0:T(8,128)(2,1)} %get-tuple-element.155) | copy-start | bytes 589828
  465.0 1.3 copy-start.19
  465.0 1.3 copy-start.20
  465.0 1.3 copy-start.21
  575.8 2.3 copy-start.15
  575.8 2.3 copy-start.16
  578.4 1.0 copy-start.11
  578.4 1.0 copy-start.12
  579.5 1.3 copy-start.9
  579.5 1.3 copy-start.10
  582.3 4.1 copy-start.18
  582.3 4.1 copy-start.17
  586.4 1.0 copy-start.5
  586.4 1.4 copy-start.4
  588.2 1.3 copy-start.7
  588.5 3.3 copy-start.6
